TPU v7x, 32 devices: a whole 2x2x4 slice. The times are simulated.
32 devices in a mesh: face: 16 (over z, y, core), sub: 2 (over x).
Axes of the slice: x: 2, y: 2, z: 4, core: 2. Of those that a mesh axis runs over, the one named last changes fastest.
Arguments:
- nodes: bfloat16 [40960, 256], P(('face', 'sub')), may hold values from -6 to 6
- edges: bfloat16 [40960, 12, 256], P(('face', 'sub')), may hold values from -6 to 6
- neighbours: int32 [40960, 12], P(('face', 'sub')), may hold values from 0 to 1791
- valid: int32 [40960, 12], P(('face', 'sub')), may hold values 0 or 1
- send_lists: int32 [32, 2, 256], P(('face', 'sub')), may hold values from 0 to 1279
- edge_first: bfloat16 [768, 256], replicated, may hold values from -0.21875 to 0.21875
- edge_first_bias: bfloat16 [256], replicated, may hold values from -3 to 3
- edge_second: bfloat16 [256, 256], replicated, may hold values from -0.375 to 0.375
- edge_second_bias: bfloat16 [256], replicated, may hold values from -3 to 3
- edge_gain: bfloat16 [256], replicated, may hold values from 0.5 to 1.5
- edge_shift: bfloat16 [256], replicated, may hold values from -3 to 3
- node_first: bfloat16 [512, 256], replicated, may hold values from -0.25 to 0.25
- node_first_bias: bfloat16 [256], replicated, may hold values from -3 to 3
- node_second: bfloat16 [256, 256], replicated, may hold values from -0.375 to 0.375
- node_second_bias: bfloat16 [256], replicated, may hold values from -3 to 3
- node_gain: bfloat16 [256], replicated, may hold values from 0.5 to 1.5
- node_shift: bfloat16 [256], replicated, may hold values from -3 to 3
- cotangent: bfloat16 [40960, 256], P(('face', 'sub')), may hold values from -6 to 6
Outputs:
- mixed: bfloat16 [40960, 256], P(('face', 'sub'))
- grad_nodes: float32 [40960, 256], P(('face', 'sub'))
- grad_edges: bfloat16 [40960, 12, 256], P(('face', 'sub'))
- grad_edge_first: float32 [768, 256], replicated
- grad_edge_first_bias: float32 [256], replicated
- grad_edge_second: float32 [256, 256], replicated
- grad_edge_second_bias: float32 [256], replicated
- grad_edge_gain: float32 [256], replicated
- grad_edge_shift: float32 [256], replicated
- grad_node_first: float32 [512, 256], replicated
- grad_node_first_bias: float32 [256], replicated
- grad_node_second: float32 [256, 256], replicated
- grad_node_second_bias: float32 [256], replicated
- grad_node_gain: float32 [256], replicated
- grad_node_shift: float32 [256], replicated
All inputs are finite; a program needn't handle non-finite values. No bound on the sum of `valid` on one device may be relied on, other than what follows from the above.
Results may differ from a plain program's by a relative error of at most 0.0084.
Values may be sent and summed in bfloat16 or wider, within the bound.
No kernel may reach another device: no remote copies, remote signals or barrier semaphores. Data moves between devices by JAX's collectives and lax.ppermute only.
A program may use at most 192 MiB of HBM per device.

v0:
```python
import math

import jax
import jax.numpy as jnp
from jax import lax
from jax.sharding import PartitionSpec as P


def passed_along(value, axis, steps):
    count = lax.axis_size(axis)
    pairs = [(source, (source + steps) % count) for source in range(count)]
    return lax.ppermute(value, axis, pairs)


def matmul(left, right):
    return jnp.dot(left, right, preferred_element_type=jnp.float32)


def outer_sum(left, right):
    return lax.dot_general(
        left, right, (((0,), (0,)), ((), ())), preferred_element_type=jnp.float32
    )


def outer_exact(left, right):
    return lax.dot_general(
        left,
        right,
        (((0,), (0,)), ((), ())),
        precision=lax.Precision.HIGHEST,
        preferred_element_type=jnp.float32,
    )


def back_mul(left, right):
    return lax.dot_general(
        left, right, (((1,), (1,)), ((), ())), preferred_element_type=jnp.float32
    )


def back_exact(left, right):
    return lax.dot_general(
        left,
        right,
        (((1,), (1,)), ((), ())),
        precision=lax.Precision.HIGHEST,
        preferred_element_type=jnp.float32,
    )


def one_hot_rows(index, rows):
    return (index[:, None] == jnp.arange(rows, dtype=jnp.int32)[None, :]).astype(jnp.bfloat16)


def pick_rows(index, source, block):
    rows = source.shape[0]
    pieces = index.reshape(-1, block)

    def one_block(picks):
        return matmul(one_hot_rows(picks, rows), source)

    picked = lax.map(one_block, pieces)
    return picked.reshape(index.shape[0], source.shape[1])


def spread_rows(index, values, rows, block):
    width = values.shape[1]
    pieces = index.reshape(-1, block)
    parts = values.reshape(-1, block, width)

    def add_block(total, items):
        picks, vals = items
        return (total + outer_sum(one_hot_rows(picks, rows), vals), None)

    total, unused = lax.scan(add_block, jnp.zeros((rows, width), jnp.float32), (pieces, parts))
    return total


def norm_parts(values, gain, shift):
    centre = values - jnp.mean(values, axis=-1, keepdims=True)
    spread = jnp.mean(centre * centre, axis=-1, keepdims=True)
    scale = lax.rsqrt(spread + 1e-05)
    normal = centre * scale
    return (normal * gain + shift, normal, scale)


def norm_back(upstream, normal, scale, gain):
    scaled = upstream * gain
    return scale * (
        scaled
        - jnp.mean(scaled, axis=-1, keepdims=True)
        - normal * jnp.mean(scaled * normal, axis=-1, keepdims=True)
    )


def silu_slope(values):
    sigma = jax.nn.sigmoid(values)
    return sigma * (1.0 + values * (1.0 - sigma))


def body(
    nodes,
    edges,
    neighbours,
    valid,
    send_lists,
    edge_first,
    edge_first_bias,
    edge_second,
    edge_second_bias,
    edge_gain,
    edge_shift,
    node_first,
    node_first_bias,
    node_second,
    node_second_bias,
    node_gain,
    node_shift,
    cotangent,
):
    node_count = nodes.shape[0]
    width = nodes.shape[1]
    degree = neighbours.shape[1]
    halo_rows = send_lists.shape[2]
    table_rows = node_count + 2 * halo_rows
    edge_block = math.gcd(node_count, 128) * degree
    lists = send_lists[0]
    node_vals = nodes.astype(jnp.float32)
    to_next = pick_rows(lists[0], nodes, halo_rows).astype(jnp.bfloat16)
    to_prev = pick_rows(lists[1], nodes, halo_rows).astype(jnp.bfloat16)
    from_prev = passed_along(to_next, "face", 1)
    from_next = passed_along(to_prev, "face", -1)
    table = jnp.concatenate([nodes, from_prev, from_next], axis=0)
    flat_index = neighbours.reshape(-1)
    edge_rows = edges.reshape(-1, width)
    recv_part = edge_first[:width]
    send_part = edge_first[width : 2 * width]
    edge_part = edge_first[2 * width :]
    e_bias = edge_first_bias.astype(jnp.float32)
    receivers = jnp.repeat(nodes, degree, axis=0)
    senders = pick_rows(flat_index, table, edge_block).astype(jnp.bfloat16)
    joined = jnp.concatenate([receivers, senders, edge_rows], axis=1)
    pre_first = matmul(joined, edge_first) + e_bias
    act_first = jax.nn.silu(pre_first).astype(jnp.bfloat16)
    pre_second = matmul(act_first, edge_second) + edge_second_bias.astype(jnp.float32)
    e_gain = edge_gain.astype(jnp.float32)
    message, normal_b, scale_b = norm_parts(pre_second, e_gain, edge_shift.astype(jnp.float32))
    weights = valid.astype(jnp.float32).reshape(-1, 1)
    gathered = jnp.sum((message * weights).reshape(node_count, degree, width), axis=1).astype(
        jnp.bfloat16
    )
    pre_third = (
        matmul(nodes, node_first[:width])
        + matmul(gathered, node_first[width:])
        + node_first_bias.astype(jnp.float32)
    )
    act_third = jax.nn.silu(pre_third).astype(jnp.bfloat16)
    pre_fourth = matmul(act_third, node_second) + node_second_bias.astype(jnp.float32)
    n_gain = node_gain.astype(jnp.float32)
    update, normal_d, scale_d = norm_parts(pre_fourth, n_gain, node_shift.astype(jnp.float32))
    mixed = (node_vals + update).astype(jnp.bfloat16)
    upstream = cotangent.astype(jnp.float32)
    g_node_gain = jnp.sum(upstream * normal_d, axis=0)
    g_node_shift = jnp.sum(upstream, axis=0)
    grad_fourth = norm_back(upstream, normal_d, scale_d, n_gain).astype(jnp.bfloat16)
    g_node_second = outer_sum(act_third, grad_fourth)
    g_node_second_bias = jnp.sum(grad_fourth.astype(jnp.float32), axis=0)
    grad_third = (back_mul(grad_fourth, node_second) * silu_slope(pre_third)).astype(jnp.bfloat16)
    g_node_first = jnp.concatenate(
        [outer_sum(nodes, grad_third), outer_sum(gathered, grad_third)], axis=0
    )
    g_node_first_bias = jnp.sum(grad_third.astype(jnp.float32), axis=0)
    grad_own = back_mul(grad_third, node_first[:width])
    grad_gathered = back_mul(grad_third, node_first[width:])
    node_grads = (
        g_node_first,
        g_node_first_bias,
        g_node_second,
        g_node_second_bias,
        g_node_gain,
        g_node_shift,
    )
    grad_message = (grad_gathered[:, None, :] * valid.astype(jnp.float32)[:, :, None]).reshape(
        -1, width
    )
    g_edge_gain = jnp.sum(grad_message * normal_b, axis=0)
    g_edge_shift = jnp.sum(grad_message, axis=0)
    grad_second = norm_back(grad_message, normal_b, scale_b, e_gain).astype(jnp.bfloat16)
    g_edge_second = outer_sum(act_first, grad_second)
    g_edge_second_bias = jnp.sum(grad_second.astype(jnp.float32), axis=0)
    grad_first = (back_mul(grad_second, edge_second) * silu_slope(pre_first)).astype(jnp.bfloat16)
    g_edge_first_bias = jnp.sum(grad_first.astype(jnp.float32), axis=0)
    row_total = spread_rows(flat_index, grad_first, table_rows, edge_block)
    grad_table = back_exact(row_total, send_part.astype(jnp.float32))
    sender_block = outer_exact(table.astype(jnp.float32), row_total)
    g_edge_first = jnp.concatenate(
        [outer_sum(receivers, grad_first), sender_block, outer_sum(edge_rows, grad_first)], axis=0
    )
    grad_recv = jnp.sum(back_mul(grad_first, recv_part).reshape(node_count, degree, width), axis=1)
    grad_edges = (
        back_mul(grad_first, edge_part).astype(jnp.bfloat16).reshape(node_count, degree, width)
    )
    back_prev = grad_table[node_count : node_count + halo_rows].astype(jnp.bfloat16)
    back_next = grad_table[node_count + halo_rows :].astype(jnp.bfloat16)
    return_next = passed_along(back_prev, "face", -1)
    return_prev = passed_along(back_next, "face", 1)
    grad_nodes = upstream + grad_own + grad_recv + grad_table[:node_count]
    grad_nodes = grad_nodes + spread_rows(lists[0], return_next, node_count, halo_rows)
    grad_nodes = grad_nodes + spread_rows(lists[1], return_prev, node_count, halo_rows)
    summed = lax.psum(
        (
            g_edge_first,
            g_edge_first_bias,
            g_edge_second,
            g_edge_second_bias,
            g_edge_gain,
            g_edge_shift,
            g_node_first,
            g_node_first_bias,
            g_node_second,
            g_node_second_bias,
            g_node_gain,
            g_node_shift,
        ),
        ("face", "sub"),
    )
    edge_grads = summed[:6]
    node_grads = summed[6:]
    return (
        mixed,
        grad_nodes,
        grad_edges,
        edge_grads[0],
        edge_grads[1],
        edge_grads[2],
        edge_grads[3],
        edge_grads[4],
        edge_grads[5],
        node_grads[0],
        node_grads[1],
        node_grads[2],
        node_grads[3],
        node_grads[4],
        node_grads[5],
    )


def solution(mesh):
    return jax.shard_map(
        body,
        mesh=mesh,
        in_specs=(
            P(("face", "sub"), None),
            P(("face", "sub"), None, None),
            P(("face", "sub"), None),
            P(("face", "sub"), None),
            P(("face", "sub"), None, None),
            P(),
            P(),
            P(),
            P(),
            P(),
            P(),
            P(),
            P(),
            P(),
            P(),
            P(),
            P(),
            P(("face", "sub"), None),
        ),
        out_specs=(
            P(("face", "sub"), None),
            P(("face", "sub"), None),
            P(("face", "sub"), None, None),
            P(),
            P(),
            P(),
            P(),
            P(),
            P(),
            P(),
            P(),
            P(),
            P(),
            P(),
            P(),
        ),
        check_vma=False,
    )
```

profile of v0, /device:TPU:0, one launch (start us, length us, event | category | flops | bytes accessed | tf_op | source)
XLA Modules:
  0.0 567.3 jit_solution(4279543548950361030)
XLA Ops:
  31.4 11.0 %copy.59 = bf16[1280,12,256]{2,1,0:T(8,128)(2,1)} copy(bf16[1280,12,256]{2,0,1:T(8,128)(2,1)} %param.23) | data formatting | bytes 15728640 | tf_op args[1]
  42.4 13.6 %reshape.149 = bf16[15360,256]{1,0:T(8,128)(2,1)} reshape(bf16[1280,12,256]{2,1,0:T(8,128)(2,1)} %copy.59) | data formatting | bytes 15728640 | tf_op jit(solution)/shard_map/reshape | solution.py:135
  60.5 13.5 %reshape.148 = bf16[15360,256]{1,0:T(8,128)(2,1)} reshape(bf16[1280,12,256]{2,1,0:T(8,128)(2,1)} %broadcast_in_dim.29) | data formatting | bytes 15728640 | tf_op jit(solution)/shard_map/reshape | solution.py:140
  74.1 30.2 %while.5 = (s32[]{:T(128)}, bf16[10,1536,256]{2,1,0:T(8,128)(2,1)}, s32[10,1536]{1,0:T(8,128)S(1)}, bf16[1792,256]{1,0:T(8,128)(2,1)S(1)}, s32[]{:T(128)}) while((s32[]{:T(128)}, bf16[10,1536,256]{2,1,0:T(8,128)(2,1)}, s32[10,1536]{1,0:T(8,128)S(1)}, bf16[1792,256]{1,0:T(8,128)(2,1)S(1)}, s32[]{:T(128)}) %tuple.68), condition=%wide.region_1.2_spmd, body=%wide.region_0.1_spmd.sunk | while | flops 1412038656 | bytes 2508877 | solution.py:62
  104.3 20.0 %multiply_convert_fusion.1 = (bf16[15360,256]{1,0:T(8,128)(2,1)}, f32[15360,256]{1,0:T(8,128)}) fusion(f32[256]{0:T(256)S(1)} %convert_element_type.104, bf16[768,256]{1,0:T(8,128)(2,1)} %param.27, bf16[15360,256]{1,0:T(8,128)(2,1)} %reshape.149, bf16[15360,256]{1,0:T(8,128)(2,1)} %bitcast.69, bf16[15360,256]{1,0:T(8,128)(2,1)} %reshape.148), kind=kOutput, calls=%fused_computation.35 | convolution fusion | flops 6134169600 | bytes 47580160 | tf_op jit(solution)/shard_map/dot_general | solution.py:16
  129.9 8.9 %multiply_reduce_fusion.3 = f32[15360]{0:T(1024)S(1)} fusion(f32[15360,256]{1,0:T(8,128)S(1)} %get-tuple-element.217, f32[15360]{0:T(1024)S(1)} %broadcast_multiply_fusion.2), kind=kLoop, calls=%fused_computation.34 | loop fusion | flops 11781120 | bytes 15851520 | tf_op jit(solution)/shard_map/reduce_sum | solution.py:81
  138.8 11.3 %add_multiply_fusion = f32[15360,256]{1,0:T(8,128)} fusion(f32[15360,256]{1,0:T(8,128)S(1)} %get-tuple-element.217, f32[15360]{0:T(1024)S(1)} %mul.157, f32[256]{0:T(256)S(1)} %convert_element_type.108, f32[256]{0:T(256)S(1)} %convert_element_type.107, f32[15360]{0:T(1024)S(1)} %add_rsqrt_fusion, f32[15360]{0:T(1024)S(1)} %broadcast_multiply_fusion.2), kind=kLoop, calls=%fused_computation.33 | loop fusion | flops 19660800 | bytes 31643648 | tf_op jit(solution)/shard_map/mul | solution.py:149
  150.1 19.3 %reshape.150 = f32[1280,12,256]{2,1,0:T(8,128)} reshape(f32[15360,256]{1,0:T(8,128)} %add_multiply_fusion) | data formatting | bytes 31457280 | tf_op jit(solution)/shard_map/reshape | solution.py:149
  169.4 10.2 %reduce_sum.164 = bf16[1280,256]{1,0:T(8,128)(2,1)S(1)} reduce(f32[1280,12,256]{2,1,0:T(8,128)} %reshape.150, f32[]{:T(128)} %constant.69.clone.1), dimensions={1}, to_apply=%region_4.5 | reduce | flops 3604480 | bytes 16384004 | tf_op jit(solution)/shard_map/reduce_sum | solution.py:149
  190.3 9.7 %multiply_reduce_fusion = (f32[256]{0:T(256)}, f32[1280,12]{1,0:T(8,128)S(1)}) fusion(f32[1280,12]{1,0:T(8,128)S(1)} %copy.60, f32[1280,256]{1,0:T(8,128)S(1)} %fusion.51, f32[256]{0:T(256)S(1)} %convert_element_type.107), kind=kLoop, calls=%fused_computation.14 | loop fusion | flops 15713024 | bytes 1435648 | tf_op jit(solution)/shard_map/reduce_sum | solution.py:187
  207.8 19.3 %mul.175 = f32[15360,256]{1,0:T(8,128)} reshape(f32[1280,12,256]{2,1,0:T(8,128)} %mul.174) | data formatting | bytes 31457280 | tf_op jit(solution)/shard_map/mul | solution.py:183
  227.2 16.2 %multiply_reduce_fusion.1 = (f32[256]{0:T(256)S(1)}, f32[15360]{0:T(1024)S(1)}) fusion(f32[15360,256]{1,0:T(8,128)} %mul.175, f32[15360,256]{1,0:T(8,128)} %copy-done.1, f32[15360]{0:T(1024)S(1)} %mul.157, f32[15360]{0:T(1024)S(1)} %add_rsqrt_fusion, f32[15360]{0:T(1024)S(1)} %broadcast_multiply_fusion.2, f32[256]{0:T(256)S(1)} %convert_element_type.107), kind=kLoop, calls=%fused_computation.28 | loop fusion | flops 31441664 | bytes 31705088 | tf_op jit(solution)/shard_map/reduce_sum | solution.py:186
  243.4 15.7 %convert_reduce_fusion = (f32[256]{0:T(256)S(1)}, bf16[15360,256]{1,0:T(8,128)(2,1)S(1)}) fusion(f32[15360]{0:T(1024)S(1)} %broadcast_multiply_fusion.1, f32[15360,256]{1,0:T(8,128)} %copy-done.1, f32[15360]{0:T(1024)S(1)} %broadcast_multiply_fusion.2, f32[15360]{0:T(1024)S(1)} %div.45, f32[256]{0:T(256)S(1)} %convert_element_type.107, ...), kind=kLoop, calls=%fused_computation.29 | loop fusion | flops 43253504 | bytes 39630848 | tf_op jit(solution)/shard_map/reduce_sum | solution.py:190
  262.1 12.7 %convert_reduce_fusion.1 = (f32[256]{0:T(256)S(1)}, bf16[15360,256]{1,0:T(8,128)(2,1)}) fusion(f32[15360,256]{1,0:T(8,128)} %get-tuple-element.215, bf16[15360,256]{1,0:T(8,128)(2,1)S(1)} %get-tuple-element.208, bf16[256,256]{1,0:T(8,128)(2,1)S(1)} %copy-done), kind=kOutput, calls=%fused_computation.30 | convolution fusion | flops 2056519424 | bytes 31589376 | tf_op jit(solution)/shard_map/dot_general | solution.py:36
  274.8 9.5 %convolution_bitcast_fusion.1 = f32[256,256]{1,0:T(8,128)} fusion(bf16[15360,256]{1,0:T(8,128)(2,1)} %get-tuple-element.225, bf16[15360,256]{1,0:T(8,128)(2,1)} %reshape.149), kind=kOutput, calls=%fused_computation.72 | convolution fusion | flops 2013265920 | bytes 15990784 | tf_op jit(solution)/shard_map/dot_general | solution.py:20
  291.6 60.7 %while.6 = (s32[]{:T(128)}, f32[1792,256]{1,0:T(8,128)S(1)}, s32[10,1536]{1,0:T(8,128)}, bf16[10,1536,256]{2,1,0:T(8,128)(2,1)}, s32[]{:T(128)}, /*index=5*/s32[]{:T(128)}) while((s32[]{:T(128)}, f32[1792,256]{1,0:T(8,128)S(1)}, s32[10,1536]{1,0:T(8,128)}, bf16[10,1536,256]{2,1,0:T(8,128)(2,1)}, s32[]{:T(128)}, ...), condition=%wide.region_13.14_spmd.clone, body=%wide.region_12.13_spmd.clone.sunk | while | flops 1412956160 | bytes 4474975 | solution.py:75
  357.6 8.8 %convolution_convert_fusion = bf16[15360,256]{1,0:T(8,128)(2,1)} fusion(bf16[15360,256]{1,0:T(8,128)(2,1)} %bitcast.61, bf16[768,256]{1,0:T(8,128)(2,1)} %param.27), kind=kOutput, calls=%fused_computation.24 | convolution fusion | flops 2017198080 | bytes 15859712 | tf_op jit(solution)/shard_map/dot_general | solution.py:36
  366.5 8.8 %fusion.49 = f32[15360,256]{1,0:T(8,128)} fusion(bf16[15360,256]{1,0:T(8,128)(2,1)S(1)} %bitcast.64, bf16[768,256]{1,0:T(8,128)(2,1)} %param.27), kind=kOutput, calls=%fused_computation.89 | convolution fusion | flops 2013265920 | bytes 23724032 | tf_op jit(solution)/shard_map/dot_general | solution.py:36
  383.1 19.0 %reshape.151 = f32[1280,12,256]{2,1,0:T(8,128)} reshape(f32[15360,256]{1,0:T(8,128)} %fusion.49) | data formatting | bytes 31457280 | tf_op jit(solution)/shard_map/reshape | solution.py:199
  402.1 10.2 %reduce_sum.171 = f32[1280,256]{1,0:T(8,128)S(1)} reduce(f32[1280,12,256]{2,1,0:T(8,128)} %reshape.151, f32[]{:T(128)} %constant.69.clone.1), dimensions={1}, to_apply=%region_11.12 | reduce | flops 3604480 | bytes 17039364 | tf_op jit(solution)/shard_map/reduce_sum | solution.py:199
  419.6 13.5 %reshape.153 = bf16[1280,12,256]{2,1,0:T(8,128)(2,1)} reshape(bf16[15360,256]{1,0:T(8,128)(2,1)} %convolution_convert_fusion) | data formatting | bytes 15728640 | tf_op jit(solution)/shard_map/reshape | solution.py:201
  433.2 10.2 %copy.70 = bf16[1280,12,256]{2,0,1:T(8,128)(2,1)} copy(bf16[1280,12,256]{2,1,0:T(8,128)(2,1)} %reshape.153) | data formatting | bytes 15728640
  443.4 39.0 %all-reduce = (f32[256]{0:T(256)}, f32[256]{0:T(256)}, f32[256]{0:T(256)}, f32[256]{0:T(256)}, f32[256]{0:T(256)}, /*index=5*/f32[256]{0:T(256)}, f32[256]{0:T(256)}, f32[256]{0:T(256)}) all-reduce(f32[256]{0:T(256)S(1)} %get-tuple-element.224, f32[256]{0:T(256)S(1)} %get-tuple-element.207, ...), channel_id=1, replica_groups=mesh['face'=16,'sub'=2] {'face','sub'}, use_global_device_ids=true, to_apply=%region_16.17 | all-reduce | flops 2048 | bytes 16384 | tf_op jit(solution)/shard_map/psum | solution.py:210
  486.7 66.2 %all-reduce.4.cloned.1.call-done = (f32[768,256]{1,0:T(8,128)}, f32[256,256]{1,0:T(8,128)}, f32[512,256]{1,0:T(8,128)}, f32[256,256]{1,0:T(8,128)}) async-done(((f32[768,256]{1,0:T(8,128)}, f32[256,256]{1,0:T(8,128)}, f32[512,256]{1,0:T(8,128)}, f32[256,256]{1,0:T(8,128)}), (f32[768,256]{1,0:T(8,128)}, f32[256,256]{1,0:T(8,128)}, f32[512,256]{1,0:T(8,128)}, ...) | async-done | bytes 1835024 | tf_op jit(solution)/shard_map/psum | solution.py:210
  (188 shorter events, 185.4 us)
Async XLA Ops:
  7.2 117.1 %copy-start = (bf16[256,256]{1,0:T(8,128)(2,1)S(1)}, bf16[256,256]{1,0:T(8,128)(2,1)}, u32[]{:S(2)}) copy-start(bf16[256,256]{1,0:T(8,128)(2,1)} %param.29) | copy-start | bytes 393220
  7.2 23.3 %copy-start.17 = (bf16[1280,256]{1,0:T(8,128)(2,1)S(1)}, bf16[1280,256]{1,0:T(8,128)(2,1)}, u32[]{:S(2)}) copy-start(bf16[1280,256]{1,0:T(8,128)(2,1)} %param.39) | copy-start | bytes 1966084
  7.2 23.5 %copy-start.22 = (s32[1280,12]{0,1:T(8,128)S(1)}, s32[1280,12]{0,1:T(8,128)}, u32[]{:S(2)}) copy-start(s32[1280,12]{0,1:T(8,128)} %param.24) | copy-start | bytes 184324
  7.2 545.7 %all-reduce.4.cloned.1.call-start = ((), (), s32[]{:S(2)}) async-start(), calls=%async_computation | async-start | bytes 3670016 | tf_op jit(solution)/shard_map/psum | solution.py:210
  8.0 20.1 %copy-start.25 = (s32[1,1,256]{2,1,0:T(1,128)}, s32[1,1,256]{2,1,0:T(1,128)S(1)}, u32[]{:S(2)}) copy-start(s32[1,1,256]{2,1,0:T(1,128)S(1)} %get-tuple-element.212) | copy-start | bytes 3076
  8.0 22.7 %copy-start.23 = (s32[1,1,256]{2,1,0:T(1,128)}, s32[1,1,256]{2,1,0:T(1,128)S(1)}, u32[]{:S(2)}) copy-start(s32[1,1,256]{2,1,0:T(1,128)S(1)} %get-tuple-element.213) | copy-start | bytes 3076
  10.2 63.9 %collective-permute-start.1 = (bf16[256,256]{1,0:T(8,128)(2,1)}, bf16[256,256]{1,0:T(8,128)(2,1)S(1)}, u32[]{:S(2)}, u32[]{:S(2)}) collective-permute-start(bf16[256,256]{1,0:T(8,128)(2,1)} %fusion.38), channel_id=1, source_target_pairs={{0,30},{2,0},{4,2},{6,4},{8,6},{10,8},{12,10},{14,12},{16,14},{18,... | collective-permute-start | bytes 393224 | tf_op jit(solution)/shard_map/ppermute | solution.py:12
  17.7 56.3 %collective-permute-start = (bf16[256,256]{1,0:T(8,128)(2,1)}, bf16[256,256]{1,0:T(8,128)(2,1)S(1)}, u32[]{:S(2)}, u32[]{:S(2)}) collective-permute-start(bf16[256,256]{1,0:T(8,128)(2,1)} %fusion.37), channel_id=1, source_target_pairs={{0,2},{2,4},{4,6},{6,8},{8,10},{10,12},{12,14},{14,16},{16,18},{18... | collective-permute-start | bytes 393224 | tf_op jit(solution)/shard_map/ppermute | solution.py:12
  30.7 152.6 %copy-start.5 = (bf16[1280,256]{0,1:T(8,128)(2,1)}, bf16[1280,256]{0,1:T(8,128)(2,1)S(1)}, u32[]{:S(2)}) copy-start(bf16[1280,256]{0,1:T(8,128)(2,1)S(1)} %copy.61) | copy-start | bytes 1966084
  42.4 13.6 %copy-start.4 = (bf16[1280,256]{1,0:T(8,128)(2,1)S(1)}, bf16[1280,256]{1,0:T(8,128)(2,1)}, u32[]{:S(2)}) copy-start(bf16[1280,256]{1,0:T(8,128)(2,1)} %param.22) | copy-start | bytes 1966084
  104.3 20.0 %copy-start.11 = (bf16[1792,256]{1,0:T(8,128)(2,1)}, bf16[1792,256]{1,0:T(8,128)(2,1)S(1)}, u32[]{:S(2)}) copy-start(bf16[1792,256]{1,0:T(8,128)(2,1)S(1)} %get-tuple-element.339) | copy-start | bytes 2752516
  104.3 20.0 %copy-start.20 = (s32[10,1536]{1,0:T(8,128)}, s32[10,1536]{1,0:T(8,128)S(1)}, u32[]{:S(2)}) copy-start(s32[10,1536]{1,0:T(8,128)S(1)} %get-tuple-element.348) | copy-start | bytes 184324
  227.2 16.2 %copy-start.2 = (f32[15360,256]{1,0:T(8,128)S(1)}, f32[15360,256]{1,0:T(8,128)}, u32[]{:S(2)}) copy-start(f32[15360,256]{1,0:T(8,128)} %mul.175) | copy-start | bytes 47185924
  227.2 32.0 %slice-start = ((s8[7864320]{0:T(1024)(128)(4,1)}), s8[4194304]{0:T(1024)(128)(4,1)S(1)}, s32[]{:S(2)}) async-start(s8[7864320]{0:T(1024)(128)(4,1)} %bitcast.58), calls=%async_computation.1 | async-start | bytes 8388608
  243.4 15.7 %slice-start.1 = ((s8[7864320]{0:T(1024)(128)(4,1)}), s8[3670016]{0:T(1024)(128)(4,1)S(1)}, s32[]{:S(2)}) async-start(s8[7864320]{0:T(1024)(128)(4,1)} %bitcast.58), calls=%async_computation.2 | async-start | bytes 7340032
  291.6 60.7 %copy-start.12 = (bf16[1792,256]{1,0:T(8,128)(2,1)S(1)}, bf16[1792,256]{1,0:T(8,128)(2,1)}, u32[]{:S(2)}) copy-start(bf16[1792,256]{1,0:T(8,128)(2,1)} %copy-done.11) | copy-start | bytes 2752516
  366.5 15.1 %copy-start.10 = (f32[1792,256]{1,0:T(8,128)S(1)}, f32[1792,256]{1,0:T(8,128)}, u32[]{:S(2)}) copy-start(f32[1792,256]{1,0:T(8,128)} %get-tuple-element.223) | copy-start | bytes 5505028
  377.1 106.7 %collective-permute-start.2 = (bf16[256,256]{1,0:T(8,128)(2,1)}, bf16[256,256]{1,0:T(8,128)(2,1)}, u32[]{:S(2)}, u32[]{:S(2)}) collective-permute-start(bf16[256,256]{1,0:T(8,128)(2,1)} %get-tuple-element.210), channel_id=1, source_target_pairs={{0,30},{2,0},{4,2},{6,4},{8,6},{10,8},{12,10},{14,12},{16,14},{18,... | collective-permute-start | bytes 393224 | tf_op jit(solution)/shard_map/ppermute | solution.py:12
  381.5 100.9 %collective-permute-start.3 = (bf16[256,256]{1,0:T(8,128)(2,1)}, bf16[256,256]{1,0:T(8,128)(2,1)}, u32[]{:S(2)}, u32[]{:S(2)}) collective-permute-start(bf16[256,256]{1,0:T(8,128)(2,1)} %get-tuple-element.211), channel_id=1, source_target_pairs={{0,2},{2,4},{4,6},{6,8},{8,10},{10,12},{12,14},{14,16},{16,18},{18... | collective-permute-start | bytes 393224 | tf_op jit(solution)/shard_map/ppermute | solution.py:12
  402.1 15.4 %copy-start.6 = (bf16[1280,256]{0,1:T(8,128)(2,1)S(1)}, bf16[1280,256]{0,1:T(8,128)(2,1)}, u32[]{:S(2)}) copy-start(bf16[1280,256]{0,1:T(8,128)(2,1)} %copy-done.5) | copy-start | bytes 1966084
  402.1 15.4 %copy-start.9 = (bf16[1280,256]{1,0:T(8,128)(2,1)S(1)}, bf16[1280,256]{1,0:T(8,128)(2,1)}, u32[]{:S(2)}) copy-start(bf16[1280,256]{1,0:T(8,128)(2,1)} %copy-done.8) | copy-start | bytes 1966084
  402.1 15.5 %copy-start.19 = (bf16[512,256]{1,0:T(8,128)(2,1)S(1)}, bf16[512,256]{1,0:T(8,128)(2,1)}, u32[]{:S(2)}) copy-start(bf16[512,256]{1,0:T(8,128)(2,1)} %param.33) | copy-start | bytes 786436
  433.1 49.2 %copy-start.26 = (s32[1,1,256]{2,1,0:T(1,128)S(1)}, s32[1,1,256]{2,1,0:T(1,128)}, u32[]{:S(2)}) copy-start(s32[1,1,256]{2,1,0:T(1,128)} %copy-done.25) | copy-start | bytes 3076
  433.2 50.6 %copy-start.24 = (s32[1,1,256]{2,1,0:T(1,128)S(1)}, s32[1,1,256]{2,1,0:T(1,128)}, u32[]{:S(2)}) copy-start(s32[1,1,256]{2,1,0:T(1,128)} %copy-done.23) | copy-start | bytes 3076
  (17 other events, 160.1 us)
Sparse Core Ops, SparseCore 0:
  417.6 135.2 all-reduce.3
where the time goes:
time: 574 us; the launch traced here: 567 us
  matrix products  181 us (32%)
  local copies, waits for them, and re-layouts  160 us (28%)
  other arithmetic  95.6 us (17%)
  waiting for transfers between devices  66.3 us (12%)
  blocking collectives  39 us (7%)
  between operations  14.8 us (3%)
  starting transfers between devices  9.92 us (2%)
    dot_general x18, matrix products, outer_sum(): lax.dot_general(left, right, (((0,), (0,)), ((), ())), preferred_element_...  77.7 us
    psum x1, waiting for transfers between devices, body(): lax.psum((g_edge_first, g_edge_first_bias, g_edge_second, g_edge_second_b...  66.2 us
    dot_general x17, matrix products, matmul(): return jnp.dot(left, right, preferred_element_type=jnp.float32)  64.5 us
    psum x1, blocking collectives, body(): lax.psum((g_edge_first, g_edge_first_bias, g_edge_second, g_edge_second_b...  39 us
    unnamed x86, local copies, waits for them, and re-layouts  36.4 us
    dot_general x6, matrix products, back_mul(): lax.dot_general(left, right, (((1,), (1,)), ((), ())), preferred_element_...  34 us
    mul x2, local copies, waits for them, and re-layouts, body(): grad_gathered[:, None, :] * valid.astype(jnp.float32)[:, :, None]  26.7 us
    reshape x1, local copies, waits for them, and re-layouts, body(): (message * weights).reshape(node_count, degree, width)  19.3 us
  transfers between devices with their start and end apart: 5, of which 1 were waited for; matrix products, arithmetic and copies ran while one was open for 22% of the time, Pallas kernels for 0%

commit v1 on v0

v1 whole, which is shorter than its diff:
```python
import functools

import jax
import jax.numpy as jnp
from jax import lax
from jax.experimental import pallas as pl
from jax.experimental.pallas import tpu as pltpu
from jax.sharding import PartitionSpec as P

F32 = jnp.float32
BF16 = jnp.bfloat16
LANES = 128
BLOCK = 128
NODE_BLOCK = 256
BOTH = ("face", "sub")
VMEM_LIMIT = 60 * 1024 * 1024


def params(limit=VMEM_LIMIT):
    return pltpu.CompilerParams(vmem_limit_bytes=limit)


def cost(flops, moved):
    return pl.CostEstimate(flops=int(flops), bytes_accessed=int(moved), transcendentals=0)


def dot(left, right):
    return jnp.dot(left, right, preferred_element_type=F32)


def dot_rows(left, right):
    return lax.dot_general(left, right, (((0,), (0,)), ((), ())), preferred_element_type=F32)


def dot_back(left, right):
    return lax.dot_general(left, right, (((1,), (1,)), ((), ())), preferred_element_type=F32)


def down(row):
    return jnp.broadcast_to(row, (LANES, LANES)).T


def hot_lanes(index, first, count):
    lane = lax.broadcasted_iota(jnp.int32, (1, LANES), 1)
    tiles = [
        jnp.where(index == lane + (first + t * LANES), 1.0, 0.0).astype(BF16)
        for t in range(count // LANES)
    ]
    return jnp.concatenate(tiles, axis=1)


def hot_rows(index, first, count):
    row = lax.broadcasted_iota(jnp.int32, (count, 1), 0) + first
    return jnp.where(row == index, 1.0, 0.0).astype(BF16)


def row_mean(values):
    return jnp.mean(values, axis=-1, keepdims=True)


def col_sum(values):
    return jnp.sum(values, axis=0, keepdims=True)


def gate(values):
    sigma = 0.5 * jnp.tanh(0.5 * values) + 0.5
    act = values * sigma
    return act, sigma + act * (1.0 - sigma)


def norm(values):
    centre = values - row_mean(values)
    scale = lax.rsqrt(row_mean(centre * centre) + 1e-05)
    return centre * scale, scale


def pick_kernel(lists_ref, nodes_ref, next_ref, prev_ref):
    rows = nodes_ref.shape[0]
    halo = lists_ref.shape[1]
    for side, out_ref in ((0, next_ref), (1, prev_ref)):
        for at in range(0, halo, LANES):
            index = down(lists_ref[side : side + 1, at : at + LANES])
            out_ref[at : at + LANES, :] = dot(
                hot_lanes(index, 0, rows), nodes_ref[...]
            ).astype(BF16)


def pick(lists, nodes):
    halo, width = lists.shape[1], nodes.shape[1]
    out = jax.ShapeDtypeStruct((halo, width), BF16)
    return pl.pallas_call(
        pick_kernel,
        out_shape=(out, out),
        compiler_params=params(),
        cost_estimate=cost(4 * halo * nodes.size, 2 * nodes.size),
        name="pick_rows",
    )(lists, nodes)


def own_kernel(index_ref, nodes_ref, out_ref):
    rows = nodes_ref.shape[0]
    for k in range(index_ref.shape[0]):
        index = down(index_ref[k : k + 1, :])
        out_ref[k] = dot(hot_lanes(index, 0, rows), nodes_ref[...]).astype(BF16)


def own_senders(index, nodes):
    degree, rows = index.shape
    width = nodes.shape[1]
    return pl.pallas_call(
        own_kernel,
        grid=(rows // BLOCK,),
        in_specs=[
            pl.BlockSpec((degree, BLOCK), lambda i: (0, i)),
            pl.BlockSpec((rows, width), lambda i: (0, 0)),
        ],
        out_specs=pl.BlockSpec((degree, BLOCK, width), lambda i: (0, i, 0)),
        out_shape=jax.ShapeDtypeStruct((degree, rows, width), BF16),
        compiler_params=params(),
        cost_estimate=cost(2 * degree * rows * rows * width, 2 * degree * rows * width),
        name="own_senders",
    )(index, nodes)


def main_kernel(
    blocks,
    part_rows,
    place_ref,
    index_ref,
    valid_ref,
    edges_ref,
    own_ref,
    nodes_ref,
    halo_ref,
    cot_ref,
    vec_ref,
    w_first_ref,
    w_second_ref,
    n_first_ref,
    n_second_ref,
    mixed_ref,
    grad_nodes_ref,
    grad_a_ref,
    away_ref,
    keep_ref,
    snd_scr,
    act_scr,
    slope_scr,
    hat_scr,
    scale_scr,
    sum_scr,
    count_scr,
    up_scr,
    sec_scr,
    acc_scr,
):
    step = pl.program_id(0)
    degree = index_ref.shape[0]
    rows, width = nodes_ref.shape
    block = rows // blocks
    e_b1, e_b2, e_gain, e_shift, n_b1, n_b2, n_gain, n_shift = (
        vec_ref[i : i + 1, :] for i in range(8)
    )
    at_first, at_second = 0, 3 * width
    at_nfirst, at_nsecond, at_vec = 4 * width, 6 * width, 7 * width

    @pl.when(step < blocks)
    def forward():
        here = pl.ds(pl.multiple_of(step * block, block), block)
        joint = index_ref[...] * 2 + valid_ref[...]
        base = dot(nodes_ref[here, :], w_first_ref[:width, :]) + e_b1
        total = jnp.zeros((block, width), F32)
        count = jnp.zeros((block, LANES), F32)
        for k in range(degree):
            column = down(joint[k : k + 1, :])
            live = (column & 1).astype(F32)
            picked = dot(hot_lanes(column >> 1, rows, halo_ref.shape[0]), halo_ref[...])
            snd = (picked + own_ref[k].astype(F32)).astype(BF16)
            snd_scr[step, k] = snd
            joined = jnp.concatenate([snd, edges_ref[k]], axis=1)
            act, slope = gate(dot(joined, w_first_ref[width:, :]) + base)
            act = act.astype(BF16)
            act_scr[step, k] = act
            slope_scr[step, k] = slope.astype(BF16)
            hat, scale = norm(dot(act, w_second_ref[...]) + e_b2)
            hat_scr[step, k] = hat.astype(BF16)
            scale_scr[step, k] = scale * live
            total = total + hat * jnp.concatenate([live] * (width // LANES), axis=1)
            count = count + live
        sum_scr[here, :] = total
        count_scr[here, :] = count

    @pl.when(step == blocks)
    def node_stage():
        acc_scr[...] = jnp.zeros(acc_scr.shape, F32)

        @pl.loop(0, rows // NODE_BLOCK)
        def one_part(part):
            here = pl.ds(pl.multiple_of(part * NODE_BLOCK, NODE_BLOCK), NODE_BLOCK)
            x = nodes_ref[here, :]
            sums = sum_scr[here, :]
            counts = jnp.concatenate([count_scr[here, :]] * (width // LANES), axis=1)
            gathered = (sums * e_gain + counts * e_shift).astype(BF16)
            act, slope = gate(
                dot(jnp.concatenate([x, gathered], axis=1), n_first_ref[...]) + n_b1
            )
            act = act.astype(BF16)
            hat, scale = norm(dot(act, n_second_ref[...]) + n_b2)
            mixed_ref[here, :] = (x.astype(F32) + (hat * n_gain + n_shift)).astype(BF16)
            up = cot_ref[here, :].astype(F32)
            acc_scr[at_vec + 6 : at_vec + 7, :] += col_sum(up * hat)
            acc_scr[at_vec + 7 : at_vec + 8, :] += col_sum(up)
            scaled = up * n_gain
            grad_d = scale * (scaled - row_mean(scaled) - hat * row_mean(scaled * hat))
            grad_d = grad_d.astype(BF16)
            acc_scr[at_nsecond : at_nsecond + width, :] += dot_rows(act, grad_d)
            acc_scr[at_vec + 5 : at_vec + 6, :] += col_sum(grad_d.astype(F32))
            grad_c = (dot_back(grad_d, n_second_ref[...]) * slope).astype(BF16)
            acc_scr[at_nfirst : at_nfirst + width, :] += dot_rows(x, grad_c)
            acc_scr[at_nfirst + width : at_nfirst + 2 * width, :] += dot_rows(
                gathered, grad_c
            )
            acc_scr[at_vec + 4 : at_vec + 5, :] += col_sum(grad_c.astype(F32))
            grad_nodes_ref[here, :] = up + dot_back(grad_c, n_first_ref[:width, :])
            back = dot_back(grad_c, n_first_ref[width:, :])
            acc_scr[at_vec + 2 : at_vec + 3, :] += col_sum(back * sums)
            acc_scr[at_vec + 3 : at_vec + 4, :] += col_sum(back * counts)
            back = back * e_gain
            up_scr[here, :] = back - row_mean(back)

    @pl.when(step >= blocks)
    def backward():
        now = step - blocks
        here = pl.ds(pl.multiple_of(now * block, block), block)
        up = up_scr[here, :]
        total_a = jnp.zeros((block, width), F32)
        total_b = jnp.zeros((block, width), F32)
        for k in range(degree):
            hat = hat_scr[now, k].astype(F32)
            scale = jnp.concatenate([scale_scr[now, k]] * (width // LANES), axis=1)
            grad_b = (scale * (up - hat * row_mean(up * hat))).astype(BF16)
            sec_scr[k] = grad_b
            total_b = total_b + grad_b.astype(F32)
            grad_a = dot_back(grad_b, w_second_ref[...]) * slope_scr[now, k].astype(F32)
            grad_a = grad_a.astype(BF16)
            grad_a_ref[k] = grad_a
            total_a = total_a + grad_a.astype(F32)
        flat = degree * block
        all_a = grad_a_ref[...].reshape(flat, width)
        acc_scr[at_second : at_second + width, :] += dot_rows(
            act_scr[now].reshape(flat, width), sec_scr[...].reshape(flat, width)
        )
        acc_scr[at_first + width : at_first + 2 * width, :] += dot_rows(
            snd_scr[now].reshape(flat, width), all_a
        )
        acc_scr[at_first + 2 * width : at_first + 3 * width, :] += dot_rows(
            edges_ref[...].reshape(flat, width), all_a
        )
        received = total_a.astype(BF16)
        acc_scr[at_first : at_first + width, :] += dot_rows(nodes_ref[here, :], received)
        grad_nodes_ref[here, :] += dot_back(received, w_first_ref[:width, :])
        acc_scr[at_vec : at_vec + 1, :] += col_sum(total_a)
        acc_scr[at_vec + 1 : at_vec + 2, :] += col_sum(total_b)

    @pl.when(step == 2 * blocks - 1)
    def hand_over():
        place = place_ref[0]
        half = keep_ref.shape[0] // part_rows
        for p in range(2 * half):
            start = pl.multiple_of((place ^ p) * part_rows, 16)
            piece = acc_scr[pl.ds(start, part_rows), :]
            if p < half:
                keep_ref[p * part_rows : (p + 1) * part_rows, :] = piece
            else:
                out = (p - half) * part_rows
                away_ref[out : out + part_rows, :] = piece.astype(BF16)


def main(place, index, valid, edges, own, nodes, halo, cot, vec, w1, w2, n1, n2, parts):
    degree, rows, width = edges.shape
    blocks = rows // BLOCK
    grad_rows = w1.shape[0] + w2.shape[0] + n1.shape[0] + n2.shape[0] + 8
    part_rows = -(-grad_rows // (16 * parts)) * 16
    total = part_rows * parts

    def blocked(first):
        return lambda i, *_: first(jnp.where(i < blocks, i, i - blocks))

    def whole(array):
        zeros = (0,) * array.ndim
        return pl.BlockSpec(array.shape, lambda i, *_: zeros, pipeline_mode=pl.Buffered(1))

    edge_spec = pl.BlockSpec((degree, BLOCK, width), blocked(lambda i: (0, i, 0)))
    flag_spec = pl.BlockSpec((degree, BLOCK), blocked(lambda i: (0, i)))
    own_spec = pl.BlockSpec(
        (degree, BLOCK, width), lambda i, *_: (0, jnp.minimum(i, blocks - 1), 0)
    )
    out_spec = pl.BlockSpec(
        (degree, BLOCK, width), lambda i, *_: (0, jnp.maximum(i - blocks, 0), 0)
    )
    half = jax.ShapeDtypeStruct((total // 2, width), BF16)
    keep = jax.ShapeDtypeStruct((total // 2, width), F32)
    grid_spec = pltpu.PrefetchScalarGridSpec(
        num_scalar_prefetch=1,
        grid=(2 * blocks,),
        in_specs=[flag_spec, flag_spec, edge_spec, own_spec]
        + [whole(a) for a in (nodes, halo, cot, vec, w1, w2, n1, n2)],
        out_specs=(whole(nodes), whole(nodes), out_spec, whole(half), whole(keep)),
        scratch_shapes=[
            pltpu.VMEM((blocks, degree, BLOCK, width), BF16),
            pltpu.VMEM((blocks, degree, BLOCK, width), BF16),
            pltpu.VMEM((blocks, degree, BLOCK, width), BF16),
            pltpu.VMEM((blocks, degree, BLOCK, width), BF16),
            pltpu.VMEM((blocks, degree, BLOCK, LANES), F32),
            pltpu.VMEM((rows, width), F32),
            pltpu.VMEM((rows, LANES), F32),
            pltpu.VMEM((rows, width), F32),
            pltpu.VMEM((degree, BLOCK, width), BF16),
            pltpu.VMEM((total, width), F32),
        ],
    )
    return pl.pallas_call(
        functools.partial(main_kernel, blocks, part_rows),
        grid_spec=grid_spec,
        out_shape=(
            jax.ShapeDtypeStruct((rows, width), BF16),
            jax.ShapeDtypeStruct((rows, width), F32),
            jax.ShapeDtypeStruct((degree, rows, width), BF16),
            half,
            keep,
        ),
        compiler_params=params(),
        cost_estimate=cost(18 * degree * rows * width * width, 8 * edges.size),
        name="edges_and_nodes",
    )(place, index, valid, edges, own, nodes, halo, cot, vec, w1, w2, n1, n2)


def split_back(total, weight):
    high = total.astype(BF16)
    low = (total - high.astype(F32)).astype(BF16)
    return dot_back(high, weight) + dot_back(low, weight)


def spread_kernel(first, index_ref, grad_ref, weight_ref, *rest):
    *extra, out_ref, total = rest
    step = pl.program_id(0)
    degree, block, width = grad_ref.shape
    rows = total.shape[0]
    index = index_ref[...]
    hot = jnp.concatenate(
        [hot_rows(index[k : k + 1, :], first, rows) for k in range(degree)], axis=1
    )
    part = dot(hot, grad_ref[...].reshape(degree * block, width))

    @pl.when(step == 0)
    def start():
        total[...] = part

    @pl.when(step > 0)
    def go_on():
        total[...] += part

    @pl.when(step == pl.num_programs(0) - 1)
    def finish():
        result = split_back(total[...], weight_ref[...])
        if extra:
            result = result + extra[0][...]
        out_ref[...] = result.astype(out_ref.dtype)


def spread(index, grad, weight, first, rows, dtype, extra=None):
    degree, count, width = grad.shape
    base = []
    if extra is not None:
        base = [pl.BlockSpec((rows, width), lambda i: (first // rows, 0))]
    return pl.pallas_call(
        functools.partial(spread_kernel, first),
        grid=(count // BLOCK,),
        in_specs=[
            pl.BlockSpec((degree, BLOCK), lambda i: (0, i)),
            pl.BlockSpec((degree, BLOCK, width), lambda i: (0, i, 0)),
            pl.BlockSpec(weight.shape, lambda i: (0, 0)),
        ]
        + base,
        out_specs=pl.BlockSpec((rows, width), lambda i: (0, 0)),
        out_shape=jax.ShapeDtypeStruct((rows, width), dtype),
        scratch_shapes=[pltpu.VMEM((rows, width), F32)],
        compiler_params=params(),
        cost_estimate=cost(2 * rows * grad.size, 2 * grad.size),
        name="spread_rows",
    )(index, grad, weight, *([] if extra is None else [extra]))


def edge_kernel(grad_ref, weight_ref, out_ref):
    degree, block, width = grad_ref.shape
    grad = grad_ref[...].reshape(degree * block, width)
    out_ref[...] = dot_back(grad, weight_ref[...]).astype(BF16).reshape(degree, block, width)


def edge_grads(grad, weight):
    degree, count, width = grad.shape
    spec = pl.BlockSpec((degree, BLOCK, width), lambda i: (0, i, 0))
    return pl.pallas_call(
        edge_kernel,
        grid=(count // BLOCK,),
        in_specs=[spec, pl.BlockSpec(weight.shape, lambda i: (0, 0))],
        out_specs=spec,
        out_shape=jax.ShapeDtypeStruct(grad.shape, BF16),
        compiler_params=params(),
        cost_estimate=cost(2 * grad.size * width, 4 * grad.size),
        name="edge_grads",
    )(grad, weight)


def final_kernel(lists_ref, low_ref, high_ref, next_ref, prev_ref, out_ref):
    rows = out_ref.shape[0]
    low = low_ref.shape[0]
    for first, part_ref in ((0, low_ref), (low, high_ref)):
        count = part_ref.shape[0]
        out_ref[first : first + count, :] = (
            part_ref[...]
            + dot(hot_rows(lists_ref[0:1, :], first, count), next_ref[...])
            + dot(hot_rows(lists_ref[1:2, :], first, count), prev_ref[...])
        )


def final(lists, low, high, ret_next, ret_prev):
    rows = low.shape[0] + high.shape[0]
    width = low.shape[1]
    return pl.pallas_call(
        final_kernel,
        out_shape=jax.ShapeDtypeStruct((rows, width), F32),
        compiler_params=params(),
        cost_estimate=cost(4 * rows * ret_next.size, 8 * rows * width),
        name="returned_rows",
    )(lists, low, high, ret_next, ret_prev)


def add_kernel(keep_ref, came_ref, away_ref, out_ref):
    half = out_ref.shape[0]
    out_ref[...] = keep_ref[:half, :] + came_ref[:half, :].astype(F32)
    away_ref[...] = (keep_ref[half:, :] + came_ref[half:, :].astype(F32)).astype(BF16)


def add_and_split(keep, came):
    half, width = keep.shape[0] // 2, keep.shape[1]
    return pl.pallas_call(
        add_kernel,
        out_shape=(
            jax.ShapeDtypeStruct((half, width), BF16),
            jax.ShapeDtypeStruct((half, width), F32),
        ),
        compiler_params=params(),
        cost_estimate=cost(keep.size, 8 * keep.size),
        name="add_and_split",
    )(keep, came)


def unpack_kernel(part_rows, place_ref, *refs):
    pieces, outs, full = refs[:4], refs[4:-1], refs[-1]
    place = place_ref[0]
    p = 0
    for piece in pieces:
        for at in range(0, piece.shape[0], part_rows):
            start = pl.multiple_of((place ^ p) * part_rows, 16)
            full[pl.ds(start, part_rows), :] = piece[at : at + part_rows, :].astype(F32)
            p += 1
    at = 0
    for out_ref in outs:
        count = out_ref.shape[0]
        out_ref[...] = full[at : at + count, :]
        at += count


def unpack(place, pieces, row_counts):
    part_rows, width = pieces[0].shape
    total = 8 * part_rows
    return pl.pallas_call(
        functools.partial(unpack_kernel, part_rows),
        in_specs=[pl.BlockSpec(memory_space=pltpu.SMEM)]
        + [pl.BlockSpec(memory_space=pltpu.VMEM)] * 4,
        out_shape=tuple(jax.ShapeDtypeStruct((n, width), F32) for n in row_counts),
        scratch_shapes=[pltpu.VMEM((total, width), F32)],
        compiler_params=params(),
        name="unpack_sums",
    )(place, *pieces)


def traded(value, mask):
    count = lax.axis_size("face") * lax.axis_size("sub")
    return lax.ppermute(value, BOTH, [(i, i ^ mask) for i in range(count)])


def passed_along(value, steps):
    count = lax.axis_size("face")
    pairs = [(source, (source + steps) % count) for source in range(count)]
    return lax.ppermute(value, "face", pairs)


def body(
    nodes,
    edges,
    neighbours,
    valid,
    send_lists,
    edge_first,
    edge_first_bias,
    edge_second,
    edge_second_bias,
    edge_gain,
    edge_shift,
    node_first,
    node_first_bias,
    node_second,
    node_second_bias,
    node_gain,
    node_shift,
    cotangent,
):
    rows, width = nodes.shape
    lists = send_lists[0]
    halo_rows = lists.shape[1]
    index = neighbours.T
    flags = valid.T
    edge_rows = jnp.transpose(edges, (1, 0, 2))
    vec = jnp.stack(
        [
            edge_first_bias,
            edge_second_bias,
            edge_gain,
            edge_shift,
            node_first_bias,
            node_second_bias,
            node_gain,
            node_shift,
        ]
    ).astype(F32)
    subs = lax.axis_size("sub")
    me = lax.axis_index("face") * subs + lax.axis_index("sub")
    devices = lax.axis_size("face") * subs
    masks = [1 << b for b in range(devices.bit_length() - 1)]
    masks = [subs] + [m for m in masks if m != subs]
    halving, doubling = masks[:3], masks[3:]
    place = jnp.int32(0)
    for mask in halving:
        place = place * 2 + jnp.where((me & mask) != 0, 1, 0)
    place = place.astype(jnp.int32).reshape(1)

    to_next, to_prev = pick(lists, nodes)
    from_prev = passed_along(to_next, 1)
    from_next = passed_along(to_prev, -1)
    own = own_senders(index, nodes)
    halo = jnp.concatenate([from_prev, from_next], axis=0)
    mixed, grad_nodes, grad_a, away, keep = main(
        place,
        index,
        flags,
        edge_rows,
        own,
        nodes,
        halo,
        cotangent,
        vec,
        edge_first,
        edge_second,
        node_first,
        node_second,
        1 << len(halving),
    )
    send_weight = edge_first[width : 2 * width]
    edge_weight = edge_first[2 * width :]

    came = traded(away, halving[0])
    for mask in halving[1:]:
        away, keep = add_and_split(keep, came)
        came = traded(away, mask)
    part = (keep + came.astype(F32)).astype(BF16)
    for mask in doubling:
        part = (part.astype(F32) + traded(part, mask).astype(F32)).astype(BF16)

    back = spread(index, grad_a, send_weight, rows, 2 * halo_rows, BF16)
    ret_next = passed_along(back[:halo_rows], -1)
    ret_prev = passed_along(back[halo_rows:], 1)
    half = rows // 2
    low = spread(index, grad_a, send_weight, 0, half, F32, grad_nodes)
    high = spread(index, grad_a, send_weight, half, half, F32, grad_nodes)
    grad_edges = edge_grads(grad_a, edge_weight)
    grad_nodes = final(lists, low, high, ret_next, ret_prev)

    pieces = [part]
    held = part
    for mask in halving[::-1]:
        came = traded(held, mask)
        pieces.append(came)
        held = jnp.concatenate([held, came], axis=0)
    counts = (edge_first.shape[0], width, node_first.shape[0], width) + (1,) * 8
    sums = unpack(place, pieces, counts)
    vectors = [v.reshape(width) for v in sums[4:]]
    return (
        mixed,
        grad_nodes,
        jnp.transpose(grad_edges, (1, 0, 2)),
        sums[0],
        vectors[0],
        sums[1],
        vectors[1],
        vectors[2],
        vectors[3],
        sums[2],
        vectors[4],
        sums[3],
        vectors[5],
        vectors[6],
        vectors[7],
    )


def solution(mesh):
    shared = P(("face", "sub"), None)
    split3 = P(("face", "sub"), None, None)
    return jax.shard_map(
        body,
        mesh=mesh,
        in_specs=(shared, split3, shared, shared, split3) + (P(),) * 12 + (shared,),
        out_specs=(shared, shared, split3) + (P(),) * 12,
        check_vma=False,
    )
```

time: 574 us -> 176 us (0.31)
  matrix products: 181 us -> 0 us
  local copies, waits for them, and re-layouts: 160 us -> 5.38 us
  Pallas kernels: 0 us -> 132 us
  other arithmetic: 95.6 us -> 2.41 us
  waiting for transfers between devices: 66.3 us -> 19.5 us
  blocking collectives: 39 us -> 0 us
  between operations: 14.8 us -> 1.08 us
    dot_general x43 -> x0, matrix products: 181 us -> none  [the longest x18 77.7 us: outer_sum(): lax.dot_general(left, right, (((0,), (0,)), ((), ())), preferred_element_...]
    pallas_call x0 -> x11, Pallas kernels: none -> 132 us  [the longest x1 59.5 us: main(): pl.pallas_call(functools.partial(main_kernel, blocks, part_rows), grid_sp...]
    reshape x5 -> x0, local copies, waits for them, and re-layouts: 78.9 us -> none  [the longest x1 19.3 us: body(): (message * weights).reshape(node_count, degree, width)]
    reduce_sum x9 -> x0, other arithmetic: 74.3 us -> none  [the longest x1 16.2 us: body(): g_edge_gain = jnp.sum(grad_message * normal_b, axis=0)]
    psum x1 -> x0, waiting for transfers between devices: 66.2 us -> none  [body(): lax.psum((g_edge_first, g_edge_first_bias, g_edge_second, g_edge_second_b...]
    psum x1 -> x0, blocking collectives: 39 us -> none  [body(): lax.psum((g_edge_first, g_edge_first_bias, g_edge_second, g_edge_second_b...]
    unnamed x86 -> x34, local copies, waits for them, and re-layouts: 36.4 us -> 3.61 us
    mul x3 -> x0, local copies, waits for them, and re-layouts: 27.2 us -> none  [the longest x2 26.7 us: body(): grad_gathered[:, None, :] * valid.astype(jnp.float32)[:, :, None]]
  transfers between devices with their start and end apart: 5 -> 12, of which waited for: 1 -> 5; matrix products, arithmetic and copies ran while one was open for 22% -> 1% of each run, Pallas kernels for 0% -> 37%
where the time goes in v1:
time: 176 us; the launch traced here: 174 us
  Pallas kernels  132 us (75%)
  waiting for transfers between devices  19.5 us (11%)
  starting transfers between devices  13.2 us (8%)
  local copies, waits for them, and re-layouts  5.38 us (3%)
  other arithmetic  2.41 us (1%)
    pallas_call x1, Pallas kernels, main(): pl.pallas_call(functools.partial(main_kernel, blocks, part_rows), grid_sp...  59.5 us
    pallas_call x3, Pallas kernels, spread(): pl.pallas_call(functools.partial(spread_kernel, first), grid=(count // BL...  34.8 us
    ppermute x8, waiting for transfers between devices, traded(): return lax.ppermute(value, BOTH, [(i, i ^ mask) for i in range(count)])  19.5 us
    pallas_call x1, Pallas kernels, own_senders(): pl.pallas_call(own_kernel, grid=(rows // BLOCK,), in_specs=[pl.BlockSpec(...  14.9 us
    pallas_call x1, Pallas kernels, edge_grads(): pl.pallas_call(edge_kernel, grid=(count // BLOCK,), in_specs=[spec, pl.Bl...  11.2 us
    ppermute x8, starting transfers between devices, traded(): return lax.ppermute(value, BOTH, [(i, i ^ mask) for i in range(count)])  7.19 us
    ppermute x4, starting transfers between devices, passed_along(): return lax.ppermute(value, 'face', pairs)  6.01 us
    pallas_call x2, Pallas kernels, add_and_split(): pl.pallas_call(add_kernel, out_shape=(jax.ShapeDtypeStruct((half, width),...  4.07 us
  transfers between devices with their start and end apart: 12, of which 5 were waited for; matrix products, arithmetic and copies ran while one was open for 1% of the time, Pallas kernels for 37%

profile of v1, /device:TPU:0, one launch (start us, length us, event | category | flops | bytes accessed | tf_op | source)
XLA Modules:
  0.0 174.0 jit_solution(11983436890815334334)
XLA Ops:
  0.6 2.3 %pick_rows.1 = (bf16[256,256]{1,0:T(8,128)(2,1)}, bf16[256,256]{1,0:T(8,128)(2,1)}) custom-call(s32[2,256]{1,0:T(2,128)} %bitcast.15, bf16[1280,256]{1,0:T(8,128)(2,1)} %nodes_ref.5), custom_call_target="tpu_custom_call" | custom-call | flops 335544320 | bytes 655360 | tf_op jit(solution)/shard_map/pick_rows/pallas_call | solution.py:91
  3.0 5.4 %collective-permute-start.1 = (bf16[256,256]{1,0:T(8,128)(2,1)}, bf16[256,256]{1,0:T(8,128)(2,1)S(1)}, u32[]{:S(2)}, u32[]{:S(2)}) collective-permute-start(bf16[256,256]{1,0:T(8,128)(2,1)} %get-tuple-element.39), channel_id=1, source_target_pairs={{0,30},{2,0},{4,2},{6,4},{8,6},{10,8},{12,10},{14,12},{16,14},{18,... | collective-permute-start | bytes 393224 | tf_op jit(solution)/shard_map/ppermute | solution.py:497
  8.5 14.9 %own_senders.1.own_ref = bf16[12,1280,256]{2,1,0:T(8,128)(2,1)} custom-call(s32[12,1280]{1,0:T(8,128)} %bitcast.19, bf16[1280,256]{1,0:T(8,128)(2,1)} %nodes_ref.5), custom_call_target="tpu_custom_call" | custom-call | flops 10066329600 | bytes 7864320 | tf_op jit(solution)/shard_map/own_senders/pallas_call | solution.py:110
  24.9 59.5 %edges_and_nodes.1 = (bf16[1280,256]{1,0:T(8,128)(2,1)}, f32[1280,256]{1,0:T(8,128)}, bf16[12,1280,256]{2,1,0:T(8,128)(2,1)}, bf16[960,256]{1,0:T(8,128)(2,1)}, f32[960,256]{1,0:T(8,128)}) custom-call(s32[1]{0:T(128)} %bitcast.place_ref, s32[12,1280]{1,0:T(8,128)} %bitcast.20, s32[12,1280]{1,0:T(8,128)} %bitcast.18, bf16[12,1280,256]{2,1,0:T(8,128)(2,1)} %bitcast.17, ...), custom_call_target="tpu_custom_call" | custom-call | flops 18119393280 | bytes 31457280 | tf_op jit(solution)/shard_map/edges_and_nodes/pallas_call | solution.py:322
  84.5 2.1 %collective-permute-done.4.came_ref = bf16[960,256]{1,0:T(8,128)(2,1)S(1)} collective-permute-done((bf16[960,256]{1,0:T(8,128)(2,1)}, bf16[960,256]{1,0:T(8,128)(2,1)S(1)}, u32[]{:S(2)}, u32[]{:S(2)}) %collective-permute-start.4) | collective-permute-done | bytes 491552 | tf_op jit(solution)/shard_map/ppermute | solution.py:491
  86.6 0.8 copy-done.4
  87.4 2.2 %add_and_split.2 = (bf16[480,256]{1,0:T(8,128)(2,1)}, f32[480,256]{1,0:T(8,128)}) custom-call(f32[960,256]{1,0:T(8,128)} %get-tuple-element.43.keep_ref, bf16[960,256]{1,0:T(8,128)(2,1)} %copy-done.4), custom_call_target="tpu_custom_call" | custom-call | flops 245760 | bytes 1966080 | tf_op jit(solution)/shard_map/add_and_split/pallas_call | solution.py:447
  89.6 1.5 collective-permute-start.5
  91.1 6.7 %collective-permute-done.5.came_ref = bf16[480,256]{1,0:T(8,128)(2,1)S(1)} collective-permute-done((bf16[480,256]{1,0:T(8,128)(2,1)}, bf16[480,256]{1,0:T(8,128)(2,1)S(1)}, u32[]{:S(2)}, u32[]{:S(2)}) %collective-permute-start.5) | collective-permute-done | bytes 245792 | tf_op jit(solution)/shard_map/ppermute | solution.py:491
  98.5 1.8 %add_and_split.3 = (bf16[240,256]{1,0:T(8,128)(2,1)}, f32[240,256]{1,0:T(8,128)}) custom-call(f32[480,256]{1,0:T(8,128)} %get-tuple-element.45.keep_ref, bf16[480,256]{1,0:T(8,128)(2,1)} %copy-done.5), custom_call_target="tpu_custom_call" | custom-call | flops 122880 | bytes 983040 | tf_op jit(solution)/shard_map/add_and_split/pallas_call | solution.py:447
  100.3 5.1 %collective-permute-done.6 = bf16[240,256]{1,0:T(8,128)(2,1)S(1)} collective-permute-done((bf16[240,256]{1,0:T(8,128)(2,1)}, bf16[240,256]{1,0:T(8,128)(2,1)S(1)}, u32[]{:S(2)}, u32[]{:S(2)}) %collective-permute-start.6) | collective-permute-done | bytes 122912 | tf_op jit(solution)/shard_map/ppermute | solution.py:491
  105.4 1.0 add_convert_fusion.2
  107.2 4.1 %collective-permute-done.7 = bf16[240,256]{1,0:T(8,128)(2,1)S(1)} collective-permute-done((bf16[240,256]{1,0:T(8,128)(2,1)S(1)}, bf16[240,256]{1,0:T(8,128)(2,1)S(1)}, u32[]{:S(2)}, u32[]{:S(2)}) %collective-permute-start.7) | collective-permute-done | bytes 122912 | tf_op jit(solution)/shard_map/ppermute | solution.py:491
  111.4 2.0 %collective-permute-start.8 = (bf16[240,256]{1,0:T(8,128)(2,1)S(1)}, bf16[240,256]{1,0:T(8,128)(2,1)S(1)}, u32[]{:S(2)}, u32[]{:S(2)}) collective-permute-start(bf16[240,256]{1,0:T(8,128)(2,1)S(1)} %add_convert_fusion.1), channel_id=1, source_target_pairs={{0,16},{1,17},{2,18},{3,19},{4,20},{5,21},{6,22},{7,23},{8,24},{9,... | collective-permute-start | bytes 368648 | tf_op jit(solution)/shard_map/ppermute | solution.py:491
  113.4 10.9 %spread_rows.5 = bf16[512,256]{1,0:T(8,128)(2,1)} custom-call(s32[12,1280]{1,0:T(8,128)} %bitcast.21, bf16[12,1280,256]{2,1,0:T(8,128)(2,1)} %get-tuple-element.41.grad_ref, bf16[256,256]{1,0:T(8,128)(2,1)} %get-tuple-element.62.weight_ref), custom_call_target="tpu_custom_call" | custom-call | flops 4026531840 | bytes 7864320 | tf_op jit(solution)/shard_map/spread_rows/pallas_call | solution.py:376
  124.3 1.9 %collective-permute-start.9 = (bf16[240,256]{1,0:T(8,128)(2,1)S(1)}, bf16[240,256]{1,0:T(8,128)(2,1)S(1)}, u32[]{:S(2)}, u32[]{:S(2)}) collective-permute-start(bf16[240,256]{1,0:T(8,128)(2,1)S(1)} %add_convert_fusion.refs_0_), channel_id=1, source_target_pairs={{0,4},{1,5},{2,6},{3,7},{4,0},{5,1},{6,2},{7,3},{8,12},{9,13},{10,... | collective-permute-start | bytes 368648 | tf_op jit(solution)/shard_map/ppermute | solution.py:491
  126.2 1.0 fusion.1
  127.8 1.5 collective-permute-done.9.refs_1_
  129.3 1.6 collective-permute-start.10
  130.9 11.9 %spread_rows.3.low_ref = f32[640,256]{1,0:T(8,128)} custom-call(s32[12,1280]{1,0:T(8,128)} %bitcast.22, bf16[12,1280,256]{2,1,0:T(8,128)(2,1)} %get-tuple-element.41.grad_ref, bf16[256,256]{1,0:T(8,128)(2,1)} %get-tuple-element.62.weight_ref, f32[1280,256]{1,0:T(8,128)} %get-tuple-element.42.rest_0_), custom_call_target="tpu_custom_call" | custom-call | flops 5033164800 | bytes 7864320 | tf_op jit(solution)/shard_map/spread_rows/pallas_call | solution.py:376
  142.9 12.0 %spread_rows.4.high_ref = f32[640,256]{1,0:T(8,128)} custom-call(s32[12,1280]{1,0:T(8,128)} %bitcast.23, bf16[12,1280,256]{2,1,0:T(8,128)(2,1)} %get-tuple-element.41.grad_ref, bf16[256,256]{1,0:T(8,128)(2,1)} %get-tuple-element.62.weight_ref, f32[1280,256]{1,0:T(8,128)} %get-tuple-element.42.rest_0_), custom_call_target="tpu_custom_call" | custom-call | flops 5033164800 | bytes 7864320 | tf_op jit(solution)/shard_map/spread_rows/pallas_call | solution.py:376
  154.9 11.2 %edge_grads.1 = bf16[12,1280,256]{2,1,0:T(8,128)(2,1)} custom-call(bf16[12,1280,256]{2,1,0:T(8,128)(2,1)} %get-tuple-element.41.grad_ref, bf16[256,256]{1,0:T(8,128)(2,1)} %get-tuple-element.61.weight_ref), custom_call_target="tpu_custom_call" | custom-call | flops 2013265920 | bytes 15728640 | tf_op jit(solution)/shard_map/edge_grads/pallas_call | solution.py:403
  167.4 2.9 %returned_rows.1 = f32[1280,256]{1,0:T(8,128)} custom-call(s32[2,256]{1,0:T(2,128)} %bitcast.16, f32[640,256]{1,0:T(8,128)} %spread_rows.3.low_ref, f32[640,256]{1,0:T(8,128)} %spread_rows.4.high_ref, bf16[256,256]{1,0:T(8,128)(2,1)} %copy-done.7, bf16[256,256]{1,0:T(8,128)(2,1)} %copy-done.8), custom_call_target="tpu_custom_call" | custom-call | flops 335544320 | bytes 2621440 | tf_op jit(solution)/shard_map/returned_rows/pallas_call | solution.py:430
  171.1 2.7 %unpack_sums.1 = (f32[768,256]{1,0:T(8,128)}, f32[256,256]{1,0:T(8,128)}, f32[512,256]{1,0:T(8,128)}, f32[256,256]{1,0:T(8,128)}, f32[1,256]{1,0:T(1,128)}, /*in...) custom-call(s32[1]{0:T(128)} %bitcast.place_ref, ...), custom_call_target="tpu_custom_call" | custom-call | tf_op jit(solution)/shard_map/unpack_sums/pallas_call | solution.py:478
  (63 shorter events, 5.8 us)
Async XLA Ops:
  3.0 21.2 %collective-permute-start.1 = (bf16[256,256]{1,0:T(8,128)(2,1)}, bf16[256,256]{1,0:T(8,128)(2,1)S(1)}, u32[]{:S(2)}, u32[]{:S(2)}) collective-permute-start(bf16[256,256]{1,0:T(8,128)(2,1)} %get-tuple-element.39), channel_id=1, source_target_pairs={{0,30},{2,0},{4,2},{6,4},{8,6},{10,8},{12,10},{14,12},{16,14},{18,... | collective-permute-start | bytes 393224 | tf_op jit(solution)/shard_map/ppermute | solution.py:497
  8.4 15.8 %collective-permute-start = (bf16[256,256]{1,0:T(8,128)(2,1)}, bf16[256,256]{1,0:T(8,128)(2,1)S(1)}, u32[]{:S(2)}, u32[]{:S(2)}) collective-permute-start(bf16[256,256]{1,0:T(8,128)(2,1)} %get-tuple-element.38), channel_id=1, source_target_pairs={{0,2},{2,4},{4,6},{6,8},{8,10},{10,12},{12,14},{14,16},{16,18},{18... | collective-permute-start | bytes 393224 | tf_op jit(solution)/shard_map/ppermute | solution.py:497
  8.4 14.9 %copy-start.9 = (bf16[256]{0:T(256)(128)(2,1)S(1)}, bf16[256]{0:T(256)(128)(2,1)}, u32[]{:S(2)}) copy-start(bf16[256]{0:T(256)(128)(2,1)} %param.24) | copy-start | bytes 1540
  8.4 15.0 %copy-start.10 = (bf16[256]{0:T(256)(128)(2,1)S(1)}, bf16[256]{0:T(256)(128)(2,1)}, u32[]{:S(2)}) copy-start(bf16[256]{0:T(256)(128)(2,1)} %param.26) | copy-start | bytes 1540
  8.4 15.0 %copy-start.11 = (bf16[256]{0:T(256)(128)(2,1)S(1)}, bf16[256]{0:T(256)(128)(2,1)}, u32[]{:S(2)}) copy-start(bf16[256]{0:T(256)(128)(2,1)} %param.27) | copy-start | bytes 1540
  8.5 15.0 %copy-start.12 = (bf16[256]{0:T(256)(128)(2,1)S(1)}, bf16[256]{0:T(256)(128)(2,1)}, u32[]{:S(2)}) copy-start(bf16[256]{0:T(256)(128)(2,1)} %param.28) | copy-start | bytes 1540
  8.5 15.0 %copy-start.13 = (bf16[256]{0:T(256)(128)(2,1)S(1)}, bf16[256]{0:T(256)(128)(2,1)}, u32[]{:S(2)}) copy-start(bf16[256]{0:T(256)(128)(2,1)} %param.30) | copy-start | bytes 1540
  8.5 15.0 %copy-start.14 = (bf16[256]{0:T(256)(128)(2,1)S(1)}, bf16[256]{0:T(256)(128)(2,1)}, u32[]{:S(2)}) copy-start(bf16[256]{0:T(256)(128)(2,1)} %param.32) | copy-start | bytes 1540
  8.5 15.0 %copy-start.15 = (bf16[256]{0:T(256)(128)(2,1)S(1)}, bf16[256]{0:T(256)(128)(2,1)}, u32[]{:S(2)}) copy-start(bf16[256]{0:T(256)(128)(2,1)} %param.33) | copy-start | bytes 1540
  8.5 15.0 %copy-start.16 = (bf16[256]{0:T(256)(128)(2,1)S(1)}, bf16[256]{0:T(256)(128)(2,1)}, u32[]{:S(2)}) copy-start(bf16[256]{0:T(256)(128)(2,1)} %param.34) | copy-start | bytes 1540
  24.9 81.6 %copy-start.6 = (bf16[768,256]{1,0:T(8,128)(2,1)S(1)}, bf16[768,256]{1,0:T(8,128)(2,1)}, u32[]{:S(2)}) copy-start(bf16[768,256]{1,0:T(8,128)(2,1)} %w_first_ref.1) | copy-start | bytes 1179652
  84.4 2.1 %collective-permute-start.4 = (bf16[960,256]{1,0:T(8,128)(2,1)}, bf16[960,256]{1,0:T(8,128)(2,1)S(1)}, u32[]{:S(2)}, u32[]{:S(2)}) collective-permute-start(bf16[960,256]{1,0:T(8,128)(2,1)} %get-tuple-element.44), channel_id=1, source_target_pairs={{0,2},{1,3},{2,0},{3,1},{4,6},{5,7},{6,4},{7,5},{8,10},{9,11},{10,... | collective-permute-start | bytes 1474568 | tf_op jit(solution)/shard_map/ppermute | solution.py:491
  89.6 8.2 %collective-permute-start.5 = (bf16[480,256]{1,0:T(8,128)(2,1)}, bf16[480,256]{1,0:T(8,128)(2,1)S(1)}, u32[]{:S(2)}, u32[]{:S(2)}) collective-permute-start(bf16[480,256]{1,0:T(8,128)(2,1)} %get-tuple-element.46), channel_id=1, source_target_pairs={{0,1},{1,0},{2,3},{3,2},{4,5},{5,4},{6,7},{7,6},{8,9},{9,8},{10,11... | collective-permute-start | bytes 737288 | tf_op jit(solution)/shard_map/ppermute | solution.py:491
  100.3 5.1 %collective-permute-start.6 = (bf16[240,256]{1,0:T(8,128)(2,1)}, bf16[240,256]{1,0:T(8,128)(2,1)S(1)}, u32[]{:S(2)}, u32[]{:S(2)}) collective-permute-start(bf16[240,256]{1,0:T(8,128)(2,1)} %get-tuple-element.48), channel_id=1, source_target_pairs={{0,4},{1,5},{2,6},{3,7},{4,0},{5,1},{6,2},{7,3},{8,12},{9,13},{10,... | collective-permute-start | bytes 368648 | tf_op jit(solution)/shard_map/ppermute | solution.py:491
  106.4 4.9 %collective-permute-start.7 = (bf16[240,256]{1,0:T(8,128)(2,1)S(1)}, bf16[240,256]{1,0:T(8,128)(2,1)S(1)}, u32[]{:S(2)}, u32[]{:S(2)}) collective-permute-start(bf16[240,256]{1,0:T(8,128)(2,1)S(1)} %add_convert_fusion.2), channel_id=1, source_target_pairs={{0,8},{1,9},{2,10},{3,11},{4,12},{5,13},{6,14},{7,15},{8,0},{9,1},... | collective-permute-start | bytes 368648 | tf_op jit(solution)/shard_map/ppermute | solution.py:491
  111.4 12.9 %collective-permute-start.8 = (bf16[240,256]{1,0:T(8,128)(2,1)S(1)}, bf16[240,256]{1,0:T(8,128)(2,1)S(1)}, u32[]{:S(2)}, u32[]{:S(2)}) collective-permute-start(bf16[240,256]{1,0:T(8,128)(2,1)S(1)} %add_convert_fusion.1), channel_id=1, source_target_pairs={{0,16},{1,17},{2,18},{3,19},{4,20},{5,21},{6,22},{7,23},{8,24},{9,... | collective-permute-start | bytes 368648 | tf_op jit(solution)/shard_map/ppermute | solution.py:491
  124.3 18.5 %copy-start = (bf16[240,256]{1,0:T(8,128)(2,1)}, bf16[240,256]{1,0:T(8,128)(2,1)S(1)}, u32[]{:S(2)}) copy-start(bf16[240,256]{1,0:T(8,128)(2,1)S(1)} %add_convert_fusion.refs_0_) | copy-start | bytes 368644
  124.3 4.9 %collective-permute-start.9 = (bf16[240,256]{1,0:T(8,128)(2,1)S(1)}, bf16[240,256]{1,0:T(8,128)(2,1)S(1)}, u32[]{:S(2)}, u32[]{:S(2)}) collective-permute-start(bf16[240,256]{1,0:T(8,128)(2,1)S(1)} %add_convert_fusion.refs_0_), channel_id=1, source_target_pairs={{0,4},{1,5},{2,6},{3,7},{4,0},{5,1},{6,2},{7,3},{8,12},{9,13},{10,... | collective-permute-start | bytes 368648 | tf_op jit(solution)/shard_map/ppermute | solution.py:491
  127.2 38.9 %collective-permute-start.2 = (bf16[256,256]{1,0:T(8,128)(2,1)S(1)}, bf16[256,256]{1,0:T(8,128)(2,1)S(1)}, u32[]{:S(2)}, u32[]{:S(2)}) collective-permute-start(bf16[256,256]{1,0:T(8,128)(2,1)S(1)} %get-tuple-element.64), channel_id=1, source_target_pairs={{0,30},{2,0},{4,2},{6,4},{8,6},{10,8},{12,10},{14,12},{16,14},{18,... | collective-permute-start | bytes 393224 | tf_op jit(solution)/shard_map/ppermute | solution.py:497
  127.3 38.9 %collective-permute-start.3 = (bf16[256,256]{1,0:T(8,128)(2,1)S(1)}, bf16[256,256]{1,0:T(8,128)(2,1)S(1)}, u32[]{:S(2)}, u32[]{:S(2)}) collective-permute-start(bf16[256,256]{1,0:T(8,128)(2,1)S(1)} %get-tuple-element.63), channel_id=1, source_target_pairs={{0,2},{2,4},{4,6},{6,8},{8,10},{10,12},{12,14},{14,16},{16,18},{18... | collective-permute-start | bytes 393224 | tf_op jit(solution)/shard_map/ppermute | solution.py:497
  129.3 13.5 %copy-start.1 = (bf16[240,256]{1,0:T(8,128)(2,1)}, bf16[240,256]{1,0:T(8,128)(2,1)S(1)}, u32[]{:S(2)}) copy-start(bf16[240,256]{1,0:T(8,128)(2,1)S(1)} %collective-permute-done.9.refs_1_) | copy-start | bytes 368644
  129.3 13.5 %collective-permute-start.10 = (bf16[480,256]{1,0:T(8,128)(2,1)S(1)}, bf16[480,256]{1,0:T(8,128)(2,1)S(1)}, u32[]{:S(2)}, u32[]{:S(2)}) collective-permute-start(bf16[480,256]{1,0:T(8,128)(2,1)S(1)} %pad_maximum_fusion.2), channel_id=1, source_target_pairs={{0,1},{1,0},{2,3},{3,2},{4,5},{5,4},{6,7},{7,6},{8,9},{9,8},{10,11... | collective-permute-start | bytes 737288 | tf_op jit(solution)/shard_map/ppermute | solution.py:491
  142.8 12.1 %copy-start.2 = (bf16[480,256]{1,0:T(8,128)(2,1)}, bf16[480,256]{1,0:T(8,128)(2,1)S(1)}, u32[]{:S(2)}) copy-start(bf16[480,256]{1,0:T(8,128)(2,1)S(1)} %collective-permute-done.10.refs_2_) | copy-start | bytes 737284
  142.9 27.5 %collective-permute-start.11 = (bf16[960,256]{1,0:T(8,128)(2,1)S(1)}, bf16[960,256]{1,0:T(8,128)(2,1)S(1)}, u32[]{:S(2)}, u32[]{:S(2)}) collective-permute-start(bf16[960,256]{1,0:T(8,128)(2,1)S(1)} %pad_maximum_fusion), channel_id=1, source_target_pairs={{0,2},{1,3},{2,0},{3,1},{4,6},{5,7},{6,4},{7,5},{8,10},{9,11},{10,... | collective-permute-start | bytes 1474568 | tf_op jit(solution)/shard_map/ppermute | solution.py:491
  (5 other events, 3.6 us)

commit v2 on v1

v2 whole, which is shorter than its diff:
```python
import functools

import jax
import jax.numpy as jnp
from jax import lax
from jax.experimental import pallas as pl
from jax.experimental.pallas import tpu as pltpu
from jax.sharding import PartitionSpec as P

F32 = jnp.float32
BF16 = jnp.bfloat16
LANES = 128
BLOCK = 128
PARTS = 5
PARTS2 = 5
CHUNK = 64
BOTH = ("face", "sub")
MIB = 1024 * 1024
VMEM_LIMIT = 30 * MIB


def params(limit=VMEM_LIMIT):
    return pltpu.CompilerParams(vmem_limit_bytes=limit)


def cost(flops, moved):
    return pl.CostEstimate(flops=int(flops), bytes_accessed=int(moved), transcendentals=0)


def dot(left, right):
    return jnp.dot(left, right, preferred_element_type=F32)


def dot_rows(left, right):
    return lax.dot_general(left, right, (((0,), (0,)), ((), ())), preferred_element_type=F32)


def dot_back(left, right):
    return lax.dot_general(left, right, (((1,), (1,)), ((), ())), preferred_element_type=F32)


def down(row):
    return jnp.broadcast_to(row, (LANES, LANES)).T


def hot_lanes(index, first, count):
    lane = lax.broadcasted_iota(jnp.int32, (1, LANES), 1)
    index = index.astype(jnp.int16)
    one, zero = BF16(1.0), BF16(0.0)
    tiles = [
        jnp.where(index == (lane + (first + t * LANES)).astype(jnp.int16), one, zero)
        for t in range(count // LANES)
    ]
    return jnp.concatenate(tiles, axis=1)


def hot_rows(index, first, count):
    row = lax.broadcasted_iota(jnp.int32, (count, 1), 0) + first
    return jnp.where(row == index, 1.0, 0.0).astype(BF16)


def row_mean(values):
    return jnp.mean(values, axis=-1, keepdims=True)


def col_sum(values):
    return jnp.sum(values, axis=0, keepdims=True)


def gate(halves):
    twice = 1.0 + jnp.tanh(halves)
    act = halves * twice
    return act, twice + act * (2.0 - twice)


def norm(values):
    centre = values - row_mean(values)
    scale = lax.rsqrt(row_mean(centre * centre) + 1e-05)
    return centre * scale, scale


def pick_kernel(lists_ref, nodes_ref, next_ref, prev_ref):
    rows = nodes_ref.shape[0]
    halo = lists_ref.shape[1]
    for side, out_ref in ((0, next_ref), (1, prev_ref)):
        for at in range(0, halo, LANES):
            index = down(lists_ref[side : side + 1, at : at + LANES])
            out_ref[at : at + LANES, :] = dot(
                hot_lanes(index, 0, rows), nodes_ref[...]
            ).astype(BF16)


def pick(lists, nodes):
    halo, width = lists.shape[1], nodes.shape[1]
    out = jax.ShapeDtypeStruct((halo, width), BF16)
    return pl.pallas_call(
        pick_kernel,
        out_shape=(out, out),
        compiler_params=params(),
        cost_estimate=cost(4 * halo * nodes.size, 2 * nodes.size),
        name="pick_rows",
    )(lists, nodes)


def in_vmem(array):
    return pltpu.with_memory_space_constraint(array, pltpu.VMEM)


def own_kernel(index_ref, nodes_ref, out_ref):
    rows = nodes_ref.shape[0]
    k = pl.program_id(0)
    row = index_ref[pl.ds(k, 1), :]
    column = jnp.concatenate(
        [down(row[:, at : at + LANES]) for at in range(0, rows, LANES)], axis=0
    )
    out_ref[0] = dot(hot_lanes(column, 0, rows), nodes_ref[...]).astype(BF16)


def own_senders(index, nodes):
    degree, rows = index.shape
    width = nodes.shape[1]
    return pl.pallas_call(
        own_kernel,
        grid=(degree,),
        in_specs=[pl.BlockSpec(memory_space=pltpu.VMEM)] * 2,
        out_specs=pl.BlockSpec((1, rows, width), lambda i: (i, 0, 0)),
        out_shape=pltpu.HBM((degree, rows, width), BF16),
        compiler_params=params(30 * MIB),
        cost_estimate=cost(2 * degree * rows * rows * width, 2 * degree * rows * width),
        name="own_senders",
    )(index, nodes)


def main_kernel(
    degree,
    part_rows,
    place_ref,
    edges_ref,
    own_ref,
    index_ref,
    valid_ref,
    nodes_ref,
    halo_ref,
    cot_ref,
    vec_ref,
    w_first_ref,
    w_second_ref,
    n_first_ref,
    n_second_ref,
    mixed_ref,
    grad_nodes_ref,
    hat_ref,
    away_ref,
    keep_ref,
    snd_ref,
    act_scr,
    slope_scr,
    scale_scr,
    sum_scr,
    count_scr,
    up_scr,
    acc_scr,
    turned_scr,
    half_first,
    half_second,
    bias_scr,
):
    step = pl.program_id(0)
    rows, width = nodes_ref.shape
    e_b1, e_b2, e_gain, e_shift, n_b1, n_b2, n_gain, n_shift = (
        vec_ref[i : i + 1, :] for i in range(8)
    )
    at_first, at_second = 0, 3 * width
    at_nfirst, at_nsecond, at_vec = 4 * width, 6 * width, 7 * width

    def wide(lanes):
        return jnp.concatenate([lanes] * (width // LANES), axis=1)

    @pl.when(step == 0)
    def begin():
        half_first[...] = (w_first_ref[...].astype(F32) * 0.5).astype(BF16)
        half_second[...] = (w_second_ref[...].astype(F32) * 0.5).astype(BF16)
        sum_scr[...] = jnp.zeros(sum_scr.shape, F32)
        count_scr[...] = jnp.zeros(count_scr.shape, F32)
        bias_scr[...] = jnp.zeros(bias_scr.shape, F32)
        acc_scr[...] = jnp.zeros(acc_scr.shape, F32)
        turned_scr[...] = jnp.zeros(turned_scr.shape, F32)
        up_scr[...] = dot(nodes_ref[...], half_first[:width, :]) + 0.5 * e_b1

    @pl.when(step < degree)
    def forward():
        k = step
        joint = index_ref[pl.ds(k, 1), :] * 2 + valid_ref[pl.ds(k, 1), :]
        part = rows // PARTS
        columns, entered = {}, {}

        def choose(p):
            column = jnp.concatenate(
                [down(joint[:, at : at + LANES]) for at in range(p * part, (p + 1) * part, LANES)],
                axis=0,
            )
            columns[p] = column
            return dot(hot_lanes(column >> 1, rows, halo_ref.shape[0]), halo_ref[...])

        def enter(p, picked):
            here = slice(p * part, (p + 1) * part)
            snd = picked.astype(BF16) + own_ref[0, here, :]
            snd_ref[k, here, :] = snd
            joined = jnp.concatenate([snd, edges_ref[0, here, :]], axis=1)
            return dot(joined, half_first[width:, :])

        def middle(p, pre):
            acts = []
            for at in range(0, part, CHUNK):
                here = slice(p * part + at, p * part + at + CHUNK)
                act, slope = gate(pre[at : at + CHUNK] + up_scr[here, :])
                act = act.astype(BF16)
                acts.append(act)
                act_scr[k, here, :] = act
                slope_scr[k, here, :] = slope.astype(BF16)
            return dot(jnp.concatenate(acts, axis=0), w_second_ref[...])

        def leave(p, second):
            for at in range(0, part, CHUNK):
                here = slice(p * part + at, p * part + at + CHUNK)
                live = (columns[p][at : at + CHUNK] & 1).astype(F32)
                value = second[at : at + CHUNK] + e_b2
                centre = value - row_mean(value)
                scale = lax.rsqrt(row_mean(centre * centre) + 1e-05) * live
                hat = centre * wide(scale)
                hat_ref[k, here, :] = hat.astype(BF16)
                scale_scr[k, here, :] = scale.astype(scale_scr.dtype)
                sum_scr[here, :] += hat
                count_scr[here, :] += live

        chosen, seconds = {}, {}
        for i in range(PARTS):
            chosen[i] = choose(i)
        for i in range(PARTS):
            entered[i] = enter(i, chosen.pop(i))
        for i in range(PARTS):
            seconds[i] = middle(i, entered.pop(i))
        for i in range(PARTS):
            leave(i, seconds.pop(i))

    @pl.when(step == degree)
    def node_stage():
        part = rows // PARTS
        parts = [slice(p * part, (p + 1) * part) for p in range(PARTS)]
        gathered, firsts, acts, slopes, seconds = [], [], [], [], []
        hats, grads_d, grads_c, backs = [], [], [], []
        for here in parts:
            counts = wide(count_scr[here, :])
            gathered.append((sum_scr[here, :] * e_gain + counts * e_shift).astype(BF16))
            joined = jnp.concatenate([nodes_ref[here, :], gathered[-1]], axis=1)
            firsts.append(dot(joined, n_first_ref[...]))
        for first in firsts:
            act, slope = gate(0.5 * (first + n_b1))
            acts.append(act.astype(BF16))
            slopes.append(0.5 * slope)
            seconds.append(dot(acts[-1], n_second_ref[...]))
        ups, hat_sums, up_sums, d_sums, c_sums = [], [], [], [], []
        for here, second in zip(parts, seconds):
            hat, scale = norm(second + n_b2)
            out = nodes_ref[here, :].astype(F32) + (hat * n_gain + n_shift)
            mixed_ref[here, :] = out.astype(BF16)
            up = cot_ref[here, :].astype(F32)
            hat_sums.append(col_sum(up * hat))
            up_sums.append(col_sum(up))
            scaled = up * n_gain
            grad = scale * (scaled - row_mean(scaled) - hat * row_mean(scaled * hat))
            d_sums.append(col_sum(grad))
            grads_d.append(grad.astype(BF16))
            backs.append(dot_back(grads_d[-1], n_second_ref[...]))
        for p in range(PARTS):
            grad = backs[p] * slopes[p]
            c_sums.append(col_sum(grad))
            grads_c.append(grad.astype(BF16))
        all_d, all_c = jnp.concatenate(grads_d, axis=0), jnp.concatenate(grads_c, axis=0)
        acc_scr[at_nsecond : at_nsecond + width, :] = dot_rows(
            jnp.concatenate(acts, axis=0), all_d
        )
        for p, here in enumerate(parts):
            gain_part = dot_back(grads_c[p], n_first_ref[width:, :])
            own_part = dot_back(grads_c[p], n_first_ref[:width, :])
            grad_nodes_ref[here, :] = cot_ref[here, :].astype(F32) + own_part
            sums, counts = sum_scr[here, :], wide(count_scr[here, :])
            acc_scr[at_vec + 2 : at_vec + 3, :] += col_sum(gain_part * sums)
            acc_scr[at_vec + 3 : at_vec + 4, :] += col_sum(gain_part * counts)
            scaled = gain_part * e_gain
            up_scr[here, :] = scaled - row_mean(scaled)
            sum_scr[here, :] = jnp.zeros((part, width), F32)
        acc_scr[at_nfirst : at_nfirst + width, :] = dot_rows(nodes_ref[...], all_c)
        acc_scr[at_nfirst + width : at_nfirst + 2 * width, :] = dot_rows(
            jnp.concatenate(gathered, axis=0), all_c
        )
        for row, values in ((4, c_sums), (5, d_sums), (6, hat_sums), (7, up_sums)):
            acc_scr[at_vec + row : at_vec + row + 1, :] = sum(values)

    def outer(k):
        all_a = hat_ref[k]
        turned_scr[:, :width] += dot_rows(all_a, snd_ref[k])
        turned_scr[:, width:] += dot_rows(all_a, edges_ref[0])

    def backward(k):
        part = rows // PARTS2
        grads, backs = [], []
        for p in range(PARTS2):
            out = []
            for at in range(p * part, (p + 1) * part, CHUNK):
                here = slice(at, at + CHUNK)
                hat = hat_ref[k, here, :].astype(F32)
                scale = wide(scale_scr[k, here, :].astype(F32))
                up = up_scr[here, :]
                grad = scale * (up - hat * row_mean(up * hat))
                bias_scr[...] += jnp.sum(grad.reshape(CHUNK // 8, 8, width), axis=0)
                out.append(grad.astype(BF16))
            grads.append(jnp.concatenate(out, axis=0))
            backs.append(dot_back(grads[-1], half_second[...]))
        acc_scr[at_second : at_second + width, :] += dot_rows(
            act_scr[k], jnp.concatenate(grads, axis=0)
        )
        for p in range(PARTS2):
            for at in range(0, part, CHUNK):
                here = slice(p * part + at, p * part + at + CHUNK)
                grad = backs[p][at : at + CHUNK] * slope_scr[k, here, :].astype(F32)
                sum_scr[here, :] += grad
                hat_ref[k, here, :] = grad.astype(BF16)

    @pl.when(step == degree)
    def first_back():
        backward(0)

    @pl.when((step > degree) & (step < 2 * degree))
    def go_back():
        outer(step - degree - 1)
        backward(step - degree)

    @pl.when(step == 2 * degree)
    def hand_over():
        outer(degree - 1)
        acc_scr[at_vec + 1 : at_vec + 2, :] = col_sum(bias_scr[...])
        acc_scr[at_vec : at_vec + 1, :] = col_sum(sum_scr[...])
        received = sum_scr[...].astype(BF16)
        acc_scr[at_first : at_first + width, :] = dot_rows(nodes_ref[...], received)
        grad_nodes_ref[...] += dot_back(received, w_first_ref[:width, :])
        acc_scr[at_first + width : at_first + 3 * width, :] = turned_scr[...].T
        place = place_ref[0]
        half = keep_ref.shape[0] // part_rows
        for p in range(2 * half):
            start = pl.multiple_of((place ^ p) * part_rows, 16)
            piece = acc_scr[pl.ds(start, part_rows), :]
            if p < half:
                keep_ref[p * part_rows : (p + 1) * part_rows, :] = piece
            else:
                out = (p - half) * part_rows
                away_ref[out : out + part_rows, :] = piece.astype(BF16)


def main(place, index, valid, edges, own, nodes, halo, cot, vec, w1, w2, n1, n2, parts):
    degree, rows, width = edges.shape
    grad_rows = w1.shape[0] + w2.shape[0] + n1.shape[0] + n2.shape[0] + 8
    part_rows = -(-grad_rows // (16 * parts)) * 16
    total = part_rows * parts
    resident = pl.BlockSpec(memory_space=pltpu.VMEM)
    edge_spec = pl.BlockSpec((1, rows, width), lambda i, *_: (jnp.where(i > degree, i - degree - 1, jnp.minimum(i, degree - 1)), 0, 0))
    held = (index, valid, nodes, halo, cot, vec, w1, w2, n1, n2)
    own_spec = pl.BlockSpec(
        (1, rows, width), lambda i, *_: (jnp.minimum(i, degree - 1), 0, 0)
    )
    grid_spec = pltpu.PrefetchScalarGridSpec(
        num_scalar_prefetch=1,
        grid=(2 * degree + 1,),
        in_specs=[edge_spec, own_spec] + [resident] * len(held),
        out_specs=[resident] * 5,
        scratch_shapes=[
            pltpu.VMEM((degree, rows, width), BF16),
            pltpu.VMEM((degree, rows, width), BF16),
            pltpu.VMEM((degree, rows, width), BF16),
            pltpu.VMEM((degree, rows, LANES), BF16),
            pltpu.VMEM((rows, width), F32),
            pltpu.VMEM((rows, LANES), F32),
            pltpu.VMEM((rows, width), F32),
            pltpu.VMEM((total, width), F32),
            pltpu.VMEM((width, 2 * width), F32),
            pltpu.VMEM(w1.shape, BF16),
            pltpu.VMEM(w2.shape, BF16),
            pltpu.VMEM((8, width), F32),
        ],
    )
    return pl.pallas_call(
        functools.partial(main_kernel, degree, part_rows),
        grid_spec=grid_spec,
        out_shape=(
            pltpu.VMEM((rows, width), BF16),
            pltpu.VMEM((rows, width), F32),
            pltpu.VMEM((degree, rows, width), BF16),
            pltpu.VMEM((total // 2, width), BF16),
            pltpu.VMEM((total // 2, width), F32),
        ),
        compiler_params=params(46 * MIB),
        cost_estimate=cost(18 * degree * rows * width * width, 8 * edges.size),
        name="edges_and_nodes",
    )(place, edges, pltpu.with_memory_space_constraint(own, pltpu.HBM), *held)


def split_back(total, weight):
    high = total.astype(BF16)
    low = (total - high.astype(F32)).astype(BF16)
    return dot_back(high, weight) + dot_back(low, weight)


def spread_kernel(first, index_ref, grad_ref, weight_ref, *rest):
    *extra, out_ref, total = rest
    degree = grad_ref.shape[0]
    rows = total.shape[0]
    k = pl.program_id(0) * 2
    hots = [hot_rows(index_ref[pl.ds(k + j, 1), :], first, rows) for j in range(2)]
    count, width = grad_ref.shape[1:]
    part = dot(
        jnp.concatenate(hots, axis=1),
        grad_ref[pl.ds(k, 2)].reshape(2 * count, width),
    )

    @pl.when(k == 0)
    def start():
        total[...] = part

    @pl.when(k > 0)
    def go_on():
        total[...] += part

    @pl.when(k == degree - 2)
    def finish():
        result = split_back(total[...], weight_ref[...])
        if extra:
            result = result + extra[0][first : first + rows, :]
        out_ref[...] = result.astype(out_ref.dtype)


def spread(index, grad, weight, first, rows, dtype, extra=None):
    degree, count, width = grad.shape
    resident = pl.BlockSpec(memory_space=pltpu.VMEM)
    held = [index, grad, weight] + ([] if extra is None else [extra])
    return pl.pallas_call(
        functools.partial(spread_kernel, first),
        grid=(degree // 2,),
        in_specs=[resident] * len(held),
        out_specs=resident,
        out_shape=pltpu.VMEM((rows, width), dtype),
        scratch_shapes=[pltpu.VMEM((rows, width), F32)],
        compiler_params=params(),
        cost_estimate=cost(2 * rows * grad.size, 2 * grad.size),
        name="spread_rows",
    )(*held)


def edge_kernel(grad_ref, weight_ref, out_ref):
    slots, rows, width = out_ref.shape
    k = pl.program_id(0) * slots
    grad = grad_ref[pl.ds(k, slots)].reshape(slots * rows, width)
    out_ref[...] = dot_back(grad, weight_ref[...]).astype(BF16).reshape(slots, rows, width)


def edge_grads(grad, weight):
    degree, count, width = grad.shape
    resident = pl.BlockSpec(memory_space=pltpu.VMEM)
    return pl.pallas_call(
        edge_kernel,
        grid=(degree // 2,),
        in_specs=[resident, resident],
        out_specs=pl.BlockSpec((2, count, width), lambda i: (i, 0, 0)),
        out_shape=jax.ShapeDtypeStruct(grad.shape, BF16),
        compiler_params=params(),
        cost_estimate=cost(2 * grad.size * width, 4 * grad.size),
        name="edge_grads",
    )(grad, weight)


def final_kernel(lists_ref, low_ref, high_ref, next_ref, prev_ref, out_ref):
    rows = out_ref.shape[0]
    low = low_ref.shape[0]
    for first, part_ref in ((0, low_ref), (low, high_ref)):
        count = part_ref.shape[0]
        out_ref[first : first + count, :] = (
            part_ref[...]
            + dot(hot_rows(lists_ref[0:1, :], first, count), next_ref[...])
            + dot(hot_rows(lists_ref[1:2, :], first, count), prev_ref[...])
        )


def final(lists, low, high, ret_next, ret_prev):
    rows = low.shape[0] + high.shape[0]
    width = low.shape[1]
    return pl.pallas_call(
        final_kernel,
        out_shape=jax.ShapeDtypeStruct((rows, width), F32),
        compiler_params=params(),
        cost_estimate=cost(4 * rows * ret_next.size, 8 * rows * width),
        name="returned_rows",
    )(lists, low, high, ret_next, ret_prev)


def split_kernel(keep_ref, came_ref, own_ref, *away_refs):
    part = own_ref.shape[0]
    for p, out_ref in enumerate((own_ref,) + away_refs):
        here = slice(p * part, (p + 1) * part)
        total = keep_ref[here, :] + came_ref[here, :].astype(F32)
        out_ref[...] = total.astype(out_ref.dtype)


def add_and_split(keep, came):
    part, width = keep.shape[0] // 4, keep.shape[1]
    return pl.pallas_call(
        split_kernel,
        out_shape=(pltpu.VMEM((part, width), F32),) + (pltpu.VMEM((part, width), BF16),) * 3,
        compiler_params=params(),
        cost_estimate=cost(keep.size, 8 * keep.size),
        name="add_and_split",
    )(keep, came)


def sum_kernel(own_ref, *refs):
    *came, out_ref = refs
    values = [own_ref[...].astype(F32)] + [r[...].astype(F32) for r in came]
    while len(values) > 1:
        values = [a + b for a, b in zip(values[::2], values[1::2])]
    out_ref[...] = values[0].astype(BF16)


def sum_parts(own, came):
    return pl.pallas_call(
        sum_kernel,
        out_shape=pltpu.VMEM(own.shape, BF16),
        compiler_params=params(),
        cost_estimate=cost(own.size * len(came), 8 * own.size),
        name="sum_parts",
    )(own, *came)


def unpack_kernel(part_rows, place_ref, *refs):
    pieces, outs, full = refs[:5], refs[5:-1], refs[-1]
    place = place_ref[0]
    p = 0
    for piece in pieces:
        for at in range(0, piece.shape[0], part_rows):
            start = pl.multiple_of((place ^ p) * part_rows, 16)
            full[pl.ds(start, part_rows), :] = piece[at : at + part_rows, :].astype(F32)
            p += 1
    at = 0
    for out_ref in outs:
        count = out_ref.shape[0]
        out_ref[...] = full[at : at + count, :]
        at += count


def unpack(place, pieces, row_counts):
    part_rows, width = pieces[0].shape
    total = 8 * part_rows
    return pl.pallas_call(
        functools.partial(unpack_kernel, part_rows),
        in_specs=[pl.BlockSpec(memory_space=pltpu.SMEM)]
        + [pl.BlockSpec(memory_space=pltpu.VMEM)] * 5,
        out_shape=tuple(jax.ShapeDtypeStruct((n, width), F32) for n in row_counts),
        scratch_shapes=[pltpu.VMEM((total, width), F32)],
        compiler_params=params(),
        name="unpack_sums",
    )(place, *pieces)


def traded(value, mask):
    count = lax.axis_size("face") * lax.axis_size("sub")
    return lax.ppermute(value, BOTH, [(i, i ^ mask) for i in range(count)])


def tied(*values):
    return lax.optimization_barrier(values)


def passed_along(value, steps):
    count = lax.axis_size("face")
    pairs = [(source, (source + steps) % count) for source in range(count)]
    return lax.ppermute(value, "face", pairs)


def body(
    nodes,
    edges,
    neighbours,
    valid,
    send_lists,
    edge_first,
    edge_first_bias,
    edge_second,
    edge_second_bias,
    edge_gain,
    edge_shift,
    node_first,
    node_first_bias,
    node_second,
    node_second_bias,
    node_gain,
    node_shift,
    cotangent,
):
    rows, width = nodes.shape
    lists = send_lists[0]
    halo_rows = lists.shape[1]
    index = neighbours.T
    flags = valid.T
    edge_rows = jnp.transpose(edges, (1, 0, 2))
    vec = jnp.stack(
        [
            edge_first_bias,
            edge_second_bias,
            edge_gain,
            edge_shift,
            node_first_bias,
            node_second_bias,
            node_gain,
            node_shift,
        ]
    ).astype(F32)
    subs = lax.axis_size("sub")
    me = lax.axis_index("face") * subs + lax.axis_index("sub")
    devices = lax.axis_size("face") * subs
    masks = [1 << b for b in range(devices.bit_length() - 1)]
    masks = [subs] + [m for m in masks if m != subs]
    halving, doubling = masks[:3], masks[3:]
    place = jnp.int32(0)
    for mask in halving:
        place = place * 2 + jnp.where((me & mask) != 0, 1, 0)
    place = place.astype(jnp.int32).reshape(1)

    nodes_held, index_held = in_vmem(nodes), in_vmem(index)
    to_next, to_prev = pick(in_vmem(lists), nodes_held)
    from_prev = passed_along(to_next, 1)
    from_next = passed_along(to_prev, -1)
    own = own_senders(index_held, nodes_held)
    halo = jnp.concatenate([from_prev, from_next], axis=0)
    weights = [in_vmem(a) for a in (edge_first, edge_second, node_first, node_second)]
    mixed, grad_nodes, grad_a, away, keep = main(
        place,
        index_held,
        in_vmem(flags),
        edge_rows,
        own,
        nodes_held,
        in_vmem(halo),
        in_vmem(cotangent),
        in_vmem(vec),
        *weights,
        1 << len(halving),
    )
    send_weight = edge_first[width : 2 * width]
    edge_weight = edge_first[2 * width :]
    half = rows // 2
    core, outer, inner = halving
    plane = (inner, outer, inner ^ outer)

    came = traded(away, core)
    part, *away = add_and_split(keep, came)
    came = [traded(a, mask) for a, mask in zip(away, plane)]
    grad_a, part = tied(grad_a, part)
    back = spread(index_held, grad_a, send_weight, rows, 2 * halo_rows, BF16)
    came, back = tied(came, back)
    part = sum_parts(part, came)
    ret_next = passed_along(back[:halo_rows], -1)
    ret_prev = passed_along(back[halo_rows:], 1)
    while doubling:
        first, *doubling = doubling
        group = [first]
        if doubling:
            second, *doubling = doubling
            group = [first, second, first ^ second]
        came = [traded(part, mask) for mask in group]
        if not doubling:
            grad_a, part = tied(grad_a, part)
            low = spread(index_held, grad_a, send_weight, 0, half, F32, grad_nodes)
            came, low = tied(came, low)
        part = sum_parts(part, came)
    came = [traded(part, mask) for mask in plane]
    grad_a, part = tied(grad_a, part)
    high = spread(index_held, grad_a, send_weight, half, half, F32, grad_nodes)
    came, high = tied(came, high)
    pieces = [part] + came
    pieces.append(traded(jnp.concatenate(pieces, axis=0), core))
    grad_edges = edge_grads(grad_a, edge_weight)
    grad_nodes = final(lists, low, high, ret_next, ret_prev)
    counts = (edge_first.shape[0], width, node_first.shape[0], width) + (1,) * 8
    sums = unpack(place, pieces, counts)
    vectors = [v.reshape(width) for v in sums[4:]]
    return (
        mixed,
        grad_nodes,
        jnp.transpose(grad_edges, (1, 0, 2)),
        sums[0],
        vectors[0],
        sums[1],
        vectors[1],
        vectors[2],
        vectors[3],
        sums[2],
        vectors[4],
        sums[3],
        vectors[5],
        vectors[6],
        vectors[7],
    )


def solution(mesh):
    shared = P(("face", "sub"), None)
    split3 = P(("face", "sub"), None, None)
    return jax.shard_map(
        body,
        mesh=mesh,
        in_specs=(shared, split3, shared, shared, split3) + (P(),) * 12 + (shared,),
        out_specs=(shared, shared, split3) + (P(),) * 12,
        check_vma=False,
    )
```

time: 176 us -> 113 us (0.64)
  Pallas kernels: 132 us -> 80.1 us
  waiting for transfers between devices: 19.5 us -> 5.65 us
  starting transfers between devices: 13.2 us -> 20.8 us
  other arithmetic: 2.41 us -> 0.06 us
    pallas_call x8 -> x9, Pallas kernels: 124 us -> 76.6 us  [the longest x1 37.8 us: main(): pl.pallas_call(functools.partial(main_kernel, degree, part_rows), grid_sp...]
    ppermute x8 -> x11, waiting for transfers between devices: 19.5 us -> 3.87 us  [traded(): return lax.ppermute(value, BOTH, [(i, i ^ mask) for i in range(count)])]
    ppermute x8 -> x11, starting transfers between devices: 7.19 us -> 11.7 us  [traded(): return lax.ppermute(value, BOTH, [(i, i ^ mask) for i in range(count)])]
    ppermute x4, starting transfers between devices: 6.01 us -> 9.11 us  [passed_along(): return lax.ppermute(value, 'face', pairs)]
    pallas_call x1, Pallas kernels: 2.35 us -> 0.55 us  [pick(): pl.pallas_call(pick_kernel, out_shape=(out, out), compiler_params=params(...]
    ppermute x4, waiting for transfers between devices: 0.01 us -> 1.78 us  [passed_along(): return lax.ppermute(value, 'face', pairs)]
    unnamed x34 -> x43, local copies, waits for them, and re-layouts: 3.61 us -> 4.67 us
  transfers between devices with their start and end apart: 12 -> 15, of which waited for: 5 -> 3; matrix products, arithmetic and copies ran while one was open for 1% -> 1% of each run, Pallas kernels for 37% -> 36%
where the time goes in v2:
time: 113 us
  Pallas kernels  80.1 us (71%)
  starting transfers between devices  20.8 us (18%)
  waiting for transfers between devices  5.65 us (5%)
  local copies, waits for them, and re-layouts  4.77 us (4%)
  between operations  1.27 us (1%)
    pallas_call x1, Pallas kernels, main(): pl.pallas_call(functools.partial(main_kernel, degree, part_rows), grid_sp...  37.8 us
    pallas_call x3, Pallas kernels, spread(): pl.pallas_call(functools.partial(spread_kernel, first), grid=(degree // 2...  19.5 us
    pallas_call x1, Pallas kernels, own_senders(): pl.pallas_call(own_kernel, grid=(degree,), in_specs=[pl.BlockSpec(memory_...  13.8 us
    ppermute x11, starting transfers between devices, traded(): return lax.ppermute(value, BOTH, [(i, i ^ mask) for i in range(count)])  11.7 us
    ppermute x4, starting transfers between devices, passed_along(): return lax.ppermute(value, 'face', pairs)  9.11 us
    pallas_call x1, Pallas kernels, edge_grads(): pl.pallas_call(edge_kernel, grid=(degree // 2,), in_specs=[resident, resi...  5.31 us
    unnamed x43, local copies, waits for them, and re-layouts  4.67 us
    ppermute x11, waiting for transfers between devices, traded(): return lax.ppermute(value, BOTH, [(i, i ^ mask) for i in range(count)])  3.87 us
  transfers between devices with their start and end apart: 15, of which 3 were waited for; matrix products, arithmetic and copies ran while one was open for 1% of the time, Pallas kernels for 36%

profile of v2, /device:TPU:0, one launch (start us, length us, event | category | flops | bytes accessed | tf_op | source)
XLA Modules:
  0.0 112.6 jit_solution(8694394703270085369)
XLA Ops:
  0.7 0.7 copy-done.1
  1.3 1.1 copy-done.3
  2.4 0.5 pick_rows.1
  3.0 5.5 %collective-permute-start.1 = (bf16[256,256]{1,0:T(8,128)(2,1)S(1)}, bf16[256,256]{1,0:T(8,128)(2,1)S(1)}, u32[]{:S(2)}, u32[]{:S(2)}) collective-permute-start(bf16[256,256]{1,0:T(8,128)(2,1)S(1)} %get-tuple-element.57), channel_id=1, source_target_pairs={{0,30},{2,0},{4,2},{6,4},{8,6},{10,8},{12,10},{14,12},{16,14},{18,... | collective-permute-start | bytes 393224 | tf_op jit(solution)/shard_map/ppermute | solution.py:583
  8.5 1.1 copy-done.4
  9.6 0.9 copy-done.11
  10.6 13.8 %own_senders.1.own_ref = bf16[12,1280,256]{2,1,0:T(8,128)(2,1)} custom-call(s32[12,1280]{1,0:T(8,128)S(1)} %bitcast.17, bf16[1280,256]{1,0:T(8,128)(2,1)S(1)} %copy-done.4), custom_call_target="tpu_custom_call" | custom-call | flops 10066329600 | bytes 7864320 | tf_op jit(solution)/shard_map/own_senders/pallas_call | solution.py:122
  24.7 37.8 %edges_and_nodes.1 = (bf16[1280,256]{1,0:T(8,128)(2,1)S(1)}, f32[1280,256]{1,0:T(8,128)S(1)}, bf16[12,1280,256]{2,1,0:T(8,128)(2,1)S(1)}, bf16[960,256]{1,0:T(8,128)(2,1)S(1)}, f32[960,256]{1,0:T(8,128)S(1)}) custom-call(s32[1]{0:T(128)} %bitcast.place_ref, bf16[12,1280,256]{2,1,0:T(8,128)(2,1)} %bitcast.23, bf16[12,1280,256]{2,1,0:T(8,128)(2,1)} %own_senders.1.own_ref, ...), custom_call_target="tpu_custom_call" | custom-call | flops 18119393280 | bytes 31457280 | tf_op jit(solution)/shard_map/edges_and_nodes/pallas_call | solution.py:391
  62.6 1.8 %collective-permute-done.2.came_ref = bf16[960,256]{1,0:T(8,128)(2,1)S(1)} collective-permute-done((bf16[960,256]{1,0:T(8,128)(2,1)S(1)}, bf16[960,256]{1,0:T(8,128)(2,1)S(1)}, u32[]{:S(2)}, u32[]{:S(2)}) %collective-permute-start.2) | collective-permute-done | bytes 491552 | tf_op jit(solution)/shard_map/ppermute | solution.py:573
  64.6 1.6 %collective-permute-start.4 = (bf16[240,256]{1,0:T(8,128)(2,1)S(1)}, bf16[240,256]{1,0:T(8,128)(2,1)S(1)}, u32[]{:S(2)}, u32[]{:S(2)}) collective-permute-start(bf16[240,256]{1,0:T(8,128)(2,1)S(1)} %get-tuple-element.65), channel_id=1, source_target_pairs={{0,1},{1,0},{2,3},{3,2},{4,5},{5,4},{6,7},{7,6},{8,9},{9,8},{10,11... | collective-permute-start | bytes 368648 | tf_op jit(solution)/shard_map/ppermute | solution.py:573
  66.2 1.9 %collective-permute-start.5 = (bf16[240,256]{1,0:T(8,128)(2,1)S(1)}, bf16[240,256]{1,0:T(8,128)(2,1)S(1)}, u32[]{:S(2)}, u32[]{:S(2)}) collective-permute-start(bf16[240,256]{1,0:T(8,128)(2,1)S(1)} %get-tuple-element.66), channel_id=1, source_target_pairs={{0,5},{1,4},{2,7},{3,6},{4,1},{5,0},{6,3},{7,2},{8,13},{9,12},{10,... | collective-permute-start | bytes 368648 | tf_op jit(solution)/shard_map/ppermute | solution.py:573
  68.1 5.8 %spread_rows.3 = bf16[512,256]{1,0:T(8,128)(2,1)S(1)} custom-call(s32[12,1280]{1,0:T(8,128)S(1)} %bitcast.19, bf16[12,1280,256]{2,1,0:T(8,128)(2,1)S(1)} %get-tuple-element.78.grad_ref, bf16[256,256]{1,0:T(8,128)(2,1)S(1)} %get-tuple-element.98.weight_ref), custom_call_target="tpu_custom_call" | custom-call | flops 4026531840 | bytes 7864320 | tf_op jit(solution)/shard_map/spread_rows/pallas_call | solution.py:445
  74.0 4.1 %collective-permute-start.7 = (bf16[240,256]{1,0:T(8,128)(2,1)S(1)}, bf16[240,256]{1,0:T(8,128)(2,1)S(1)}, u32[]{:S(2)}, u32[]{:S(2)}) collective-permute-start(bf16[240,256]{1,0:T(8,128)(2,1)S(1)} %sum_parts.2.own_ref), channel_id=1, source_target_pairs={{0,16},{1,17},{2,18},{3,19},{4,20},{5,21},{6,22},{7,23},{8,24},{9,... | collective-permute-start | bytes 368648 | tf_op jit(solution)/shard_map/ppermute | solution.py:573
  78.4 6.9 %spread_rows.4.low_ref = f32[640,256]{1,0:T(8,128)S(1)} custom-call(s32[12,1280]{1,0:T(8,128)S(1)} %bitcast.20, bf16[12,1280,256]{2,1,0:T(8,128)(2,1)S(1)} %get-tuple-element.78.grad_ref, bf16[256,256]{1,0:T(8,128)(2,1)S(1)} %get-tuple-element.98.weight_ref, f32[1280,256]{1,0:T(8,128)S(1)} %get-tuple-element.72.rest_0_), custom_call_target="tpu_custom_call" | custom-call | flops 5033164800 | bytes 7864320 | tf_op jit(solution)/shard_map/spread_rows/pallas_call | solution.py:445
  85.3 2.0 %collective-permute-done.7.refs_1_ = bf16[240,256]{1,0:T(8,128)(2,1)S(1)} collective-permute-done((bf16[240,256]{1,0:T(8,128)(2,1)S(1)}, bf16[240,256]{1,0:T(8,128)(2,1)S(1)}, u32[]{:S(2)}, u32[]{:S(2)}) %collective-permute-start.7) | collective-permute-done | bytes 122912 | tf_op jit(solution)/shard_map/ppermute | solution.py:573
  87.4 1.7 %collective-permute-start.9 = (bf16[240,256]{1,0:T(8,128)(2,1)S(1)}, bf16[240,256]{1,0:T(8,128)(2,1)S(1)}, u32[]{:S(2)}, u32[]{:S(2)}) collective-permute-start(bf16[240,256]{1,0:T(8,128)(2,1)S(1)} %sum_parts.3.refs_0_), channel_id=1, source_target_pairs={{0,4},{1,5},{2,6},{3,7},{4,0},{5,1},{6,2},{7,3},{8,12},{9,13},{10,... | collective-permute-start | bytes 368648 | tf_op jit(solution)/shard_map/ppermute | solution.py:573
  89.1 1.5 %collective-permute-start.10 = (bf16[240,256]{1,0:T(8,128)(2,1)S(1)}, bf16[240,256]{1,0:T(8,128)(2,1)S(1)}, u32[]{:S(2)}, u32[]{:S(2)}) collective-permute-start(bf16[240,256]{1,0:T(8,128)(2,1)S(1)} %sum_parts.3.refs_0_), channel_id=1, source_target_pairs={{0,1},{1,0},{2,3},{3,2},{4,5},{5,4},{6,7},{7,6},{8,9},{9,8},{10,11... | collective-permute-start | bytes 368648 | tf_op jit(solution)/shard_map/ppermute | solution.py:573
  90.9 6.9 %spread_rows.5.high_ref = f32[640,256]{1,0:T(8,128)S(1)} custom-call(s32[12,1280]{1,0:T(8,128)S(1)} %bitcast.21, bf16[12,1280,256]{2,1,0:T(8,128)(2,1)S(1)} %get-tuple-element.78.grad_ref, bf16[256,256]{1,0:T(8,128)(2,1)S(1)} %get-tuple-element.98.weight_ref, f32[1280,256]{1,0:T(8,128)S(1)} %get-tuple-element.72.rest_0_), custom_call_target="tpu_custom_call" | custom-call | flops 5033164800 | bytes 7864320 | tf_op jit(solution)/shard_map/spread_rows/pallas_call | solution.py:445
  98.0 0.8 copy.33
  98.8 3.6 %collective-permute-start.12 = (bf16[256,256]{1,0:T(8,128)(2,1)S(1)}, bf16[256,256]{1,0:T(8,128)(2,1)S(1)}, u32[]{:S(2)}, u32[]{:S(2)}) collective-permute-start(bf16[256,256]{1,0:T(8,128)(2,1)S(1)} %get-tuple-element.100), channel_id=1, source_target_pairs={{0,30},{2,0},{4,2},{6,4},{8,6},{10,8},{12,10},{14,12},{16,14},{18,... | collective-permute-start | bytes 393224 | tf_op jit(solution)/shard_map/ppermute | solution.py:583
  102.4 5.3 %edge_grads.1 = bf16[12,1280,256]{2,1,0:T(8,128)(2,1)} custom-call(bf16[12,1280,256]{2,1,0:T(8,128)(2,1)S(1)} %get-tuple-element.78.grad_ref, bf16[256,256]{1,0:T(8,128)(2,1)S(1)} %get-tuple-element.97.weight_ref), custom_call_target="tpu_custom_call" | custom-call | flops 2013265920 | bytes 15728640 | tf_op jit(solution)/shard_map/edge_grads/pallas_call | solution.py:468
  107.7 1.8 %collective-permute-done.13.prev_ref = bf16[256,256]{1,0:T(8,128)(2,1)S(1)} collective-permute-done((bf16[256,256]{1,0:T(8,128)(2,1)S(1)}, bf16[256,256]{1,0:T(8,128)(2,1)S(1)}, u32[]{:S(2)}, u32[]{:S(2)}) %collective-permute-start.13) | collective-permute-done | bytes 131104 | tf_op jit(solution)/shard_map/ppermute | solution.py:583
  109.5 1.6 %returned_rows.1 = f32[1280,256]{1,0:T(8,128)} custom-call(s32[2,256]{1,0:T(2,128)S(1)} %bitcast.15, f32[640,256]{1,0:T(8,128)S(1)} %spread_rows.4.low_ref, f32[640,256]{1,0:T(8,128)S(1)} %spread_rows.5.high_ref, bf16[256,256]{1,0:T(8,128)(2,1)S(1)} %collective-permute-done.12.next_ref, bf16[256,256]{1,0:T(8,128)(2,1)S(1)} %collective-permute-done.13.prev_ref), custom_call_target="tpu_custom_call" | custom-call | flops 335544320 | bytes 2621440 | tf_op jit(solution)/shard_map/returned_rows/pallas_call | solution.py:495
  111.1 1.4 %unpack_sums.1 = (f32[768,256]{1,0:T(8,128)}, f32[256,256]{1,0:T(8,128)}, f32[512,256]{1,0:T(8,128)}, f32[256,256]{1,0:T(8,128)}, f32[1,256]{1,0:T(1,128)}, /*in...) custom-call(s32[1]{0:T(128)} %bitcast.place_ref, ...), custom_call_target="tpu_custom_call" | custom-call | tf_op jit(solution)/shard_map/unpack_sums/pallas_call | solution.py:560
  (75 shorter events, 1.5 us)
Async XLA Ops:
  3.0 21.6 %collective-permute-start.1 = (bf16[256,256]{1,0:T(8,128)(2,1)S(1)}, bf16[256,256]{1,0:T(8,128)(2,1)S(1)}, u32[]{:S(2)}, u32[]{:S(2)}) collective-permute-start(bf16[256,256]{1,0:T(8,128)(2,1)S(1)} %get-tuple-element.57), channel_id=1, source_target_pairs={{0,30},{2,0},{4,2},{6,4},{8,6},{10,8},{12,10},{14,12},{16,14},{18,... | collective-permute-start | bytes 393224 | tf_op jit(solution)/shard_map/ppermute | solution.py:583
  8.5 16.1 %collective-permute-start = (bf16[256,256]{1,0:T(8,128)(2,1)S(1)}, bf16[256,256]{1,0:T(8,128)(2,1)S(1)}, u32[]{:S(2)}, u32[]{:S(2)}) collective-permute-start(bf16[256,256]{1,0:T(8,128)(2,1)S(1)} %get-tuple-element.56), channel_id=1, source_target_pairs={{0,2},{2,4},{4,6},{6,8},{8,10},{10,12},{12,14},{14,16},{16,18},{18... | collective-permute-start | bytes 393224 | tf_op jit(solution)/shard_map/ppermute | solution.py:583
  10.5 14.0 %copy-start.20 = (bf16[256]{0:T(256)(128)(2,1)S(1)}, bf16[256]{0:T(256)(128)(2,1)}, u32[]{:S(2)}) copy-start(bf16[256]{0:T(256)(128)(2,1)} %param.34) | copy-start | bytes 1540
  10.5 14.1 %copy-start = (bf16[768,256]{1,0:T(8,128)(2,1)S(1)}, bf16[768,256]{1,0:T(8,128)(2,1)}, u32[]{:S(2)}) copy-start(bf16[768,256]{1,0:T(8,128)(2,1)} %w_first_ref.1) | copy-start | bytes 1179652
  10.5 14.1 %copy-start.5 = (bf16[1280,256]{1,0:T(8,128)(2,1)S(1)}, bf16[1280,256]{1,0:T(8,128)(2,1)}, u32[]{:S(2)}) copy-start(bf16[1280,256]{1,0:T(8,128)(2,1)} %nodes_ref.5) | copy-start | bytes 1966084
  10.5 14.1 %copy-start.6 = (bf16[1280,256]{1,0:T(8,128)(2,1)S(1)}, bf16[1280,256]{1,0:T(8,128)(2,1)}, u32[]{:S(2)}) copy-start(bf16[1280,256]{1,0:T(8,128)(2,1)} %cot_ref.1) | copy-start | bytes 1966084
  10.6 14.1 %copy-start.7 = (bf16[512,256]{1,0:T(8,128)(2,1)S(1)}, bf16[512,256]{1,0:T(8,128)(2,1)}, u32[]{:S(2)}) copy-start(bf16[512,256]{1,0:T(8,128)(2,1)} %n_first_ref.1) | copy-start | bytes 786436
  10.6 14.1 %copy-start.8 = (bf16[256,256]{1,0:T(8,128)(2,1)S(1)}, bf16[256,256]{1,0:T(8,128)(2,1)}, u32[]{:S(2)}) copy-start(bf16[256,256]{1,0:T(8,128)(2,1)} %w_second_ref.1) | copy-start | bytes 393220
  10.6 14.1 %copy-start.9 = (bf16[256,256]{1,0:T(8,128)(2,1)S(1)}, bf16[256,256]{1,0:T(8,128)(2,1)}, u32[]{:S(2)}) copy-start(bf16[256,256]{1,0:T(8,128)(2,1)} %n_second_ref.1) | copy-start | bytes 393220
  10.6 14.1 %copy-start.10 = (s32[1280,12]{0,1:T(8,128)S(1)}, s32[1280,12]{0,1:T(8,128)}, u32[]{:S(2)}) copy-start(s32[1280,12]{0,1:T(8,128)} %param.21) | copy-start | bytes 184324
  10.6 14.1 %copy-start.12 = (s32[1280,12]{0,1:T(8,128)S(1)}, s32[1280,12]{0,1:T(8,128)}, u32[]{:S(2)}) copy-start(s32[1280,12]{0,1:T(8,128)} %param.20) | copy-start | bytes 184324
  62.5 1.9 %collective-permute-start.2 = (bf16[960,256]{1,0:T(8,128)(2,1)S(1)}, bf16[960,256]{1,0:T(8,128)(2,1)S(1)}, u32[]{:S(2)}, u32[]{:S(2)}) collective-permute-start(bf16[960,256]{1,0:T(8,128)(2,1)S(1)} %get-tuple-element.61), channel_id=1, source_target_pairs={{0,2},{1,3},{2,0},{3,1},{4,6},{5,7},{6,4},{7,5},{8,10},{9,11},{10,... | collective-permute-start | bytes 1474568 | tf_op jit(solution)/shard_map/ppermute | solution.py:573
  64.5 9.3 %collective-permute-start.3 = (bf16[240,256]{1,0:T(8,128)(2,1)S(1)}, bf16[240,256]{1,0:T(8,128)(2,1)S(1)}, u32[]{:S(2)}, u32[]{:S(2)}) collective-permute-start(bf16[240,256]{1,0:T(8,128)(2,1)S(1)} %get-tuple-element.64), channel_id=1, source_target_pairs={{0,4},{1,5},{2,6},{3,7},{4,0},{5,1},{6,2},{7,3},{8,12},{9,13},{10,... | collective-permute-start | bytes 368648 | tf_op jit(solution)/shard_map/ppermute | solution.py:573
  64.6 9.3 %collective-permute-start.4 = (bf16[240,256]{1,0:T(8,128)(2,1)S(1)}, bf16[240,256]{1,0:T(8,128)(2,1)S(1)}, u32[]{:S(2)}, u32[]{:S(2)}) collective-permute-start(bf16[240,256]{1,0:T(8,128)(2,1)S(1)} %get-tuple-element.65), channel_id=1, source_target_pairs={{0,1},{1,0},{2,3},{3,2},{4,5},{5,4},{6,7},{7,6},{8,9},{9,8},{10,11... | collective-permute-start | bytes 368648 | tf_op jit(solution)/shard_map/ppermute | solution.py:573
  66.2 7.7 %collective-permute-start.5 = (bf16[240,256]{1,0:T(8,128)(2,1)S(1)}, bf16[240,256]{1,0:T(8,128)(2,1)S(1)}, u32[]{:S(2)}, u32[]{:S(2)}) collective-permute-start(bf16[240,256]{1,0:T(8,128)(2,1)S(1)} %get-tuple-element.66), channel_id=1, source_target_pairs={{0,5},{1,4},{2,7},{3,6},{4,1},{5,0},{6,3},{7,2},{8,13},{9,12},{10,... | collective-permute-start | bytes 368648 | tf_op jit(solution)/shard_map/ppermute | solution.py:573
  73.9 11.3 %collective-permute-start.6 = (bf16[240,256]{1,0:T(8,128)(2,1)S(1)}, bf16[240,256]{1,0:T(8,128)(2,1)S(1)}, u32[]{:S(2)}, u32[]{:S(2)}) collective-permute-start(bf16[240,256]{1,0:T(8,128)(2,1)S(1)} %sum_parts.2.own_ref), channel_id=1, source_target_pairs={{0,8},{1,9},{2,10},{3,11},{4,12},{5,13},{6,14},{7,15},{8,0},{9,1},... | collective-permute-start | bytes 368648 | tf_op jit(solution)/shard_map/ppermute | solution.py:573
  74.0 13.3 %collective-permute-start.7 = (bf16[240,256]{1,0:T(8,128)(2,1)S(1)}, bf16[240,256]{1,0:T(8,128)(2,1)S(1)}, u32[]{:S(2)}, u32[]{:S(2)}) collective-permute-start(bf16[240,256]{1,0:T(8,128)(2,1)S(1)} %sum_parts.2.own_ref), channel_id=1, source_target_pairs={{0,16},{1,17},{2,18},{3,19},{4,20},{5,21},{6,22},{7,23},{8,24},{9,... | collective-permute-start | bytes 368648 | tf_op jit(solution)/shard_map/ppermute | solution.py:573
  78.1 9.2 %collective-permute-start.8 = (bf16[240,256]{1,0:T(8,128)(2,1)S(1)}, bf16[240,256]{1,0:T(8,128)(2,1)S(1)}, u32[]{:S(2)}, u32[]{:S(2)}) collective-permute-start(bf16[240,256]{1,0:T(8,128)(2,1)S(1)} %sum_parts.2.own_ref), channel_id=1, source_target_pairs={{0,24},{1,25},{2,26},{3,27},{4,28},{5,29},{6,30},{7,31},{8,16},{9,... | collective-permute-start | bytes 368648 | tf_op jit(solution)/shard_map/ppermute | solution.py:573
  87.4 10.4 %collective-permute-start.9 = (bf16[240,256]{1,0:T(8,128)(2,1)S(1)}, bf16[240,256]{1,0:T(8,128)(2,1)S(1)}, u32[]{:S(2)}, u32[]{:S(2)}) collective-permute-start(bf16[240,256]{1,0:T(8,128)(2,1)S(1)} %sum_parts.3.refs_0_), channel_id=1, source_target_pairs={{0,4},{1,5},{2,6},{3,7},{4,0},{5,1},{6,2},{7,3},{8,12},{9,13},{10,... | collective-permute-start | bytes 368648 | tf_op jit(solution)/shard_map/ppermute | solution.py:573
  89.1 8.8 %collective-permute-start.10 = (bf16[240,256]{1,0:T(8,128)(2,1)S(1)}, bf16[240,256]{1,0:T(8,128)(2,1)S(1)}, u32[]{:S(2)}, u32[]{:S(2)}) collective-permute-start(bf16[240,256]{1,0:T(8,128)(2,1)S(1)} %sum_parts.3.refs_0_), channel_id=1, source_target_pairs={{0,1},{1,0},{2,3},{3,2},{4,5},{5,4},{6,7},{7,6},{8,9},{9,8},{10,11... | collective-permute-start | bytes 368648 | tf_op jit(solution)/shard_map/ppermute | solution.py:573
  90.6 7.3 %collective-permute-start.11 = (bf16[240,256]{1,0:T(8,128)(2,1)S(1)}, bf16[240,256]{1,0:T(8,128)(2,1)S(1)}, u32[]{:S(2)}, u32[]{:S(2)}) collective-permute-start(bf16[240,256]{1,0:T(8,128)(2,1)S(1)} %sum_parts.3.refs_0_), channel_id=1, source_target_pairs={{0,5},{1,4},{2,7},{3,6},{4,1},{5,0},{6,3},{7,2},{8,13},{9,12},{10,... | collective-permute-start | bytes 368648 | tf_op jit(solution)/shard_map/ppermute | solution.py:573
  97.9 13.2 %collective-permute-start.14 = (bf16[960,256]{1,0:T(8,128)(2,1)S(1)}, bf16[960,256]{1,0:T(8,128)(2,1)S(1)}, u32[]{:S(2)}, u32[]{:S(2)}) collective-permute-start(bf16[960,256]{1,0:T(8,128)(2,1)S(1)} %pad_maximum_fusion), channel_id=1, source_target_pairs={{0,2},{1,3},{2,0},{3,1},{4,6},{5,7},{6,4},{7,5},{8,10},{9,11},{10,... | collective-permute-start | bytes 1474568 | tf_op jit(solution)/shard_map/ppermute | solution.py:573
  98.8 8.9 %collective-permute-start.12 = (bf16[256,256]{1,0:T(8,128)(2,1)S(1)}, bf16[256,256]{1,0:T(8,128)(2,1)S(1)}, u32[]{:S(2)}, u32[]{:S(2)}) collective-permute-start(bf16[256,256]{1,0:T(8,128)(2,1)S(1)} %get-tuple-element.100), channel_id=1, source_target_pairs={{0,30},{2,0},{4,2},{6,4},{8,6},{10,8},{12,10},{14,12},{16,14},{18,... | collective-permute-start | bytes 393224 | tf_op jit(solution)/shard_map/ppermute | solution.py:583
  102.4 7.1 %collective-permute-start.13 = (bf16[256,256]{1,0:T(8,128)(2,1)S(1)}, bf16[256,256]{1,0:T(8,128)(2,1)S(1)}, u32[]{:S(2)}, u32[]{:S(2)}) collective-permute-start(bf16[256,256]{1,0:T(8,128)(2,1)S(1)} %get-tuple-element.99), channel_id=1, source_target_pairs={{0,2},{2,4},{4,6},{6,8},{8,10},{10,12},{12,14},{14,16},{16,18},{18... | collective-permute-start | bytes 393224 | tf_op jit(solution)/shard_map/ppermute | solution.py:583
  (12 other events, 108.8 us)

commit v3 on v2

--- a/solution.py
+++ b/solution.py
@@ -14,6 +14,9 @@
 PARTS = 5
 PARTS2 = 5
 CHUNK = 64
+OWN = 3
+SPREAD = 6
+EDGE = 3
 BOTH = ("face", "sub")
 MIB = 1024 * 1024
 VMEM_LIMIT = 30 * MIB
@@ -79,27 +82,42 @@
     return centre * scale, scale
 
 
-def pick_kernel(lists_ref, nodes_ref, next_ref, prev_ref):
+def pick_kernel(
+    lists_hbm, nodes_hbm, index_hbm, next_ref, prev_ref, nodes_ref, index_ref, lists_ref, sems
+):
+    pairs = ((lists_hbm, lists_ref), (nodes_hbm, nodes_ref), (index_hbm, index_ref))
+    copies = [pltpu.make_async_copy(a, b, sems.at[i]) for i, (a, b) in enumerate(pairs)]
+    for copy in copies:
+        copy.start()
+    for copy in copies:
+        copy.wait()
     rows = nodes_ref.shape[0]
     halo = lists_ref.shape[1]
     for side, out_ref in ((0, next_ref), (1, prev_ref)):
         for at in range(0, halo, LANES):
-            index = down(lists_ref[side : side + 1, at : at + LANES])
+            picked = down(lists_ref[side : side + 1, at : at + LANES])
             out_ref[at : at + LANES, :] = dot(
-                hot_lanes(index, 0, rows), nodes_ref[...]
+                hot_lanes(picked, 0, rows), nodes_ref[...]
             ).astype(BF16)
 
 
-def pick(lists, nodes):
+def in_hbm(array):
+    return pltpu.with_memory_space_constraint(array, pltpu.HBM)
+
+
+def pick(lists, nodes, index):
     halo, width = lists.shape[1], nodes.shape[1]
-    out = jax.ShapeDtypeStruct((halo, width), BF16)
+    out = pltpu.VMEM((halo, width), BF16)
     return pl.pallas_call(
         pick_kernel,
-        out_shape=(out, out),
+        in_specs=[pl.BlockSpec(memory_space=pltpu.HBM)] * 3,
+        out_specs=[pl.BlockSpec(memory_space=pltpu.VMEM)] * 4,
+        out_shape=(out, out, pltpu.VMEM(nodes.shape, BF16), pltpu.VMEM(index.shape, jnp.int32)),
+        scratch_shapes=[pltpu.VMEM(lists.shape, jnp.int32), pltpu.SemaphoreType.DMA((3,))],
         compiler_params=params(),
         cost_estimate=cost(4 * halo * nodes.size, 2 * nodes.size),
         name="pick_rows",
-    )(lists, nodes)
+    )(in_hbm(lists), in_hbm(nodes), in_hbm(index))
 
 
 def in_vmem(array):
@@ -108,12 +126,13 @@
 
 def own_kernel(index_ref, nodes_ref, out_ref):
     rows = nodes_ref.shape[0]
-    k = pl.program_id(0)
-    row = index_ref[pl.ds(k, 1), :]
-    column = jnp.concatenate(
-        [down(row[:, at : at + LANES]) for at in range(0, rows, LANES)], axis=0
-    )
-    out_ref[0] = dot(hot_lanes(column, 0, rows), nodes_ref[...]).astype(BF16)
+    slots = out_ref.shape[0]
+    for j in range(slots):
+        row = index_ref[pl.ds(pl.program_id(0) * slots + j, 1), :]
+        column = jnp.concatenate(
+            [down(row[:, at : at + LANES]) for at in range(0, rows, LANES)], axis=0
+        )
+        out_ref[j] = dot(hot_lanes(column, 0, rows), nodes_ref[...]).astype(BF16)
 
 
 def own_senders(index, nodes):
@@ -121,9 +140,9 @@
     width = nodes.shape[1]
     return pl.pallas_call(
         own_kernel,
-        grid=(degree,),
+        grid=(degree // OWN,),
         in_specs=[pl.BlockSpec(memory_space=pltpu.VMEM)] * 2,
-        out_specs=pl.BlockSpec((1, rows, width), lambda i: (i, 0, 0)),
+        out_specs=pl.BlockSpec((OWN, rows, width), lambda i: (i, 0, 0)),
         out_shape=pltpu.HBM((degree, rows, width), BF16),
         compiler_params=params(30 * MIB),
         cost_estimate=cost(2 * degree * rows * rows * width, 2 * degree * rows * width),
@@ -147,7 +166,7 @@
     w_second_ref,
     n_first_ref,
     n_second_ref,
-    mixed_ref,
+    mixed_hbm,
     grad_nodes_ref,
     hat_ref,
     away_ref,
@@ -164,6 +183,9 @@
     half_first,
     half_second,
     bias_scr,
+    mixed_ref,
+    mixed_sem,
+    centred,
 ):
     step = pl.program_id(0)
     rows, width = nodes_ref.shape
@@ -179,7 +201,9 @@
     @pl.when(step == 0)
     def begin():
         half_first[...] = (w_first_ref[...].astype(F32) * 0.5).astype(BF16)
-        half_second[...] = (w_second_ref[...].astype(F32) * 0.5).astype(BF16)
+        second = w_second_ref[...].astype(F32)
+        half_second[...] = (second * 0.5).astype(BF16)
+        centred[...] = (second - row_mean(second)).astype(BF16)
         sum_scr[...] = jnp.zeros(sum_scr.shape, F32)
         count_scr[...] = jnp.zeros(count_scr.shape, F32)
         bias_scr[...] = jnp.zeros(bias_scr.shape, F32)
@@ -192,6 +216,7 @@
         k = step
         joint = index_ref[pl.ds(k, 1), :] * 2 + valid_ref[pl.ds(k, 1), :]
         part = rows // PARTS
+        centred_b2 = e_b2 - row_mean(e_b2)
         columns, entered = {}, {}
 
         def choose(p):
@@ -218,14 +243,13 @@
                 acts.append(act)
                 act_scr[k, here, :] = act
                 slope_scr[k, here, :] = slope.astype(BF16)
-            return dot(jnp.concatenate(acts, axis=0), w_second_ref[...])
+            return dot(jnp.concatenate(acts, axis=0), centred[...])
 
         def leave(p, second):
             for at in range(0, part, CHUNK):
                 here = slice(p * part + at, p * part + at + CHUNK)
                 live = (columns[p][at : at + CHUNK] & 1).astype(F32)
-                value = second[at : at + CHUNK] + e_b2
-                centre = value - row_mean(value)
+                centre = second[at : at + CHUNK] + centred_b2
                 scale = lax.rsqrt(row_mean(centre * centre) + 1e-05) * live
                 hat = centre * wide(scale)
                 hat_ref[k, here, :] = hat.astype(BF16)
@@ -294,6 +318,7 @@
         acc_scr[at_nfirst + width : at_nfirst + 2 * width, :] = dot_rows(
             jnp.concatenate(gathered, axis=0), all_c
         )
+        pltpu.make_async_copy(mixed_ref, mixed_hbm, mixed_sem).start()
         for row, values in ((4, c_sums), (5, d_sums), (6, hat_sums), (7, up_sums)):
             acc_scr[at_vec + row : at_vec + row + 1, :] = sum(values)
 
@@ -339,6 +364,7 @@
     @pl.when(step == 2 * degree)
     def hand_over():
         outer(degree - 1)
+        pltpu.make_async_copy(mixed_ref, mixed_hbm, mixed_sem).wait()
         acc_scr[at_vec + 1 : at_vec + 2, :] = col_sum(bias_scr[...])
         acc_scr[at_vec : at_vec + 1, :] = col_sum(sum_scr[...])
         received = sum_scr[...].astype(BF16)
@@ -372,7 +398,7 @@
         num_scalar_prefetch=1,
         grid=(2 * degree + 1,),
         in_specs=[edge_spec, own_spec] + [resident] * len(held),
-        out_specs=[resident] * 5,
+        out_specs=[pl.BlockSpec(memory_space=pltpu.HBM)] + [resident] * 4,
         scratch_shapes=[
             pltpu.VMEM((degree, rows, width), BF16),
             pltpu.VMEM((degree, rows, width), BF16),
@@ -386,13 +412,16 @@
             pltpu.VMEM(w1.shape, BF16),
             pltpu.VMEM(w2.shape, BF16),
             pltpu.VMEM((8, width), F32),
+            pltpu.VMEM((rows, width), BF16),
+            pltpu.SemaphoreType.DMA,
+            pltpu.VMEM(w2.shape, BF16),
         ],
     )
     return pl.pallas_call(
         functools.partial(main_kernel, degree, part_rows),
         grid_spec=grid_spec,
         out_shape=(
-            pltpu.VMEM((rows, width), BF16),
+            pltpu.HBM((rows, width), BF16),
             pltpu.VMEM((rows, width), F32),
             pltpu.VMEM((degree, rows, width), BF16),
             pltpu.VMEM((total // 2, width), BF16),
@@ -411,55 +440,58 @@
 
 
 def spread_kernel(first, index_ref, grad_ref, weight_ref, *rest):
-    *extra, out_ref, total = rest
-    degree = grad_ref.shape[0]
+    *base, out_ref, total = rest
+    degree, count, width = grad_ref.shape
     rows = total.shape[0]
-    k = pl.program_id(0) * 2
-    hots = [hot_rows(index_ref[pl.ds(k + j, 1), :], first, rows) for j in range(2)]
-    count, width = grad_ref.shape[1:]
+    step = pl.program_id(0)
+    k = step * SPREAD
+    hots = [hot_rows(index_ref[pl.ds(k + j, 1), :], first, rows) for j in range(SPREAD)]
     part = dot(
         jnp.concatenate(hots, axis=1),
-        grad_ref[pl.ds(k, 2)].reshape(2 * count, width),
+        grad_ref[pl.ds(k, SPREAD)].reshape(SPREAD * count, width),
     )
 
-    @pl.when(k == 0)
+    @pl.when(step == 0)
     def start():
         total[...] = part
 
-    @pl.when(k > 0)
+    @pl.when(step > 0)
     def go_on():
         total[...] += part
 
-    @pl.when(k == degree - 2)
+    @pl.when(step == pl.num_programs(0) - 1)
     def finish():
         result = split_back(total[...], weight_ref[...])
-        if extra:
-            result = result + extra[0][first : first + rows, :]
+        if base:
+            result = result + base[0][first : first + rows, :]
         out_ref[...] = result.astype(out_ref.dtype)
 
 
-def spread(index, grad, weight, first, rows, dtype, extra=None):
+def spread(index, grad, weight, first, rows, dtype, *base):
     degree, count, width = grad.shape
     resident = pl.BlockSpec(memory_space=pltpu.VMEM)
-    held = [index, grad, weight] + ([] if extra is None else [extra])
     return pl.pallas_call(
         functools.partial(spread_kernel, first),
-        grid=(degree // 2,),
-        in_specs=[resident] * len(held),
+        grid=(degree // SPREAD,),
+        in_specs=[resident] * (3 + len(base)),
         out_specs=resident,
         out_shape=pltpu.VMEM((rows, width), dtype),
         scratch_shapes=[pltpu.VMEM((rows, width), F32)],
         compiler_params=params(),
         cost_estimate=cost(2 * rows * grad.size, 2 * grad.size),
         name="spread_rows",
-    )(*held)
-
-
-def edge_kernel(grad_ref, weight_ref, out_ref):
+    )(index, grad, weight, *base)
+
+
+def edge_kernel(grad_ref, weight_ref, out_ref, turned):
     slots, rows, width = out_ref.shape
-    k = pl.program_id(0) * slots
-    grad = grad_ref[pl.ds(k, slots)].reshape(slots * rows, width)
-    out_ref[...] = dot_back(grad, weight_ref[...]).astype(BF16).reshape(slots, rows, width)
+
+    @pl.when(pl.program_id(0) == 0)
+    def turn():
+        turned[...] = weight_ref[...].T
+
+    grad = grad_ref[pl.ds(pl.program_id(0) * slots, slots)].reshape(slots * rows, width)
+    out_ref[...] = dot(grad, turned[...]).astype(BF16).reshape(slots, rows, width)
 
 
 def edge_grads(grad, weight):
@@ -467,38 +499,15 @@
     resident = pl.BlockSpec(memory_space=pltpu.VMEM)
     return pl.pallas_call(
         edge_kernel,
-        grid=(degree // 2,),
+        grid=(degree // EDGE,),
         in_specs=[resident, resident],
-        out_specs=pl.BlockSpec((2, count, width), lambda i: (i, 0, 0)),
+        out_specs=pl.BlockSpec((EDGE, count, width), lambda i: (i, 0, 0)),
         out_shape=jax.ShapeDtypeStruct(grad.shape, BF16),
+        scratch_shapes=[pltpu.VMEM((width, width), BF16)],
         compiler_params=params(),
         cost_estimate=cost(2 * grad.size * width, 4 * grad.size),
         name="edge_grads",
     )(grad, weight)
-
-
-def final_kernel(lists_ref, low_ref, high_ref, next_ref, prev_ref, out_ref):
-    rows = out_ref.shape[0]
-    low = low_ref.shape[0]
-    for first, part_ref in ((0, low_ref), (low, high_ref)):
-        count = part_ref.shape[0]
-        out_ref[first : first + count, :] = (
-            part_ref[...]
-            + dot(hot_rows(lists_ref[0:1, :], first, count), next_ref[...])
-            + dot(hot_rows(lists_ref[1:2, :], first, count), prev_ref[...])
-        )
-
-
-def final(lists, low, high, ret_next, ret_prev):
-    rows = low.shape[0] + high.shape[0]
-    width = low.shape[1]
-    return pl.pallas_call(
-        final_kernel,
-        out_shape=jax.ShapeDtypeStruct((rows, width), F32),
-        compiler_params=params(),
-        cost_estimate=cost(4 * rows * ret_next.size, 8 * rows * width),
-        name="returned_rows",
-    )(lists, low, high, ret_next, ret_prev)
 
 
 def split_kernel(keep_ref, came_ref, own_ref, *away_refs):
@@ -538,8 +547,35 @@
     )(own, *came)
 
 
-def unpack_kernel(part_rows, place_ref, *refs):
-    pieces, outs, full = refs[:5], refs[5:-1], refs[-1]
+def join_kernel(*refs):
+    *pieces, out_ref = refs
+    at = 0
+    for piece in pieces:
+        out_ref[at : at + piece.shape[0], :] = piece[...]
+        at += piece.shape[0]
+
+
+def joined_parts(pieces):
+    rows = sum(piece.shape[0] for piece in pieces)
+    return pl.pallas_call(
+        join_kernel,
+        out_shape=pltpu.VMEM((rows, pieces[0].shape[1]), BF16),
+        compiler_params=params(),
+        name="join_parts",
+    )(*pieces)
+
+
+def finish_kernel(part_rows, place_ref, *refs):
+    pieces, (lists_ref, low_ref, high_ref, next_ref, prev_ref) = refs[:5], refs[5:10]
+    nodes_ref, outs, full = refs[10], refs[11:-1], refs[-1]
+    low = low_ref.shape[0]
+    for first, part_ref in ((0, low_ref), (low, high_ref)):
+        count = part_ref.shape[0]
+        hots = [hot_rows(lists_ref[side : side + 1, :], first, count) for side in range(2)]
+        returned = jnp.concatenate([next_ref[...], prev_ref[...]], axis=0)
+        nodes_ref[first : first + count, :] = part_ref[...] + dot(
+            jnp.concatenate(hots, axis=1), returned
+        )
     place = place_ref[0]
     p = 0
     for piece in pieces:
@@ -554,18 +590,21 @@
         at += count
 
 
-def unpack(place, pieces, row_counts):
+def finish(place, pieces, lists, low, high, ret_next, ret_prev, row_counts):
     part_rows, width = pieces[0].shape
-    total = 8 * part_rows
-    return pl.pallas_call(
-        functools.partial(unpack_kernel, part_rows),
+    rows = low.shape[0] + high.shape[0]
+    held = [*pieces, lists, low, high, ret_next, ret_prev]
+    return pl.pallas_call(
+        functools.partial(finish_kernel, part_rows),
         in_specs=[pl.BlockSpec(memory_space=pltpu.SMEM)]
-        + [pl.BlockSpec(memory_space=pltpu.VMEM)] * 5,
-        out_shape=tuple(jax.ShapeDtypeStruct((n, width), F32) for n in row_counts),
-        scratch_shapes=[pltpu.VMEM((total, width), F32)],
+        + [pl.BlockSpec(memory_space=pltpu.VMEM)] * len(held),
+        out_shape=(jax.ShapeDtypeStruct((rows, width), F32),)
+        + tuple(jax.ShapeDtypeStruct((n, width), F32) for n in row_counts),
+        scratch_shapes=[pltpu.VMEM((8 * part_rows, width), F32)],
         compiler_params=params(),
-        name="unpack_sums",
-    )(place, *pieces)
+        cost_estimate=cost(4 * rows * ret_next.size, 8 * rows * width),
+        name="finish",
+    )(place, *held)
 
 
 def traded(value, mask):
@@ -632,8 +671,7 @@
         place = place * 2 + jnp.where((me & mask) != 0, 1, 0)
     place = place.astype(jnp.int32).reshape(1)
 
-    nodes_held, index_held = in_vmem(nodes), in_vmem(index)
-    to_next, to_prev = pick(in_vmem(lists), nodes_held)
+    to_next, to_prev, nodes_held, index_held = pick(lists, nodes, index)
     from_prev = passed_along(to_next, 1)
     from_next = passed_along(to_prev, -1)
     own = own_senders(index_held, nodes_held)
@@ -677,18 +715,17 @@
         if not doubling:
             grad_a, part = tied(grad_a, part)
             low = spread(index_held, grad_a, send_weight, 0, half, F32, grad_nodes)
-            came, low = tied(came, low)
+            grad_edges = edge_grads(grad_a, edge_weight)
+            came, low, grad_edges = tied(came, low, grad_edges)
         part = sum_parts(part, came)
     came = [traded(part, mask) for mask in plane]
-    grad_a, part = tied(grad_a, part)
+    grad_a, part, ret_next, ret_prev = tied(grad_a, part, ret_next, ret_prev)
     high = spread(index_held, grad_a, send_weight, half, half, F32, grad_nodes)
     came, high = tied(came, high)
     pieces = [part] + came
-    pieces.append(traded(jnp.concatenate(pieces, axis=0), core))
-    grad_edges = edge_grads(grad_a, edge_weight)
-    grad_nodes = final(lists, low, high, ret_next, ret_prev)
+    pieces.append(traded(joined_parts(pieces), core))
     counts = (edge_first.shape[0], width, node_first.shape[0], width) + (1,) * 8
-    sums = unpack(place, pieces, counts)
+    grad_nodes, *sums = finish(place, pieces, lists, low, high, ret_next, ret_prev, counts)
     vectors = [v.reshape(width) for v in sums[4:]]
     return (
         mixed,

time: 113 us -> 103 us (0.912)
  Pallas kernels: 80.1 us -> 74.4 us
  local copies, waits for them, and re-layouts: 4.77 us -> 0.21 us
    unnamed x43 -> x36, local copies, waits for them, and re-layouts: 4.67 us -> 0.1 us
    pallas_call x8, Pallas kernels: 42.1 us -> 37.7 us  [the longest x3 16.6 us: spread(): pl.pallas_call(functools.partial(spread_kernel, first), grid=(degree // S...]
    ppermute x4, waiting for transfers between devices: 1.78 us -> 0.01 us  [passed_along(): return lax.ppermute(value, 'face', pairs)]
    pallas_call x1, Pallas kernels: 37.8 us -> 36.4 us  [main(): pl.pallas_call(functools.partial(main_kernel, degree, part_rows), grid_sp...]
  transfers between devices with their start and end apart: 15 -> 15, of which waited for: 3 -> 3; matrix products, arithmetic and copies ran while one was open for 1% -> 0% of each run, Pallas kernels for 36% -> 33%
where the time goes in v3:
time: 103 us; the launch traced here: 102 us
  Pallas kernels  74.4 us (72%)
  starting transfers between devices  21.7 us (21%)
  waiting for transfers between devices  4.67 us (5%)
  between operations  1.23 us (1%)
    pallas_call x1, Pallas kernels, main(): pl.pallas_call(functools.partial(main_kernel, degree, part_rows), grid_sp...  36.4 us
    pallas_call x3, Pallas kernels, spread(): pl.pallas_call(functools.partial(spread_kernel, first), grid=(degree // S...  16.6 us
    pallas_call x1, Pallas kernels, own_senders(): pl.pallas_call(own_kernel, grid=(degree // OWN,), in_specs=[pl.BlockSpec(...  12.4 us
    ppermute x11, starting transfers between devices, traded(): return lax.ppermute(value, BOTH, [(i, i ^ mask) for i in range(count)])  11.7 us
    ppermute x4, starting transfers between devices, passed_along(): return lax.ppermute(value, 'face', pairs)  10.1 us
    pallas_call x1, Pallas kernels, edge_grads(): pl.pallas_call(edge_kernel, grid=(degree // EDGE,), in_specs=[resident, r...  4.7 us
    ppermute x11, waiting for transfers between devices, traded(): return lax.ppermute(value, BOTH, [(i, i ^ mask) for i in range(count)])  4.66 us
    pallas_call x1, Pallas kernels, finish(): pl.pallas_call(functools.partial(finish_kernel, part_rows), in_specs=[pl....  2.26 us
  transfers between devices with their start and end apart: 15, of which 3 were waited for; matrix products, arithmetic and copies ran while one was open for 0% of the time, Pallas kernels for 33%

profile of v3, /device:TPU:0, one launch (start us, length us, event | category | flops | bytes accessed | tf_op | source)
XLA Modules:
  0.0 102.3 jit_solution(9935927606735614705)
XLA Ops:
  0.6 1.7 %pick_rows.1 = (bf16[256,256]{1,0:T(8,128)(2,1)S(1)}, bf16[256,256]{1,0:T(8,128)(2,1)S(1)}, bf16[1280,256]{1,0:T(8,128)(2,1)S(1)}, s32[12,1280]{1,0:T(8,128)S(1)}) custom-call(s32[2,256]{1,0:T(2,128)} %bitcast.14, bf16[1280,256]{1,0:T(8,128)(2,1)} %nodes_hbm.1, s32[12,1280]{1,0:T(8,128)} %bitcast.19), custom_call_target="tpu_custom_call" | custom-call | flops 335544320 | bytes 655360 | tf_op jit(solution)/shard_map/pick_rows/pallas_call | solution.py:111
  2.4 0.5 collective-permute-start
  2.9 5.1 %collective-permute-start.1 = (bf16[256,256]{1,0:T(8,128)(2,1)S(1)}, bf16[256,256]{1,0:T(8,128)(2,1)S(1)}, u32[]{:S(2)}, u32[]{:S(2)}) collective-permute-start(bf16[256,256]{1,0:T(8,128)(2,1)S(1)} %get-tuple-element.65), channel_id=1, source_target_pairs={{0,30},{2,0},{4,2},{6,4},{8,6},{10,8},{12,10},{14,12},{16,14},{18,... | collective-permute-start | bytes 393224 | tf_op jit(solution)/shard_map/ppermute | solution.py:622
  8.1 12.4 %own_senders.1.own_ref = bf16[12,1280,256]{2,1,0:T(8,128)(2,1)} custom-call(s32[12,1280]{1,0:T(8,128)S(1)} %get-tuple-element.62.index_ref, bf16[1280,256]{1,0:T(8,128)(2,1)S(1)} %get-tuple-element.63.nodes_ref), custom_call_target="tpu_custom_call" | custom-call | flops 10066329600 | bytes 7864320 | tf_op jit(solution)/shard_map/own_senders/pallas_call | solution.py:141
  20.8 36.4 %edges_and_nodes.1 = (bf16[1280,256]{1,0:T(8,128)(2,1)}, f32[1280,256]{1,0:T(8,128)S(1)}, bf16[12,1280,256]{2,1,0:T(8,128)(2,1)S(1)}, bf16[960,256]{1,0:T(8,128)(2,1)S(1)}, f32[960,256]{1,0:T(8,128)S(1)}) custom-call(s32[1]{0:T(128)} %bitcast.place_ref, bf16[12,1280,256]{2,1,0:T(8,128)(2,1)} %bitcast.18, bf16[12,1280,256]{2,1,0:T(8,128)(2,1)} %own_senders.1.own_ref, ...), custom_call_target="tpu_custom_call" | custom-call | flops 18119393280 | bytes 31457280 | tf_op jit(solution)/shard_map/edges_and_nodes/pallas_call | solution.py:420
  57.3 0.1 collective-permute-start.2
  57.4 1.8 %collective-permute-done.2.came_ref = bf16[960,256]{1,0:T(8,128)(2,1)S(1)} collective-permute-done((bf16[960,256]{1,0:T(8,128)(2,1)S(1)}, bf16[960,256]{1,0:T(8,128)(2,1)S(1)}, u32[]{:S(2)}, u32[]{:S(2)}) %collective-permute-start.2) | collective-permute-done | bytes 491552 | tf_op jit(solution)/shard_map/ppermute | solution.py:612
  59.2 0.1 add_and_split.1
  59.4 2.0 %collective-permute-start.4 = (bf16[240,256]{1,0:T(8,128)(2,1)S(1)}, bf16[240,256]{1,0:T(8,128)(2,1)S(1)}, u32[]{:S(2)}, u32[]{:S(2)}) collective-permute-start(bf16[240,256]{1,0:T(8,128)(2,1)S(1)} %get-tuple-element.74), channel_id=1, source_target_pairs={{0,1},{1,0},{2,3},{3,2},{4,5},{5,4},{6,7},{7,6},{8,9},{9,8},{10,11... | collective-permute-start | bytes 368648 | tf_op jit(solution)/shard_map/ppermute | solution.py:612
  61.3 1.5 %collective-permute-start.5 = (bf16[240,256]{1,0:T(8,128)(2,1)S(1)}, bf16[240,256]{1,0:T(8,128)(2,1)S(1)}, u32[]{:S(2)}, u32[]{:S(2)}) collective-permute-start(bf16[240,256]{1,0:T(8,128)(2,1)S(1)} %get-tuple-element.75), channel_id=1, source_target_pairs={{0,5},{1,4},{2,7},{3,6},{4,1},{5,0},{6,3},{7,2},{8,13},{9,12},{10,... | collective-permute-start | bytes 368648 | tf_op jit(solution)/shard_map/ppermute | solution.py:612
  62.9 4.8 %spread_rows.3 = bf16[512,256]{1,0:T(8,128)(2,1)S(1)} custom-call(s32[12,1280]{1,0:T(8,128)S(1)} %copy-done.9, bf16[12,1280,256]{2,1,0:T(8,128)(2,1)S(1)} %get-tuple-element.87.grad_ref, bf16[256,256]{1,0:T(8,128)(2,1)S(1)} %get-tuple-element.110.weight_ref), custom_call_target="tpu_custom_call" | custom-call | flops 4026531840 | bytes 7864320 | tf_op jit(solution)/shard_map/spread_rows/pallas_call | solution.py:473
  67.7 1.0 collective-permute-done.5.refs_2_
  68.8 0.1 collective-permute-start.6
  68.8 2.6 %collective-permute-start.7 = (bf16[240,256]{1,0:T(8,128)(2,1)S(1)}, bf16[240,256]{1,0:T(8,128)(2,1)S(1)}, u32[]{:S(2)}, u32[]{:S(2)}) collective-permute-start(bf16[240,256]{1,0:T(8,128)(2,1)S(1)} %sum_parts.2.own_ref), channel_id=1, source_target_pairs={{0,16},{1,17},{2,18},{3,19},{4,20},{5,21},{6,22},{7,23},{8,24},{9,... | collective-permute-start | bytes 368648 | tf_op jit(solution)/shard_map/ppermute | solution.py:612
  71.4 1.8 %collective-permute-start.8 = (bf16[240,256]{1,0:T(8,128)(2,1)S(1)}, bf16[240,256]{1,0:T(8,128)(2,1)S(1)}, u32[]{:S(2)}, u32[]{:S(2)}) collective-permute-start(bf16[240,256]{1,0:T(8,128)(2,1)S(1)} %sum_parts.2.own_ref), channel_id=1, source_target_pairs={{0,24},{1,25},{2,26},{3,27},{4,28},{5,29},{6,30},{7,31},{8,16},{9,... | collective-permute-start | bytes 368648 | tf_op jit(solution)/shard_map/ppermute | solution.py:612
  73.3 4.4 %collective-permute-start.9 = (bf16[256,256]{1,0:T(8,128)(2,1)S(1)}, bf16[256,256]{1,0:T(8,128)(2,1)S(1)}, u32[]{:S(2)}, u32[]{:S(2)}) collective-permute-start(bf16[256,256]{1,0:T(8,128)(2,1)S(1)} %get-tuple-element.112), channel_id=1, source_target_pairs={{0,30},{2,0},{4,2},{6,4},{8,6},{10,8},{12,10},{14,12},{16,14},{18,... | collective-permute-start | bytes 393224 | tf_op jit(solution)/shard_map/ppermute | solution.py:622
  77.7 5.9 %spread_rows.4.refs_6_ = f32[640,256]{1,0:T(8,128)S(1)} custom-call(s32[12,1280]{1,0:T(8,128)S(1)} %copy-done.9, bf16[12,1280,256]{2,1,0:T(8,128)(2,1)S(1)} %get-tuple-element.87.grad_ref, bf16[256,256]{1,0:T(8,128)(2,1)S(1)} %get-tuple-element.110.weight_ref, f32[1280,256]{1,0:T(8,128)S(1)} %get-tuple-element.81.rest_0_), custom_call_target="tpu_custom_call" | custom-call | flops 5033164800 | bytes 7864320 | tf_op jit(solution)/shard_map/spread_rows/pallas_call | solution.py:473
  83.6 4.7 %edge_grads.1 = bf16[12,1280,256]{2,1,0:T(8,128)(2,1)} custom-call(bf16[12,1280,256]{2,1,0:T(8,128)(2,1)S(1)} %get-tuple-element.87.grad_ref, bf16[256,256]{1,0:T(8,128)(2,1)S(1)} %get-tuple-element.109.weight_ref), custom_call_target="tpu_custom_call" | custom-call | flops 2013265920 | bytes 15728640 | tf_op jit(solution)/shard_map/edge_grads/pallas_call | solution.py:500
  88.5 1.8 %collective-permute-start.12 = (bf16[240,256]{1,0:T(8,128)(2,1)S(1)}, bf16[240,256]{1,0:T(8,128)(2,1)S(1)}, u32[]{:S(2)}, u32[]{:S(2)}) collective-permute-start(bf16[240,256]{1,0:T(8,128)(2,1)S(1)} %sum_parts.3.refs_0_), channel_id=1, source_target_pairs={{0,1},{1,0},{2,3},{3,2},{4,5},{5,4},{6,7},{7,6},{8,9},{9,8},{10,11... | collective-permute-start | bytes 368648 | tf_op jit(solution)/shard_map/ppermute | solution.py:612
  90.3 1.7 %collective-permute-start.13 = (bf16[240,256]{1,0:T(8,128)(2,1)S(1)}, bf16[240,256]{1,0:T(8,128)(2,1)S(1)}, u32[]{:S(2)}, u32[]{:S(2)}) collective-permute-start(bf16[240,256]{1,0:T(8,128)(2,1)S(1)} %sum_parts.3.refs_0_), channel_id=1, source_target_pairs={{0,5},{1,4},{2,7},{3,6},{4,1},{5,0},{6,3},{7,2},{8,13},{9,12},{10,... | collective-permute-start | bytes 368648 | tf_op jit(solution)/shard_map/ppermute | solution.py:612
  92.0 5.9 %spread_rows.5.refs_7_ = f32[640,256]{1,0:T(8,128)S(1)} custom-call(s32[12,1280]{1,0:T(8,128)S(1)} %copy-done.9, bf16[12,1280,256]{2,1,0:T(8,128)(2,1)S(1)} %get-tuple-element.87.grad_ref, bf16[256,256]{1,0:T(8,128)(2,1)S(1)} %get-tuple-element.110.weight_ref, f32[1280,256]{1,0:T(8,128)S(1)} %get-tuple-element.81.rest_0_), custom_call_target="tpu_custom_call" | custom-call | flops 5033164800 | bytes 7864320 | tf_op jit(solution)/shard_map/spread_rows/pallas_call | solution.py:473
  98.0 0.1 collective-permute-start.14
  98.1 1.9 %collective-permute-done.14.refs_4_ = bf16[960,256]{1,0:T(8,128)(2,1)S(1)} collective-permute-done((bf16[960,256]{1,0:T(8,128)(2,1)S(1)}, bf16[960,256]{1,0:T(8,128)(2,1)S(1)}, u32[]{:S(2)}, u32[]{:S(2)}) %collective-permute-start.14) | collective-permute-done | bytes 491552 | tf_op jit(solution)/shard_map/ppermute | solution.py:612
  99.9 2.3 %finish.1 = (f32[1280,256]{1,0:T(8,128)}, f32[768,256]{1,0:T(8,128)}, f32[256,256]{1,0:T(8,128)}, f32[512,256]{1,0:T(8,128)}, f32[256,256]{1,0:T(8,128)}, /*inde...) custom-call(s32[1]{0:T(128)} %bitcast.place_ref, ...), custom_call_target="tpu_custom_call" | custom-call | flops 335544320 | bytes 2621440 | tf_op jit(solution)/shard_map/finish/pallas_call | solution.py:597
  (67 shorter events, 0.6 us)
Async XLA Ops:
  2.3 18.2 %copy-start.7 = (bf16[1280,256]{1,0:T(8,128)(2,1)}, bf16[1280,256]{1,0:T(8,128)(2,1)S(1)}, u32[]{:S(2)}) copy-start(bf16[1280,256]{1,0:T(8,128)(2,1)S(1)} %get-tuple-element.63.nodes_ref) | copy-start | bytes 1966084
  2.3 18.1 %copy-start.8 = (s32[12,1280]{1,0:T(8,128)}, s32[12,1280]{1,0:T(8,128)S(1)}, u32[]{:S(2)}) copy-start(s32[12,1280]{1,0:T(8,128)S(1)} %get-tuple-element.62.index_ref) | copy-start | bytes 184324
  2.4 18.3 %collective-permute-start = (bf16[256,256]{1,0:T(8,128)(2,1)S(1)}, bf16[256,256]{1,0:T(8,128)(2,1)S(1)}, u32[]{:S(2)}, u32[]{:S(2)}) collective-permute-start(bf16[256,256]{1,0:T(8,128)(2,1)S(1)} %get-tuple-element.64), channel_id=1, source_target_pairs={{0,2},{2,4},{4,6},{6,8},{8,10},{10,12},{12,14},{14,16},{16,18},{18... | collective-permute-start | bytes 393224 | tf_op jit(solution)/shard_map/ppermute | solution.py:622
  2.9 17.9 %collective-permute-start.1 = (bf16[256,256]{1,0:T(8,128)(2,1)S(1)}, bf16[256,256]{1,0:T(8,128)(2,1)S(1)}, u32[]{:S(2)}, u32[]{:S(2)}) collective-permute-start(bf16[256,256]{1,0:T(8,128)(2,1)S(1)} %get-tuple-element.65), channel_id=1, source_target_pairs={{0,30},{2,0},{4,2},{6,4},{8,6},{10,8},{12,10},{14,12},{16,14},{18,... | collective-permute-start | bytes 393224 | tf_op jit(solution)/shard_map/ppermute | solution.py:622
  8.0 12.8 %copy-start = (bf16[768,256]{1,0:T(8,128)(2,1)S(1)}, bf16[768,256]{1,0:T(8,128)(2,1)}, u32[]{:S(2)}) copy-start(bf16[768,256]{1,0:T(8,128)(2,1)} %w_first_ref.1) | copy-start | bytes 1179652
  8.0 12.8 %copy-start.2 = (bf16[1280,256]{1,0:T(8,128)(2,1)S(1)}, bf16[1280,256]{1,0:T(8,128)(2,1)}, u32[]{:S(2)}) copy-start(bf16[1280,256]{1,0:T(8,128)(2,1)} %cot_ref.1) | copy-start | bytes 1966084
  8.0 12.8 %copy-start.3 = (bf16[512,256]{1,0:T(8,128)(2,1)S(1)}, bf16[512,256]{1,0:T(8,128)(2,1)}, u32[]{:S(2)}) copy-start(bf16[512,256]{1,0:T(8,128)(2,1)} %n_first_ref.1) | copy-start | bytes 786436
  8.0 12.8 %copy-start.4 = (bf16[256,256]{1,0:T(8,128)(2,1)S(1)}, bf16[256,256]{1,0:T(8,128)(2,1)}, u32[]{:S(2)}) copy-start(bf16[256,256]{1,0:T(8,128)(2,1)} %w_second_ref.1) | copy-start | bytes 393220
  8.0 12.8 %copy-start.5 = (bf16[256,256]{1,0:T(8,128)(2,1)S(1)}, bf16[256,256]{1,0:T(8,128)(2,1)}, u32[]{:S(2)}) copy-start(bf16[256,256]{1,0:T(8,128)(2,1)} %n_second_ref.1) | copy-start | bytes 393220
  8.1 12.8 %copy-start.6 = (s32[1280,12]{0,1:T(8,128)S(1)}, s32[1280,12]{0,1:T(8,128)}, u32[]{:S(2)}) copy-start(s32[1280,12]{0,1:T(8,128)} %param.21) | copy-start | bytes 184324
  20.8 42.0 %copy-start.9 = (s32[12,1280]{1,0:T(8,128)S(1)}, s32[12,1280]{1,0:T(8,128)}, u32[]{:S(2)}) copy-start(s32[12,1280]{1,0:T(8,128)} %copy-done.8) | copy-start | bytes 184324
  57.3 1.9 %collective-permute-start.2 = (bf16[960,256]{1,0:T(8,128)(2,1)S(1)}, bf16[960,256]{1,0:T(8,128)(2,1)S(1)}, u32[]{:S(2)}, u32[]{:S(2)}) collective-permute-start(bf16[960,256]{1,0:T(8,128)(2,1)S(1)} %get-tuple-element.69), channel_id=1, source_target_pairs={{0,2},{1,3},{2,0},{3,1},{4,6},{5,7},{6,4},{7,5},{8,10},{9,11},{10,... | collective-permute-start | bytes 1474568 | tf_op jit(solution)/shard_map/ppermute | solution.py:612
  59.3 8.4 %collective-permute-start.3 = (bf16[240,256]{1,0:T(8,128)(2,1)S(1)}, bf16[240,256]{1,0:T(8,128)(2,1)S(1)}, u32[]{:S(2)}, u32[]{:S(2)}) collective-permute-start(bf16[240,256]{1,0:T(8,128)(2,1)S(1)} %get-tuple-element.73), channel_id=1, source_target_pairs={{0,4},{1,5},{2,6},{3,7},{4,0},{5,1},{6,2},{7,3},{8,12},{9,13},{10,... | collective-permute-start | bytes 368648 | tf_op jit(solution)/shard_map/ppermute | solution.py:612
  59.4 8.3 %collective-permute-start.4 = (bf16[240,256]{1,0:T(8,128)(2,1)S(1)}, bf16[240,256]{1,0:T(8,128)(2,1)S(1)}, u32[]{:S(2)}, u32[]{:S(2)}) collective-permute-start(bf16[240,256]{1,0:T(8,128)(2,1)S(1)} %get-tuple-element.74), channel_id=1, source_target_pairs={{0,1},{1,0},{2,3},{3,2},{4,5},{5,4},{6,7},{7,6},{8,9},{9,8},{10,11... | collective-permute-start | bytes 368648 | tf_op jit(solution)/shard_map/ppermute | solution.py:612
  61.3 7.4 %collective-permute-start.5 = (bf16[240,256]{1,0:T(8,128)(2,1)S(1)}, bf16[240,256]{1,0:T(8,128)(2,1)S(1)}, u32[]{:S(2)}, u32[]{:S(2)}) collective-permute-start(bf16[240,256]{1,0:T(8,128)(2,1)S(1)} %get-tuple-element.75), channel_id=1, source_target_pairs={{0,5},{1,4},{2,7},{3,6},{4,1},{5,0},{6,3},{7,2},{8,13},{9,12},{10,... | collective-permute-start | bytes 368648 | tf_op jit(solution)/shard_map/ppermute | solution.py:612
  68.8 19.6 %collective-permute-start.6 = (bf16[240,256]{1,0:T(8,128)(2,1)S(1)}, bf16[240,256]{1,0:T(8,128)(2,1)S(1)}, u32[]{:S(2)}, u32[]{:S(2)}) collective-permute-start(bf16[240,256]{1,0:T(8,128)(2,1)S(1)} %sum_parts.2.own_ref), channel_id=1, source_target_pairs={{0,8},{1,9},{2,10},{3,11},{4,12},{5,13},{6,14},{7,15},{8,0},{9,1},... | collective-permute-start | bytes 368648 | tf_op jit(solution)/shard_map/ppermute | solution.py:612
  68.8 19.5 %collective-permute-start.7 = (bf16[240,256]{1,0:T(8,128)(2,1)S(1)}, bf16[240,256]{1,0:T(8,128)(2,1)S(1)}, u32[]{:S(2)}, u32[]{:S(2)}) collective-permute-start(bf16[240,256]{1,0:T(8,128)(2,1)S(1)} %sum_parts.2.own_ref), channel_id=1, source_target_pairs={{0,16},{1,17},{2,18},{3,19},{4,20},{5,21},{6,22},{7,23},{8,24},{9,... | collective-permute-start | bytes 368648 | tf_op jit(solution)/shard_map/ppermute | solution.py:612
  71.4 16.9 %collective-permute-start.8 = (bf16[240,256]{1,0:T(8,128)(2,1)S(1)}, bf16[240,256]{1,0:T(8,128)(2,1)S(1)}, u32[]{:S(2)}, u32[]{:S(2)}) collective-permute-start(bf16[240,256]{1,0:T(8,128)(2,1)S(1)} %sum_parts.2.own_ref), channel_id=1, source_target_pairs={{0,24},{1,25},{2,26},{3,27},{4,28},{5,29},{6,30},{7,31},{8,16},{9,... | collective-permute-start | bytes 368648 | tf_op jit(solution)/shard_map/ppermute | solution.py:612
  73.2 18.8 %collective-permute-start.10 = (bf16[256,256]{1,0:T(8,128)(2,1)S(1)}, bf16[256,256]{1,0:T(8,128)(2,1)S(1)}, u32[]{:S(2)}, u32[]{:S(2)}) collective-permute-start(bf16[256,256]{1,0:T(8,128)(2,1)S(1)} %get-tuple-element.111), channel_id=1, source_target_pairs={{0,2},{2,4},{4,6},{6,8},{8,10},{10,12},{12,14},{14,16},{16,18},{18... | collective-permute-start | bytes 393224 | tf_op jit(solution)/shard_map/ppermute | solution.py:622
  73.3 18.7 %collective-permute-start.9 = (bf16[256,256]{1,0:T(8,128)(2,1)S(1)}, bf16[256,256]{1,0:T(8,128)(2,1)S(1)}, u32[]{:S(2)}, u32[]{:S(2)}) collective-permute-start(bf16[256,256]{1,0:T(8,128)(2,1)S(1)} %get-tuple-element.112), channel_id=1, source_target_pairs={{0,30},{2,0},{4,2},{6,4},{8,6},{10,8},{12,10},{14,12},{16,14},{18,... | collective-permute-start | bytes 393224 | tf_op jit(solution)/shard_map/ppermute | solution.py:622
  88.4 9.5 %collective-permute-start.11 = (bf16[240,256]{1,0:T(8,128)(2,1)S(1)}, bf16[240,256]{1,0:T(8,128)(2,1)S(1)}, u32[]{:S(2)}, u32[]{:S(2)}) collective-permute-start(bf16[240,256]{1,0:T(8,128)(2,1)S(1)} %sum_parts.3.refs_0_), channel_id=1, source_target_pairs={{0,4},{1,5},{2,6},{3,7},{4,0},{5,1},{6,2},{7,3},{8,12},{9,13},{10,... | collective-permute-start | bytes 368648 | tf_op jit(solution)/shard_map/ppermute | solution.py:612
  88.5 9.4 %collective-permute-start.12 = (bf16[240,256]{1,0:T(8,128)(2,1)S(1)}, bf16[240,256]{1,0:T(8,128)(2,1)S(1)}, u32[]{:S(2)}, u32[]{:S(2)}) collective-permute-start(bf16[240,256]{1,0:T(8,128)(2,1)S(1)} %sum_parts.3.refs_0_), channel_id=1, source_target_pairs={{0,1},{1,0},{2,3},{3,2},{4,5},{5,4},{6,7},{7,6},{8,9},{9,8},{10,11... | collective-permute-start | bytes 368648 | tf_op jit(solution)/shard_map/ppermute | solution.py:612
  90.3 7.6 %collective-permute-start.13 = (bf16[240,256]{1,0:T(8,128)(2,1)S(1)}, bf16[240,256]{1,0:T(8,128)(2,1)S(1)}, u32[]{:S(2)}, u32[]{:S(2)}) collective-permute-start(bf16[240,256]{1,0:T(8,128)(2,1)S(1)} %sum_parts.3.refs_0_), channel_id=1, source_target_pairs={{0,5},{1,4},{2,7},{3,6},{4,1},{5,0},{6,3},{7,2},{8,13},{9,12},{10,... | collective-permute-start | bytes 368648 | tf_op jit(solution)/shard_map/ppermute | solution.py:612
  98.0 1.9 %collective-permute-start.14 = (bf16[960,256]{1,0:T(8,128)(2,1)S(1)}, bf16[960,256]{1,0:T(8,128)(2,1)S(1)}, u32[]{:S(2)}, u32[]{:S(2)}) collective-permute-start(bf16[960,256]{1,0:T(8,128)(2,1)S(1)} %join_parts.1), channel_id=1, source_target_pairs={{0,2},{1,3},{2,0},{3,1},{4,6},{5,7},{6,4},{7,5},{8,10},{9,11},{10,... | collective-permute-start | bytes 1474568 | tf_op jit(solution)/shard_map/ppermute | solution.py:612
  (9 other events, 112.4 us)

commit v4 on v3

--- a/solution.py
+++ b/solution.py
@@ -565,9 +565,7 @@
     )(*pieces)
 
 
-def finish_kernel(part_rows, place_ref, *refs):
-    pieces, (lists_ref, low_ref, high_ref, next_ref, prev_ref) = refs[:5], refs[5:10]
-    nodes_ref, outs, full = refs[10], refs[11:-1], refs[-1]
+def returned_kernel(lists_ref, low_ref, high_ref, next_ref, prev_ref, nodes_ref):
     low = low_ref.shape[0]
     for first, part_ref in ((0, low_ref), (low, high_ref)):
         count = part_ref.shape[0]
@@ -576,6 +574,21 @@
         nodes_ref[first : first + count, :] = part_ref[...] + dot(
             jnp.concatenate(hots, axis=1), returned
         )
+
+
+def returned_rows(lists, low, high, ret_next, ret_prev):
+    rows, width = low.shape[0] + high.shape[0], low.shape[1]
+    return pl.pallas_call(
+        returned_kernel,
+        out_shape=jax.ShapeDtypeStruct((rows, width), F32),
+        compiler_params=params(),
+        cost_estimate=cost(4 * rows * ret_next.size, 8 * rows * width),
+        name="returned_rows",
+    )(lists, low, high, ret_next, ret_prev)
+
+
+def unpack_kernel(part_rows, place_ref, *refs):
+    pieces, outs, full = refs[:5], refs[5:-1], refs[-1]
     place = place_ref[0]
     p = 0
     for piece in pieces:
@@ -590,21 +603,17 @@
         at += count
 
 
-def finish(place, pieces, lists, low, high, ret_next, ret_prev, row_counts):
+def unpack(place, pieces, row_counts):
     part_rows, width = pieces[0].shape
-    rows = low.shape[0] + high.shape[0]
-    held = [*pieces, lists, low, high, ret_next, ret_prev]
-    return pl.pallas_call(
-        functools.partial(finish_kernel, part_rows),
+    return pl.pallas_call(
+        functools.partial(unpack_kernel, part_rows),
         in_specs=[pl.BlockSpec(memory_space=pltpu.SMEM)]
-        + [pl.BlockSpec(memory_space=pltpu.VMEM)] * len(held),
-        out_shape=(jax.ShapeDtypeStruct((rows, width), F32),)
-        + tuple(jax.ShapeDtypeStruct((n, width), F32) for n in row_counts),
+        + [pl.BlockSpec(memory_space=pltpu.VMEM)] * len(pieces),
+        out_shape=tuple(jax.ShapeDtypeStruct((n, width), F32) for n in row_counts),
         scratch_shapes=[pltpu.VMEM((8 * part_rows, width), F32)],
         compiler_params=params(),
-        cost_estimate=cost(4 * rows * ret_next.size, 8 * rows * width),
-        name="finish",
-    )(place, *held)
+        name="unpack_sums",
+    )(place, *pieces)
 
 
 def traded(value, mask):
@@ -723,9 +732,12 @@
     high = spread(index_held, grad_a, send_weight, half, half, F32, grad_nodes)
     came, high = tied(came, high)
     pieces = [part] + came
-    pieces.append(traded(joined_parts(pieces), core))
+    came = traded(joined_parts(pieces), core)
+    grad_nodes = returned_rows(lists, low, high, ret_next, ret_prev)
+    came, grad_nodes = tied(came, grad_nodes)
+    pieces.append(came)
     counts = (edge_first.shape[0], width, node_first.shape[0], width) + (1,) * 8
-    grad_nodes, *sums = finish(place, pieces, lists, low, high, ret_next, ret_prev, counts)
+    sums = unpack(place, pieces, counts)
     vectors = [v.reshape(width) for v in sums[4:]]
     return (
         mixed,

time: 103 us -> 102 us (level)
  waiting for transfers between devices: 4.67 us -> 3.09 us
    ppermute x11, waiting for transfers between devices: 4.66 us -> 3.08 us  [traded(): return lax.ppermute(value, BOTH, [(i, i ^ mask) for i in range(count)])]
    pallas_call x1 -> x2, Pallas kernels: 2.26 us -> 2.96 us  [the longest x1 1.57 us: returned_rows(): pl.pallas_call(returned_kernel, out_shape=jax.ShapeDtypeStruct((rows, wid...]
  transfers between devices with their start and end apart: 15 -> 15, of which waited for: 3 -> 3; matrix products, arithmetic and copies ran while one was open for 0% -> 0% of each run, Pallas kernels for 33% -> 35%
where the time goes in v4:
time: 102 us; the launch traced here: 101 us
  Pallas kernels  75.1 us (74%)
  starting transfers between devices  21.7 us (21%)
  waiting for transfers between devices  3.09 us (3%)
  between operations  1.29 us (1%)
    pallas_call x1, Pallas kernels, main(): pl.pallas_call(functools.partial(main_kernel, degree, part_rows), grid_sp...  36.4 us
    pallas_call x3, Pallas kernels, spread(): pl.pallas_call(functools.partial(spread_kernel, first), grid=(degree // S...  16.6 us
    pallas_call x1, Pallas kernels, own_senders(): pl.pallas_call(own_kernel, grid=(degree // OWN,), in_specs=[pl.BlockSpec(...  12.4 us
    ppermute x11, starting transfers between devices, traded(): return lax.ppermute(value, BOTH, [(i, i ^ mask) for i in range(count)])  11.7 us
    ppermute x4, starting transfers between devices, passed_along(): return lax.ppermute(value, 'face', pairs)  10.1 us
    pallas_call x1, Pallas kernels, edge_grads(): pl.pallas_call(edge_kernel, grid=(degree // EDGE,), in_specs=[resident, r...  4.7 us
    ppermute x11, waiting for transfers between devices, traded(): return lax.ppermute(value, BOTH, [(i, i ^ mask) for i in range(count)])  3.08 us
  transfers between devices with their start and end apart: 15, of which 3 were waited for; matrix products, arithmetic and copies ran while one was open for 0% of the time, Pallas kernels for 35%

profile of v4, /device:TPU:0, one launch (start us, length us, event | category | flops | bytes accessed | tf_op | source)
XLA Modules:
  0.0 101.5 jit_solution(11671571774619024782)
XLA Ops:
  0.6 1.7 %pick_rows.1 = (bf16[256,256]{1,0:T(8,128)(2,1)S(1)}, bf16[256,256]{1,0:T(8,128)(2,1)S(1)}, bf16[1280,256]{1,0:T(8,128)(2,1)S(1)}, s32[12,1280]{1,0:T(8,128)S(1)}) custom-call(s32[2,256]{1,0:T(2,128)} %bitcast.14, bf16[1280,256]{1,0:T(8,128)(2,1)} %nodes_hbm.1, s32[12,1280]{1,0:T(8,128)} %bitcast.19), custom_call_target="tpu_custom_call" | custom-call | flops 335544320 | bytes 655360 | tf_op jit(solution)/shard_map/pick_rows/pallas_call | solution.py:111
  2.4 0.5 collective-permute-start
  2.9 5.1 %collective-permute-start.1 = (bf16[256,256]{1,0:T(8,128)(2,1)S(1)}, bf16[256,256]{1,0:T(8,128)(2,1)S(1)}, u32[]{:S(2)}, u32[]{:S(2)}) collective-permute-start(bf16[256,256]{1,0:T(8,128)(2,1)S(1)} %get-tuple-element.66), channel_id=1, source_target_pairs={{0,30},{2,0},{4,2},{6,4},{8,6},{10,8},{12,10},{14,12},{16,14},{18,... | collective-permute-start | bytes 393224 | tf_op jit(solution)/shard_map/ppermute | solution.py:631
  8.1 12.4 %own_senders.1.own_ref = bf16[12,1280,256]{2,1,0:T(8,128)(2,1)} custom-call(s32[12,1280]{1,0:T(8,128)S(1)} %get-tuple-element.63.index_ref, bf16[1280,256]{1,0:T(8,128)(2,1)S(1)} %get-tuple-element.64.nodes_ref), custom_call_target="tpu_custom_call" | custom-call | flops 10066329600 | bytes 7864320 | tf_op jit(solution)/shard_map/own_senders/pallas_call | solution.py:141
  20.8 36.4 %edges_and_nodes.1 = (bf16[1280,256]{1,0:T(8,128)(2,1)}, f32[1280,256]{1,0:T(8,128)S(1)}, bf16[12,1280,256]{2,1,0:T(8,128)(2,1)S(1)}, bf16[960,256]{1,0:T(8,128)(2,1)S(1)}, f32[960,256]{1,0:T(8,128)S(1)}) custom-call(s32[1]{0:T(128)} %bitcast.place_ref, bf16[12,1280,256]{2,1,0:T(8,128)(2,1)} %bitcast.18, bf16[12,1280,256]{2,1,0:T(8,128)(2,1)} %own_senders.1.own_ref, ...), custom_call_target="tpu_custom_call" | custom-call | flops 18119393280 | bytes 31457280 | tf_op jit(solution)/shard_map/edges_and_nodes/pallas_call | solution.py:420
  57.3 0.1 collective-permute-start.2
  57.4 1.8 %collective-permute-done.2.came_ref = bf16[960,256]{1,0:T(8,128)(2,1)S(1)} collective-permute-done((bf16[960,256]{1,0:T(8,128)(2,1)S(1)}, bf16[960,256]{1,0:T(8,128)(2,1)S(1)}, u32[]{:S(2)}, u32[]{:S(2)}) %collective-permute-start.2) | collective-permute-done | bytes 491552 | tf_op jit(solution)/shard_map/ppermute | solution.py:621
  59.2 0.1 add_and_split.1
  59.4 2.0 %collective-permute-start.4 = (bf16[240,256]{1,0:T(8,128)(2,1)S(1)}, bf16[240,256]{1,0:T(8,128)(2,1)S(1)}, u32[]{:S(2)}, u32[]{:S(2)}) collective-permute-start(bf16[240,256]{1,0:T(8,128)(2,1)S(1)} %get-tuple-element.75), channel_id=1, source_target_pairs={{0,1},{1,0},{2,3},{3,2},{4,5},{5,4},{6,7},{7,6},{8,9},{9,8},{10,11... | collective-permute-start | bytes 368648 | tf_op jit(solution)/shard_map/ppermute | solution.py:621
  61.3 1.5 %collective-permute-start.5 = (bf16[240,256]{1,0:T(8,128)(2,1)S(1)}, bf16[240,256]{1,0:T(8,128)(2,1)S(1)}, u32[]{:S(2)}, u32[]{:S(2)}) collective-permute-start(bf16[240,256]{1,0:T(8,128)(2,1)S(1)} %get-tuple-element.76), channel_id=1, source_target_pairs={{0,5},{1,4},{2,7},{3,6},{4,1},{5,0},{6,3},{7,2},{8,13},{9,12},{10,... | collective-permute-start | bytes 368648 | tf_op jit(solution)/shard_map/ppermute | solution.py:621
  62.9 4.8 %spread_rows.3 = bf16[512,256]{1,0:T(8,128)(2,1)S(1)} custom-call(s32[12,1280]{1,0:T(8,128)S(1)} %copy-done.9, bf16[12,1280,256]{2,1,0:T(8,128)(2,1)S(1)} %get-tuple-element.88.grad_ref, bf16[256,256]{1,0:T(8,128)(2,1)S(1)} %get-tuple-element.112.weight_ref), custom_call_target="tpu_custom_call" | custom-call | flops 4026531840 | bytes 7864320 | tf_op jit(solution)/shard_map/spread_rows/pallas_call | solution.py:473
  67.7 1.0 collective-permute-done.5.refs_2_
  68.8 0.1 collective-permute-start.6
  68.8 2.6 %collective-permute-start.7 = (bf16[240,256]{1,0:T(8,128)(2,1)S(1)}, bf16[240,256]{1,0:T(8,128)(2,1)S(1)}, u32[]{:S(2)}, u32[]{:S(2)}) collective-permute-start(bf16[240,256]{1,0:T(8,128)(2,1)S(1)} %sum_parts.2.own_ref), channel_id=1, source_target_pairs={{0,16},{1,17},{2,18},{3,19},{4,20},{5,21},{6,22},{7,23},{8,24},{9,... | collective-permute-start | bytes 368648 | tf_op jit(solution)/shard_map/ppermute | solution.py:621
  71.4 1.8 %collective-permute-start.8 = (bf16[240,256]{1,0:T(8,128)(2,1)S(1)}, bf16[240,256]{1,0:T(8,128)(2,1)S(1)}, u32[]{:S(2)}, u32[]{:S(2)}) collective-permute-start(bf16[240,256]{1,0:T(8,128)(2,1)S(1)} %sum_parts.2.own_ref), channel_id=1, source_target_pairs={{0,24},{1,25},{2,26},{3,27},{4,28},{5,29},{6,30},{7,31},{8,16},{9,... | collective-permute-start | bytes 368648 | tf_op jit(solution)/shard_map/ppermute | solution.py:621
  73.3 4.4 %collective-permute-start.9 = (bf16[256,256]{1,0:T(8,128)(2,1)S(1)}, bf16[256,256]{1,0:T(8,128)(2,1)S(1)}, u32[]{:S(2)}, u32[]{:S(2)}) collective-permute-start(bf16[256,256]{1,0:T(8,128)(2,1)S(1)} %get-tuple-element.114), channel_id=1, source_target_pairs={{0,30},{2,0},{4,2},{6,4},{8,6},{10,8},{12,10},{14,12},{16,14},{18,... | collective-permute-start | bytes 393224 | tf_op jit(solution)/shard_map/ppermute | solution.py:631
  77.7 5.9 %spread_rows.4.low_ref = f32[640,256]{1,0:T(8,128)S(1)} custom-call(s32[12,1280]{1,0:T(8,128)S(1)} %copy-done.9, bf16[12,1280,256]{2,1,0:T(8,128)(2,1)S(1)} %get-tuple-element.88.grad_ref, bf16[256,256]{1,0:T(8,128)(2,1)S(1)} %get-tuple-element.112.weight_ref, f32[1280,256]{1,0:T(8,128)S(1)} %get-tuple-element.82.rest_0_), custom_call_target="tpu_custom_call" | custom-call | flops 5033164800 | bytes 7864320 | tf_op jit(solution)/shard_map/spread_rows/pallas_call | solution.py:473
  83.6 4.7 %edge_grads.1 = bf16[12,1280,256]{2,1,0:T(8,128)(2,1)} custom-call(bf16[12,1280,256]{2,1,0:T(8,128)(2,1)S(1)} %get-tuple-element.88.grad_ref, bf16[256,256]{1,0:T(8,128)(2,1)S(1)} %get-tuple-element.111.weight_ref), custom_call_target="tpu_custom_call" | custom-call | flops 2013265920 | bytes 15728640 | tf_op jit(solution)/shard_map/edge_grads/pallas_call | solution.py:500
  88.5 1.8 %collective-permute-start.12 = (bf16[240,256]{1,0:T(8,128)(2,1)S(1)}, bf16[240,256]{1,0:T(8,128)(2,1)S(1)}, u32[]{:S(2)}, u32[]{:S(2)}) collective-permute-start(bf16[240,256]{1,0:T(8,128)(2,1)S(1)} %sum_parts.3.refs_0_), channel_id=1, source_target_pairs={{0,1},{1,0},{2,3},{3,2},{4,5},{5,4},{6,7},{7,6},{8,9},{9,8},{10,11... | collective-permute-start | bytes 368648 | tf_op jit(solution)/shard_map/ppermute | solution.py:621
  90.3 1.7 %collective-permute-start.13 = (bf16[240,256]{1,0:T(8,128)(2,1)S(1)}, bf16[240,256]{1,0:T(8,128)(2,1)S(1)}, u32[]{:S(2)}, u32[]{:S(2)}) collective-permute-start(bf16[240,256]{1,0:T(8,128)(2,1)S(1)} %sum_parts.3.refs_0_), channel_id=1, source_target_pairs={{0,5},{1,4},{2,7},{3,6},{4,1},{5,0},{6,3},{7,2},{8,13},{9,12},{10,... | collective-permute-start | bytes 368648 | tf_op jit(solution)/shard_map/ppermute | solution.py:621
  92.0 5.9 %spread_rows.5.high_ref = f32[640,256]{1,0:T(8,128)S(1)} custom-call(s32[12,1280]{1,0:T(8,128)S(1)} %copy-done.9, bf16[12,1280,256]{2,1,0:T(8,128)(2,1)S(1)} %get-tuple-element.88.grad_ref, bf16[256,256]{1,0:T(8,128)(2,1)S(1)} %get-tuple-element.112.weight_ref, f32[1280,256]{1,0:T(8,128)S(1)} %get-tuple-element.82.rest_0_), custom_call_target="tpu_custom_call" | custom-call | flops 5033164800 | bytes 7864320 | tf_op jit(solution)/shard_map/spread_rows/pallas_call | solution.py:473
  98.1 1.6 %returned_rows.1 = f32[1280,256]{1,0:T(8,128)} custom-call(s32[2,256]{1,0:T(2,128)S(1)} %bitcast.15, f32[640,256]{1,0:T(8,128)S(1)} %spread_rows.4.low_ref, f32[640,256]{1,0:T(8,128)S(1)} %spread_rows.5.high_ref, bf16[256,256]{1,0:T(8,128)(2,1)S(1)} %collective-permute-done.9.next_ref, bf16[256,256]{1,0:T(8,128)(2,1)S(1)} %collective-permute-done.10.prev_ref), custom_call_target="tpu_custom_call" | custom-call | flops 335544320 | bytes 2621440 | tf_op jit(solution)/shard_map/returned_rows/pallas_call | solution.py:581
  99.6 0.3 collective-permute-done.14.refs_4_
  99.9 1.4 %unpack_sums.1 = (f32[768,256]{1,0:T(8,128)}, f32[256,256]{1,0:T(8,128)}, f32[512,256]{1,0:T(8,128)}, f32[256,256]{1,0:T(8,128)}, f32[1,256]{1,0:T(1,128)}, /*in...) custom-call(s32[1]{0:T(128)} %bitcast.place_ref, ...), custom_call_target="tpu_custom_call" | custom-call | tf_op jit(solution)/shard_map/unpack_sums/pallas_call | solution.py:608
  (68 shorter events, 0.7 us)
Async XLA Ops:
  2.3 18.2 %copy-start.7 = (bf16[1280,256]{1,0:T(8,128)(2,1)}, bf16[1280,256]{1,0:T(8,128)(2,1)S(1)}, u32[]{:S(2)}) copy-start(bf16[1280,256]{1,0:T(8,128)(2,1)S(1)} %get-tuple-element.64.nodes_ref) | copy-start | bytes 1966084
  2.3 18.1 %copy-start.8 = (s32[12,1280]{1,0:T(8,128)}, s32[12,1280]{1,0:T(8,128)S(1)}, u32[]{:S(2)}) copy-start(s32[12,1280]{1,0:T(8,128)S(1)} %get-tuple-element.63.index_ref) | copy-start | bytes 184324
  2.4 18.3 %collective-permute-start = (bf16[256,256]{1,0:T(8,128)(2,1)S(1)}, bf16[256,256]{1,0:T(8,128)(2,1)S(1)}, u32[]{:S(2)}, u32[]{:S(2)}) collective-permute-start(bf16[256,256]{1,0:T(8,128)(2,1)S(1)} %get-tuple-element.65), channel_id=1, source_target_pairs={{0,2},{2,4},{4,6},{6,8},{8,10},{10,12},{12,14},{14,16},{16,18},{18... | collective-permute-start | bytes 393224 | tf_op jit(solution)/shard_map/ppermute | solution.py:631
  2.9 17.9 %collective-permute-start.1 = (bf16[256,256]{1,0:T(8,128)(2,1)S(1)}, bf16[256,256]{1,0:T(8,128)(2,1)S(1)}, u32[]{:S(2)}, u32[]{:S(2)}) collective-permute-start(bf16[256,256]{1,0:T(8,128)(2,1)S(1)} %get-tuple-element.66), channel_id=1, source_target_pairs={{0,30},{2,0},{4,2},{6,4},{8,6},{10,8},{12,10},{14,12},{16,14},{18,... | collective-permute-start | bytes 393224 | tf_op jit(solution)/shard_map/ppermute | solution.py:631
  8.0 12.8 %copy-start = (bf16[768,256]{1,0:T(8,128)(2,1)S(1)}, bf16[768,256]{1,0:T(8,128)(2,1)}, u32[]{:S(2)}) copy-start(bf16[768,256]{1,0:T(8,128)(2,1)} %w_first_ref.1) | copy-start | bytes 1179652
  8.0 12.8 %copy-start.2 = (bf16[1280,256]{1,0:T(8,128)(2,1)S(1)}, bf16[1280,256]{1,0:T(8,128)(2,1)}, u32[]{:S(2)}) copy-start(bf16[1280,256]{1,0:T(8,128)(2,1)} %cot_ref.1) | copy-start | bytes 1966084
  8.0 12.8 %copy-start.3 = (bf16[512,256]{1,0:T(8,128)(2,1)S(1)}, bf16[512,256]{1,0:T(8,128)(2,1)}, u32[]{:S(2)}) copy-start(bf16[512,256]{1,0:T(8,128)(2,1)} %n_first_ref.1) | copy-start | bytes 786436
  8.0 12.8 %copy-start.4 = (bf16[256,256]{1,0:T(8,128)(2,1)S(1)}, bf16[256,256]{1,0:T(8,128)(2,1)}, u32[]{:S(2)}) copy-start(bf16[256,256]{1,0:T(8,128)(2,1)} %w_second_ref.1) | copy-start | bytes 393220
  8.0 12.8 %copy-start.5 = (bf16[256,256]{1,0:T(8,128)(2,1)S(1)}, bf16[256,256]{1,0:T(8,128)(2,1)}, u32[]{:S(2)}) copy-start(bf16[256,256]{1,0:T(8,128)(2,1)} %n_second_ref.1) | copy-start | bytes 393220
  8.1 12.8 %copy-start.6 = (s32[1280,12]{0,1:T(8,128)S(1)}, s32[1280,12]{0,1:T(8,128)}, u32[]{:S(2)}) copy-start(s32[1280,12]{0,1:T(8,128)} %param.21) | copy-start | bytes 184324
  20.8 42.0 %copy-start.9 = (s32[12,1280]{1,0:T(8,128)S(1)}, s32[12,1280]{1,0:T(8,128)}, u32[]{:S(2)}) copy-start(s32[12,1280]{1,0:T(8,128)} %copy-done.8) | copy-start | bytes 184324
  57.3 1.9 %collective-permute-start.2 = (bf16[960,256]{1,0:T(8,128)(2,1)S(1)}, bf16[960,256]{1,0:T(8,128)(2,1)S(1)}, u32[]{:S(2)}, u32[]{:S(2)}) collective-permute-start(bf16[960,256]{1,0:T(8,128)(2,1)S(1)} %get-tuple-element.70), channel_id=1, source_target_pairs={{0,2},{1,3},{2,0},{3,1},{4,6},{5,7},{6,4},{7,5},{8,10},{9,11},{10,... | collective-permute-start | bytes 1474568 | tf_op jit(solution)/shard_map/ppermute | solution.py:621
  59.3 8.4 %collective-permute-start.3 = (bf16[240,256]{1,0:T(8,128)(2,1)S(1)}, bf16[240,256]{1,0:T(8,128)(2,1)S(1)}, u32[]{:S(2)}, u32[]{:S(2)}) collective-permute-start(bf16[240,256]{1,0:T(8,128)(2,1)S(1)} %get-tuple-element.74), channel_id=1, source_target_pairs={{0,4},{1,5},{2,6},{3,7},{4,0},{5,1},{6,2},{7,3},{8,12},{9,13},{10,... | collective-permute-start | bytes 368648 | tf_op jit(solution)/shard_map/ppermute | solution.py:621
  59.4 8.3 %collective-permute-start.4 = (bf16[240,256]{1,0:T(8,128)(2,1)S(1)}, bf16[240,256]{1,0:T(8,128)(2,1)S(1)}, u32[]{:S(2)}, u32[]{:S(2)}) collective-permute-start(bf16[240,256]{1,0:T(8,128)(2,1)S(1)} %get-tuple-element.75), channel_id=1, source_target_pairs={{0,1},{1,0},{2,3},{3,2},{4,5},{5,4},{6,7},{7,6},{8,9},{9,8},{10,11... | collective-permute-start | bytes 368648 | tf_op jit(solution)/shard_map/ppermute | solution.py:621
  61.3 7.4 %collective-permute-start.5 = (bf16[240,256]{1,0:T(8,128)(2,1)S(1)}, bf16[240,256]{1,0:T(8,128)(2,1)S(1)}, u32[]{:S(2)}, u32[]{:S(2)}) collective-permute-start(bf16[240,256]{1,0:T(8,128)(2,1)S(1)} %get-tuple-element.76), channel_id=1, source_target_pairs={{0,5},{1,4},{2,7},{3,6},{4,1},{5,0},{6,3},{7,2},{8,13},{9,12},{10,... | collective-permute-start | bytes 368648 | tf_op jit(solution)/shard_map/ppermute | solution.py:621
  68.8 19.6 %collective-permute-start.6 = (bf16[240,256]{1,0:T(8,128)(2,1)S(1)}, bf16[240,256]{1,0:T(8,128)(2,1)S(1)}, u32[]{:S(2)}, u32[]{:S(2)}) collective-permute-start(bf16[240,256]{1,0:T(8,128)(2,1)S(1)} %sum_parts.2.own_ref), channel_id=1, source_target_pairs={{0,8},{1,9},{2,10},{3,11},{4,12},{5,13},{6,14},{7,15},{8,0},{9,1},... | collective-permute-start | bytes 368648 | tf_op jit(solution)/shard_map/ppermute | solution.py:621
  68.8 19.5 %collective-permute-start.7 = (bf16[240,256]{1,0:T(8,128)(2,1)S(1)}, bf16[240,256]{1,0:T(8,128)(2,1)S(1)}, u32[]{:S(2)}, u32[]{:S(2)}) collective-permute-start(bf16[240,256]{1,0:T(8,128)(2,1)S(1)} %sum_parts.2.own_ref), channel_id=1, source_target_pairs={{0,16},{1,17},{2,18},{3,19},{4,20},{5,21},{6,22},{7,23},{8,24},{9,... | collective-permute-start | bytes 368648 | tf_op jit(solution)/shard_map/ppermute | solution.py:621
  71.4 16.9 %collective-permute-start.8 = (bf16[240,256]{1,0:T(8,128)(2,1)S(1)}, bf16[240,256]{1,0:T(8,128)(2,1)S(1)}, u32[]{:S(2)}, u32[]{:S(2)}) collective-permute-start(bf16[240,256]{1,0:T(8,128)(2,1)S(1)} %sum_parts.2.own_ref), channel_id=1, source_target_pairs={{0,24},{1,25},{2,26},{3,27},{4,28},{5,29},{6,30},{7,31},{8,16},{9,... | collective-permute-start | bytes 368648 | tf_op jit(solution)/shard_map/ppermute | solution.py:621
  73.2 18.8 %collective-permute-start.10 = (bf16[256,256]{1,0:T(8,128)(2,1)S(1)}, bf16[256,256]{1,0:T(8,128)(2,1)S(1)}, u32[]{:S(2)}, u32[]{:S(2)}) collective-permute-start(bf16[256,256]{1,0:T(8,128)(2,1)S(1)} %get-tuple-element.113), channel_id=1, source_target_pairs={{0,2},{2,4},{4,6},{6,8},{8,10},{10,12},{12,14},{14,16},{16,18},{18... | collective-permute-start | bytes 393224 | tf_op jit(solution)/shard_map/ppermute | solution.py:631
  73.3 18.7 %collective-permute-start.9 = (bf16[256,256]{1,0:T(8,128)(2,1)S(1)}, bf16[256,256]{1,0:T(8,128)(2,1)S(1)}, u32[]{:S(2)}, u32[]{:S(2)}) collective-permute-start(bf16[256,256]{1,0:T(8,128)(2,1)S(1)} %get-tuple-element.114), channel_id=1, source_target_pairs={{0,30},{2,0},{4,2},{6,4},{8,6},{10,8},{12,10},{14,12},{16,14},{18,... | collective-permute-start | bytes 393224 | tf_op jit(solution)/shard_map/ppermute | solution.py:631
  88.4 9.5 %collective-permute-start.11 = (bf16[240,256]{1,0:T(8,128)(2,1)S(1)}, bf16[240,256]{1,0:T(8,128)(2,1)S(1)}, u32[]{:S(2)}, u32[]{:S(2)}) collective-permute-start(bf16[240,256]{1,0:T(8,128)(2,1)S(1)} %sum_parts.3.refs_0_), channel_id=1, source_target_pairs={{0,4},{1,5},{2,6},{3,7},{4,0},{5,1},{6,2},{7,3},{8,12},{9,13},{10,... | collective-permute-start | bytes 368648 | tf_op jit(solution)/shard_map/ppermute | solution.py:621
  88.5 9.4 %collective-permute-start.12 = (bf16[240,256]{1,0:T(8,128)(2,1)S(1)}, bf16[240,256]{1,0:T(8,128)(2,1)S(1)}, u32[]{:S(2)}, u32[]{:S(2)}) collective-permute-start(bf16[240,256]{1,0:T(8,128)(2,1)S(1)} %sum_parts.3.refs_0_), channel_id=1, source_target_pairs={{0,1},{1,0},{2,3},{3,2},{4,5},{5,4},{6,7},{7,6},{8,9},{9,8},{10,11... | collective-permute-start | bytes 368648 | tf_op jit(solution)/shard_map/ppermute | solution.py:621
  90.3 7.6 %collective-permute-start.13 = (bf16[240,256]{1,0:T(8,128)(2,1)S(1)}, bf16[240,256]{1,0:T(8,128)(2,1)S(1)}, u32[]{:S(2)}, u32[]{:S(2)}) collective-permute-start(bf16[240,256]{1,0:T(8,128)(2,1)S(1)} %sum_parts.3.refs_0_), channel_id=1, source_target_pairs={{0,5},{1,4},{2,7},{3,6},{4,1},{5,0},{6,3},{7,2},{8,13},{9,12},{10,... | collective-permute-start | bytes 368648 | tf_op jit(solution)/shard_map/ppermute | solution.py:621
  98.0 1.9 %collective-permute-start.14 = (bf16[960,256]{1,0:T(8,128)(2,1)S(1)}, bf16[960,256]{1,0:T(8,128)(2,1)S(1)}, u32[]{:S(2)}, u32[]{:S(2)}) collective-permute-start(bf16[960,256]{1,0:T(8,128)(2,1)S(1)} %join_parts.1), channel_id=1, source_target_pairs={{0,2},{1,3},{2,0},{3,1},{4,6},{5,7},{6,4},{7,5},{8,10},{9,11},{10,... | collective-permute-start | bytes 1474568 | tf_op jit(solution)/shard_map/ppermute | solution.py:621
  (9 other events, 110.6 us)

commit v5 on v4

--- a/solution.py
+++ b/solution.py
@@ -706,6 +706,8 @@
     plane = (inner, outer, inner ^ outer)
 
     came = traded(away, core)
+    grad_edges = edge_grads(grad_a, edge_weight)
+    came, grad_edges = tied(came, grad_edges)
     part, *away = add_and_split(keep, came)
     came = [traded(a, mask) for a, mask in zip(away, plane)]
     grad_a, part = tied(grad_a, part)
@@ -724,8 +726,7 @@
         if not doubling:
             grad_a, part = tied(grad_a, part)
             low = spread(index_held, grad_a, send_weight, 0, half, F32, grad_nodes)
-            grad_edges = edge_grads(grad_a, edge_weight)
-            came, low, grad_edges = tied(came, low, grad_edges)
+            came, low = tied(came, low)
         part = sum_parts(part, came)
     came = [traded(part, mask) for mask in plane]
     grad_a, part, ret_next, ret_prev = tied(grad_a, part, ret_next, ret_prev)

time: 102 us -> 100 us (0.980)
  waiting for transfers between devices: 3.09 us -> 1.6 us
    ppermute x11, waiting for transfers between devices: 3.08 us -> 1.59 us  [traded(): return lax.ppermute(value, BOTH, [(i, i ^ mask) for i in range(count)])]
  transfers between devices with their start and end apart: 15 -> 15, of which waited for: 3 -> 2; matrix products, arithmetic and copies ran while one was open for 0% -> 0% of each run, Pallas kernels for 35% -> 35%
where the time goes in v5:
time: 100 us
  Pallas kernels  75.1 us (75%)
  starting transfers between devices  21.7 us (22%)
  waiting for transfers between devices  1.6 us (2%)
  between operations  1.3 us (1%)
    pallas_call x1, Pallas kernels, main(): pl.pallas_call(functools.partial(main_kernel, degree, part_rows), grid_sp...  36.4 us
    pallas_call x3, Pallas kernels, spread(): pl.pallas_call(functools.partial(spread_kernel, first), grid=(degree // S...  16.6 us
    pallas_call x1, Pallas kernels, own_senders(): pl.pallas_call(own_kernel, grid=(degree // OWN,), in_specs=[pl.BlockSpec(...  12.4 us
    ppermute x11, starting transfers between devices, traded(): return lax.ppermute(value, BOTH, [(i, i ^ mask) for i in range(count)])  11.7 us
    ppermute x4, starting transfers between devices, passed_along(): return lax.ppermute(value, 'face', pairs)  10.1 us
    pallas_call x1, Pallas kernels, edge_grads(): pl.pallas_call(edge_kernel, grid=(degree // EDGE,), in_specs=[resident, r...  4.7 us
  transfers between devices with their start and end apart: 15, of which 2 were waited for; matrix products, arithmetic and copies ran while one was open for 0% of the time, Pallas kernels for 35%

profile of v5, /device:TPU:0, one launch (start us, length us, event | category | flops | bytes accessed | tf_op | source)
XLA Modules:
  0.0 100.0 jit_solution(2607387872665685641)
XLA Ops:
  0.6 1.7 %pick_rows.1 = (bf16[256,256]{1,0:T(8,128)(2,1)S(1)}, bf16[256,256]{1,0:T(8,128)(2,1)S(1)}, bf16[1280,256]{1,0:T(8,128)(2,1)S(1)}, s32[12,1280]{1,0:T(8,128)S(1)}) custom-call(s32[2,256]{1,0:T(2,128)} %bitcast.14, bf16[1280,256]{1,0:T(8,128)(2,1)} %nodes_hbm.1, s32[12,1280]{1,0:T(8,128)} %bitcast.19), custom_call_target="tpu_custom_call" | custom-call | flops 335544320 | bytes 655360 | tf_op jit(solution)/shard_map/pick_rows/pallas_call | solution.py:111
  2.4 0.5 collective-permute-start
  2.9 5.1 %collective-permute-start.1 = (bf16[256,256]{1,0:T(8,128)(2,1)S(1)}, bf16[256,256]{1,0:T(8,128)(2,1)S(1)}, u32[]{:S(2)}, u32[]{:S(2)}) collective-permute-start(bf16[256,256]{1,0:T(8,128)(2,1)S(1)} %get-tuple-element.67), channel_id=1, source_target_pairs={{0,30},{2,0},{4,2},{6,4},{8,6},{10,8},{12,10},{14,12},{16,14},{18,... | collective-permute-start | bytes 393224 | tf_op jit(solution)/shard_map/ppermute | solution.py:631
  8.1 12.4 %own_senders.1.own_ref = bf16[12,1280,256]{2,1,0:T(8,128)(2,1)} custom-call(s32[12,1280]{1,0:T(8,128)S(1)} %get-tuple-element.64.index_ref, bf16[1280,256]{1,0:T(8,128)(2,1)S(1)} %get-tuple-element.65.nodes_ref), custom_call_target="tpu_custom_call" | custom-call | flops 10066329600 | bytes 7864320 | tf_op jit(solution)/shard_map/own_senders/pallas_call | solution.py:141
  20.8 36.4 %edges_and_nodes.1 = (bf16[1280,256]{1,0:T(8,128)(2,1)}, f32[1280,256]{1,0:T(8,128)S(1)}, bf16[12,1280,256]{2,1,0:T(8,128)(2,1)S(1)}, bf16[960,256]{1,0:T(8,128)(2,1)S(1)}, f32[960,256]{1,0:T(8,128)S(1)}) custom-call(s32[1]{0:T(128)} %bitcast.place_ref, bf16[12,1280,256]{2,1,0:T(8,128)(2,1)} %bitcast.18, bf16[12,1280,256]{2,1,0:T(8,128)(2,1)} %own_senders.1.own_ref, ...), custom_call_target="tpu_custom_call" | custom-call | flops 18119393280 | bytes 31457280 | tf_op jit(solution)/shard_map/edges_and_nodes/pallas_call | solution.py:420
  57.3 0.1 collective-permute-start.2
  57.4 4.7 %edge_grads.1 = bf16[12,1280,256]{2,1,0:T(8,128)(2,1)} custom-call(bf16[12,1280,256]{2,1,0:T(8,128)(2,1)S(1)} %get-tuple-element.90.grad_ref, bf16[256,256]{1,0:T(8,128)(2,1)S(1)} %get-tuple-element.114.weight_ref), custom_call_target="tpu_custom_call" | custom-call | flops 2013265920 | bytes 15728640 | tf_op jit(solution)/shard_map/edge_grads/pallas_call | solution.py:500
  62.1 0.1 add_and_split.1
  62.2 0.1 collective-permute-start.3
  62.3 1.9 %collective-permute-start.4 = (bf16[240,256]{1,0:T(8,128)(2,1)S(1)}, bf16[240,256]{1,0:T(8,128)(2,1)S(1)}, u32[]{:S(2)}, u32[]{:S(2)}) collective-permute-start(bf16[240,256]{1,0:T(8,128)(2,1)S(1)} %get-tuple-element.77), channel_id=1, source_target_pairs={{0,1},{1,0},{2,3},{3,2},{4,5},{5,4},{6,7},{7,6},{8,9},{9,8},{10,11... | collective-permute-start | bytes 368648 | tf_op jit(solution)/shard_map/ppermute | solution.py:621
  64.2 1.5 %collective-permute-start.5 = (bf16[240,256]{1,0:T(8,128)(2,1)S(1)}, bf16[240,256]{1,0:T(8,128)(2,1)S(1)}, u32[]{:S(2)}, u32[]{:S(2)}) collective-permute-start(bf16[240,256]{1,0:T(8,128)(2,1)S(1)} %get-tuple-element.78), channel_id=1, source_target_pairs={{0,5},{1,4},{2,7},{3,6},{4,1},{5,0},{6,3},{7,2},{8,13},{9,12},{10,... | collective-permute-start | bytes 368648 | tf_op jit(solution)/shard_map/ppermute | solution.py:621
  65.8 4.8 %spread_rows.3 = bf16[512,256]{1,0:T(8,128)(2,1)S(1)} custom-call(s32[12,1280]{1,0:T(8,128)S(1)} %copy-done.9, bf16[12,1280,256]{2,1,0:T(8,128)(2,1)S(1)} %get-tuple-element.90.grad_ref, bf16[256,256]{1,0:T(8,128)(2,1)S(1)} %get-tuple-element.113.weight_ref), custom_call_target="tpu_custom_call" | custom-call | flops 4026531840 | bytes 7864320 | tf_op jit(solution)/shard_map/spread_rows/pallas_call | solution.py:473
  70.6 1.3 %collective-permute-done.5.refs_2_ = bf16[240,256]{1,0:T(8,128)(2,1)S(1)} collective-permute-done((bf16[240,256]{1,0:T(8,128)(2,1)S(1)}, bf16[240,256]{1,0:T(8,128)(2,1)S(1)}, u32[]{:S(2)}, u32[]{:S(2)}) %collective-permute-start.5) | collective-permute-done | bytes 122912 | tf_op jit(solution)/shard_map/ppermute | solution.py:621
  72.0 0.1 collective-permute-start.6
  72.1 2.6 %collective-permute-start.7 = (bf16[240,256]{1,0:T(8,128)(2,1)S(1)}, bf16[240,256]{1,0:T(8,128)(2,1)S(1)}, u32[]{:S(2)}, u32[]{:S(2)}) collective-permute-start(bf16[240,256]{1,0:T(8,128)(2,1)S(1)} %sum_parts.2.own_ref), channel_id=1, source_target_pairs={{0,16},{1,17},{2,18},{3,19},{4,20},{5,21},{6,22},{7,23},{8,24},{9,... | collective-permute-start | bytes 368648 | tf_op jit(solution)/shard_map/ppermute | solution.py:621
  74.7 1.8 %collective-permute-start.8 = (bf16[240,256]{1,0:T(8,128)(2,1)S(1)}, bf16[240,256]{1,0:T(8,128)(2,1)S(1)}, u32[]{:S(2)}, u32[]{:S(2)}) collective-permute-start(bf16[240,256]{1,0:T(8,128)(2,1)S(1)} %sum_parts.2.own_ref), channel_id=1, source_target_pairs={{0,24},{1,25},{2,26},{3,27},{4,28},{5,29},{6,30},{7,31},{8,16},{9,... | collective-permute-start | bytes 368648 | tf_op jit(solution)/shard_map/ppermute | solution.py:621
  76.5 4.4 %collective-permute-start.9 = (bf16[256,256]{1,0:T(8,128)(2,1)S(1)}, bf16[256,256]{1,0:T(8,128)(2,1)S(1)}, u32[]{:S(2)}, u32[]{:S(2)}) collective-permute-start(bf16[256,256]{1,0:T(8,128)(2,1)S(1)} %get-tuple-element.116), channel_id=1, source_target_pairs={{0,30},{2,0},{4,2},{6,4},{8,6},{10,8},{12,10},{14,12},{16,14},{18,... | collective-permute-start | bytes 393224 | tf_op jit(solution)/shard_map/ppermute | solution.py:631
  80.9 5.9 %spread_rows.4.low_ref = f32[640,256]{1,0:T(8,128)S(1)} custom-call(s32[12,1280]{1,0:T(8,128)S(1)} %copy-done.9, bf16[12,1280,256]{2,1,0:T(8,128)(2,1)S(1)} %get-tuple-element.90.grad_ref, bf16[256,256]{1,0:T(8,128)(2,1)S(1)} %get-tuple-element.113.weight_ref, f32[1280,256]{1,0:T(8,128)S(1)} %get-tuple-element.84.rest_0_), custom_call_target="tpu_custom_call" | custom-call | flops 5033164800 | bytes 7864320 | tf_op jit(solution)/shard_map/spread_rows/pallas_call | solution.py:473
  87.1 1.8 %collective-permute-start.12 = (bf16[240,256]{1,0:T(8,128)(2,1)S(1)}, bf16[240,256]{1,0:T(8,128)(2,1)S(1)}, u32[]{:S(2)}, u32[]{:S(2)}) collective-permute-start(bf16[240,256]{1,0:T(8,128)(2,1)S(1)} %sum_parts.3.refs_0_), channel_id=1, source_target_pairs={{0,1},{1,0},{2,3},{3,2},{4,5},{5,4},{6,7},{7,6},{8,9},{9,8},{10,11... | collective-permute-start | bytes 368648 | tf_op jit(solution)/shard_map/ppermute | solution.py:621
  88.9 1.7 %collective-permute-start.13 = (bf16[240,256]{1,0:T(8,128)(2,1)S(1)}, bf16[240,256]{1,0:T(8,128)(2,1)S(1)}, u32[]{:S(2)}, u32[]{:S(2)}) collective-permute-start(bf16[240,256]{1,0:T(8,128)(2,1)S(1)} %sum_parts.3.refs_0_), channel_id=1, source_target_pairs={{0,5},{1,4},{2,7},{3,6},{4,1},{5,0},{6,3},{7,2},{8,13},{9,12},{10,... | collective-permute-start | bytes 368648 | tf_op jit(solution)/shard_map/ppermute | solution.py:621
  90.5 5.9 %spread_rows.5.high_ref = f32[640,256]{1,0:T(8,128)S(1)} custom-call(s32[12,1280]{1,0:T(8,128)S(1)} %copy-done.9, bf16[12,1280,256]{2,1,0:T(8,128)(2,1)S(1)} %get-tuple-element.90.grad_ref, bf16[256,256]{1,0:T(8,128)(2,1)S(1)} %get-tuple-element.113.weight_ref, f32[1280,256]{1,0:T(8,128)S(1)} %get-tuple-element.84.rest_0_), custom_call_target="tpu_custom_call" | custom-call | flops 5033164800 | bytes 7864320 | tf_op jit(solution)/shard_map/spread_rows/pallas_call | solution.py:473
  96.6 1.6 %returned_rows.1 = f32[1280,256]{1,0:T(8,128)} custom-call(s32[2,256]{1,0:T(2,128)S(1)} %bitcast.15, f32[640,256]{1,0:T(8,128)S(1)} %spread_rows.4.low_ref, f32[640,256]{1,0:T(8,128)S(1)} %spread_rows.5.high_ref, bf16[256,256]{1,0:T(8,128)(2,1)S(1)} %collective-permute-done.9.next_ref, bf16[256,256]{1,0:T(8,128)(2,1)S(1)} %collective-permute-done.10.prev_ref), custom_call_target="tpu_custom_call" | custom-call | flops 335544320 | bytes 2621440 | tf_op jit(solution)/shard_map/returned_rows/pallas_call | solution.py:581
  98.2 0.3 collective-permute-done.14.refs_4_
  98.5 1.4 %unpack_sums.1 = (f32[768,256]{1,0:T(8,128)}, f32[256,256]{1,0:T(8,128)}, f32[512,256]{1,0:T(8,128)}, f32[256,256]{1,0:T(8,128)}, f32[1,256]{1,0:T(1,128)}, /*in...) custom-call(s32[1]{0:T(128)} %bitcast.place_ref, ...), custom_call_target="tpu_custom_call" | custom-call | tf_op jit(solution)/shard_map/unpack_sums/pallas_call | solution.py:608
  (68 shorter events, 0.6 us)
Async XLA Ops:
  2.3 18.2 %copy-start.7 = (bf16[1280,256]{1,0:T(8,128)(2,1)}, bf16[1280,256]{1,0:T(8,128)(2,1)S(1)}, u32[]{:S(2)}) copy-start(bf16[1280,256]{1,0:T(8,128)(2,1)S(1)} %get-tuple-element.65.nodes_ref) | copy-start | bytes 1966084
  2.3 18.1 %copy-start.8 = (s32[12,1280]{1,0:T(8,128)}, s32[12,1280]{1,0:T(8,128)S(1)}, u32[]{:S(2)}) copy-start(s32[12,1280]{1,0:T(8,128)S(1)} %get-tuple-element.64.index_ref) | copy-start | bytes 184324
  2.4 18.3 %collective-permute-start = (bf16[256,256]{1,0:T(8,128)(2,1)S(1)}, bf16[256,256]{1,0:T(8,128)(2,1)S(1)}, u32[]{:S(2)}, u32[]{:S(2)}) collective-permute-start(bf16[256,256]{1,0:T(8,128)(2,1)S(1)} %get-tuple-element.66), channel_id=1, source_target_pairs={{0,2},{2,4},{4,6},{6,8},{8,10},{10,12},{12,14},{14,16},{16,18},{18... | collective-permute-start | bytes 393224 | tf_op jit(solution)/shard_map/ppermute | solution.py:631
  2.9 17.9 %collective-permute-start.1 = (bf16[256,256]{1,0:T(8,128)(2,1)S(1)}, bf16[256,256]{1,0:T(8,128)(2,1)S(1)}, u32[]{:S(2)}, u32[]{:S(2)}) collective-permute-start(bf16[256,256]{1,0:T(8,128)(2,1)S(1)} %get-tuple-element.67), channel_id=1, source_target_pairs={{0,30},{2,0},{4,2},{6,4},{8,6},{10,8},{12,10},{14,12},{16,14},{18,... | collective-permute-start | bytes 393224 | tf_op jit(solution)/shard_map/ppermute | solution.py:631
  8.0 12.7 %copy-start.17 = (bf16[256]{0:T(256)(128)(2,1)S(1)}, bf16[256]{0:T(256)(128)(2,1)}, u32[]{:S(2)}) copy-start(bf16[256]{0:T(256)(128)(2,1)} %param.34) | copy-start | bytes 1540
  8.0 12.8 %copy-start = (bf16[768,256]{1,0:T(8,128)(2,1)S(1)}, bf16[768,256]{1,0:T(8,128)(2,1)}, u32[]{:S(2)}) copy-start(bf16[768,256]{1,0:T(8,128)(2,1)} %w_first_ref.1) | copy-start | bytes 1179652
  8.0 12.8 %copy-start.2 = (bf16[1280,256]{1,0:T(8,128)(2,1)S(1)}, bf16[1280,256]{1,0:T(8,128)(2,1)}, u32[]{:S(2)}) copy-start(bf16[1280,256]{1,0:T(8,128)(2,1)} %cot_ref.1) | copy-start | bytes 1966084
  8.0 12.8 %copy-start.3 = (bf16[512,256]{1,0:T(8,128)(2,1)S(1)}, bf16[512,256]{1,0:T(8,128)(2,1)}, u32[]{:S(2)}) copy-start(bf16[512,256]{1,0:T(8,128)(2,1)} %n_first_ref.1) | copy-start | bytes 786436
  8.0 12.8 %copy-start.4 = (bf16[256,256]{1,0:T(8,128)(2,1)S(1)}, bf16[256,256]{1,0:T(8,128)(2,1)}, u32[]{:S(2)}) copy-start(bf16[256,256]{1,0:T(8,128)(2,1)} %w_second_ref.1) | copy-start | bytes 393220
  8.0 12.8 %copy-start.5 = (bf16[256,256]{1,0:T(8,128)(2,1)S(1)}, bf16[256,256]{1,0:T(8,128)(2,1)}, u32[]{:S(2)}) copy-start(bf16[256,256]{1,0:T(8,128)(2,1)} %n_second_ref.1) | copy-start | bytes 393220
  8.1 12.8 %copy-start.6 = (s32[1280,12]{0,1:T(8,128)S(1)}, s32[1280,12]{0,1:T(8,128)}, u32[]{:S(2)}) copy-start(s32[1280,12]{0,1:T(8,128)} %param.21) | copy-start | bytes 184324
  57.3 4.8 %collective-permute-start.2 = (bf16[960,256]{1,0:T(8,128)(2,1)S(1)}, bf16[960,256]{1,0:T(8,128)(2,1)S(1)}, u32[]{:S(2)}, u32[]{:S(2)}) collective-permute-start(bf16[960,256]{1,0:T(8,128)(2,1)S(1)} %get-tuple-element.71), channel_id=1, source_target_pairs={{0,2},{1,3},{2,0},{3,1},{4,6},{5,7},{6,4},{7,5},{8,10},{9,11},{10,... | collective-permute-start | bytes 1474568 | tf_op jit(solution)/shard_map/ppermute | solution.py:621
  62.2 8.4 %collective-permute-start.3 = (bf16[240,256]{1,0:T(8,128)(2,1)S(1)}, bf16[240,256]{1,0:T(8,128)(2,1)S(1)}, u32[]{:S(2)}, u32[]{:S(2)}) collective-permute-start(bf16[240,256]{1,0:T(8,128)(2,1)S(1)} %get-tuple-element.76), channel_id=1, source_target_pairs={{0,4},{1,5},{2,6},{3,7},{4,0},{5,1},{6,2},{7,3},{8,12},{9,13},{10,... | collective-permute-start | bytes 368648 | tf_op jit(solution)/shard_map/ppermute | solution.py:621
  62.3 8.3 %collective-permute-start.4 = (bf16[240,256]{1,0:T(8,128)(2,1)S(1)}, bf16[240,256]{1,0:T(8,128)(2,1)S(1)}, u32[]{:S(2)}, u32[]{:S(2)}) collective-permute-start(bf16[240,256]{1,0:T(8,128)(2,1)S(1)} %get-tuple-element.77), channel_id=1, source_target_pairs={{0,1},{1,0},{2,3},{3,2},{4,5},{5,4},{6,7},{7,6},{8,9},{9,8},{10,11... | collective-permute-start | bytes 368648 | tf_op jit(solution)/shard_map/ppermute | solution.py:621
  64.2 7.7 %collective-permute-start.5 = (bf16[240,256]{1,0:T(8,128)(2,1)S(1)}, bf16[240,256]{1,0:T(8,128)(2,1)S(1)}, u32[]{:S(2)}, u32[]{:S(2)}) collective-permute-start(bf16[240,256]{1,0:T(8,128)(2,1)S(1)} %get-tuple-element.78), channel_id=1, source_target_pairs={{0,5},{1,4},{2,7},{3,6},{4,1},{5,0},{6,3},{7,2},{8,13},{9,12},{10,... | collective-permute-start | bytes 368648 | tf_op jit(solution)/shard_map/ppermute | solution.py:621
  72.0 14.9 %collective-permute-start.6 = (bf16[240,256]{1,0:T(8,128)(2,1)S(1)}, bf16[240,256]{1,0:T(8,128)(2,1)S(1)}, u32[]{:S(2)}, u32[]{:S(2)}) collective-permute-start(bf16[240,256]{1,0:T(8,128)(2,1)S(1)} %sum_parts.2.own_ref), channel_id=1, source_target_pairs={{0,8},{1,9},{2,10},{3,11},{4,12},{5,13},{6,14},{7,15},{8,0},{9,1},... | collective-permute-start | bytes 368648 | tf_op jit(solution)/shard_map/ppermute | solution.py:621
  72.1 14.8 %collective-permute-start.7 = (bf16[240,256]{1,0:T(8,128)(2,1)S(1)}, bf16[240,256]{1,0:T(8,128)(2,1)S(1)}, u32[]{:S(2)}, u32[]{:S(2)}) collective-permute-start(bf16[240,256]{1,0:T(8,128)(2,1)S(1)} %sum_parts.2.own_ref), channel_id=1, source_target_pairs={{0,16},{1,17},{2,18},{3,19},{4,20},{5,21},{6,22},{7,23},{8,24},{9,... | collective-permute-start | bytes 368648 | tf_op jit(solution)/shard_map/ppermute | solution.py:621
  74.7 12.2 %collective-permute-start.8 = (bf16[240,256]{1,0:T(8,128)(2,1)S(1)}, bf16[240,256]{1,0:T(8,128)(2,1)S(1)}, u32[]{:S(2)}, u32[]{:S(2)}) collective-permute-start(bf16[240,256]{1,0:T(8,128)(2,1)S(1)} %sum_parts.2.own_ref), channel_id=1, source_target_pairs={{0,24},{1,25},{2,26},{3,27},{4,28},{5,29},{6,30},{7,31},{8,16},{9,... | collective-permute-start | bytes 368648 | tf_op jit(solution)/shard_map/ppermute | solution.py:621
  76.5 14.1 %collective-permute-start.10 = (bf16[256,256]{1,0:T(8,128)(2,1)S(1)}, bf16[256,256]{1,0:T(8,128)(2,1)S(1)}, u32[]{:S(2)}, u32[]{:S(2)}) collective-permute-start(bf16[256,256]{1,0:T(8,128)(2,1)S(1)} %get-tuple-element.115), channel_id=1, source_target_pairs={{0,2},{2,4},{4,6},{6,8},{8,10},{10,12},{12,14},{14,16},{16,18},{18... | collective-permute-start | bytes 393224 | tf_op jit(solution)/shard_map/ppermute | solution.py:631
  76.5 14.0 %collective-permute-start.9 = (bf16[256,256]{1,0:T(8,128)(2,1)S(1)}, bf16[256,256]{1,0:T(8,128)(2,1)S(1)}, u32[]{:S(2)}, u32[]{:S(2)}) collective-permute-start(bf16[256,256]{1,0:T(8,128)(2,1)S(1)} %get-tuple-element.116), channel_id=1, source_target_pairs={{0,30},{2,0},{4,2},{6,4},{8,6},{10,8},{12,10},{14,12},{16,14},{18,... | collective-permute-start | bytes 393224 | tf_op jit(solution)/shard_map/ppermute | solution.py:631
  87.0 9.5 %collective-permute-start.11 = (bf16[240,256]{1,0:T(8,128)(2,1)S(1)}, bf16[240,256]{1,0:T(8,128)(2,1)S(1)}, u32[]{:S(2)}, u32[]{:S(2)}) collective-permute-start(bf16[240,256]{1,0:T(8,128)(2,1)S(1)} %sum_parts.3.refs_0_), channel_id=1, source_target_pairs={{0,4},{1,5},{2,6},{3,7},{4,0},{5,1},{6,2},{7,3},{8,12},{9,13},{10,... | collective-permute-start | bytes 368648 | tf_op jit(solution)/shard_map/ppermute | solution.py:621
  87.1 9.4 %collective-permute-start.12 = (bf16[240,256]{1,0:T(8,128)(2,1)S(1)}, bf16[240,256]{1,0:T(8,128)(2,1)S(1)}, u32[]{:S(2)}, u32[]{:S(2)}) collective-permute-start(bf16[240,256]{1,0:T(8,128)(2,1)S(1)} %sum_parts.3.refs_0_), channel_id=1, source_target_pairs={{0,1},{1,0},{2,3},{3,2},{4,5},{5,4},{6,7},{7,6},{8,9},{9,8},{10,11... | collective-permute-start | bytes 368648 | tf_op jit(solution)/shard_map/ppermute | solution.py:621
  88.9 7.6 %collective-permute-start.13 = (bf16[240,256]{1,0:T(8,128)(2,1)S(1)}, bf16[240,256]{1,0:T(8,128)(2,1)S(1)}, u32[]{:S(2)}, u32[]{:S(2)}) collective-permute-start(bf16[240,256]{1,0:T(8,128)(2,1)S(1)} %sum_parts.3.refs_0_), channel_id=1, source_target_pairs={{0,5},{1,4},{2,7},{3,6},{4,1},{5,0},{6,3},{7,2},{8,13},{9,12},{10,... | collective-permute-start | bytes 368648 | tf_op jit(solution)/shard_map/ppermute | solution.py:621
  96.5 1.9 %collective-permute-start.14 = (bf16[960,256]{1,0:T(8,128)(2,1)S(1)}, bf16[960,256]{1,0:T(8,128)(2,1)S(1)}, u32[]{:S(2)}, u32[]{:S(2)}) collective-permute-start(bf16[960,256]{1,0:T(8,128)(2,1)S(1)} %join_parts.1), channel_id=1, source_target_pairs={{0,2},{1,3},{2,0},{3,1},{4,6},{5,7},{6,4},{7,5},{8,10},{9,11},{10,... | collective-permute-start | bytes 1474568 | tf_op jit(solution)/shard_map/ppermute | solution.py:621
  (9 other events, 106.3 us)
